TPU v7x, 128 devices: a whole 4x4x4 slice. The times are simulated.
128 devices in a mesh: expert: 8 (over x, z_lo), fsdp: 16 (over y, z_hi, core).
Axes of the slice: x: 4, y: 4, z: 4 (z_hi: 2, z_lo: 2; z = z_hi * 2 + z_lo), core: 2. Of those that a mesh axis runs over, the one named last changes fastest.
Arguments:
- tokens: bfloat16 [16, 1024, 1536], P('fsdp', 'expert'), may hold values from -6 to 6
- seg_ids: int32 [16, 1024], P('fsdp'), may hold values from 0 to 1023, as said below
- routes: int32 [16, 1024, 8], P('fsdp', 'expert'), may hold values from 0 to 39, all different within a row; in each aligned block of 128 rows (0 to 127, 128 to 255, ..., all dimensions but the last counted through in order) at most 48 rows name the same one
- gain_attn: bfloat16 [1536], P('fsdp'), may hold values from 0.5 to 1.5
- query_key_value_weight: bfloat16 [1536, 2560], P('fsdp'), may hold values from -0.15625 to 0.15625
- w_out: bfloat16 [1536, 1536], P('fsdp'), may hold values from -0.875 to 0.875
- gain_moe: bfloat16 [1536], P('fsdp'), may hold values from 0.5 to 1.5
- w_router: bfloat16 [1536, 40], P('fsdp'), may hold values from -0.078125 to 0.078125
- w_gate_up: bfloat16 [40, 1536, 1024], P('expert', 'fsdp'), may hold values from -0.15625 to 0.15625
- w_down: bfloat16 [40, 512, 1536], P('expert', 'fsdp'), may hold values from -1.5 to 1.5
- cotangent: bfloat16 [16, 1024, 1536], P('fsdp', 'expert'), may hold values from -6 to 6
Outputs:
- output: bfloat16 [16, 1024, 1536], P('fsdp', 'expert')
- grad_tokens: bfloat16 [16, 1024, 1536], P('fsdp', 'expert')
- grad_gain_attn: float32 [1536], P('fsdp')
- grad_w_qkv: float32 [1536, 2560], P('fsdp')
- grad_w_out: float32 [1536, 1536], P('fsdp')
- grad_gain_moe: float32 [1536], P('fsdp')
- grad_w_router: float32 [1536, 40], P('fsdp')
- grad_w_gate_up: float32 [40, 1536, 1024], P('expert', 'fsdp')
- grad_w_down: float32 [40, 512, 1536], P('expert', 'fsdp')
Inputs may be any that keep to these rules, and one draw needn't show every extreme that they name: `seg_ids`: never falls along a sequence; a document's number is the position of its first token, so equal numbers mark one document of consecutive positions; in one sequence, drawn from the seed, a single document covers all 1024 positions, and some other sequence ends in a document of one token. `routes`: A token's 8 experts are distinct. Within each aligned block of 128 tokens (the tokens of one device) no expert is named by more than 48 tokens, and in some block some expert is named by exactly 48.
All inputs are finite; a program needn't handle non-finite values.
Results may differ from a plain program's by a relative error of at most 0.03.
Values may be sent and summed in bfloat16 or wider, within the bound.
No kernel may reach another device: no remote copies, remote signals or barrier semaphores. Data moves between devices by JAX's collectives and lax.ppermute only.
A program may use at most 192 MiB of HBM per device.

v0:
```python
import math

import jax
import jax.numpy as jnp
from jax import lax
from jax.sharding import PartitionSpec as P

QUERY_HEADS = 24
KEY_VALUE_HEADS = 8
HEAD_SIZE = 64
FFE = 512
TOP = 8
EXP_DEV = 5


EPS = 1e-06
THETA = 10000.0
LARGE_NEGATIVE = -1e30


def rms_inverse(features):
    return lax.rsqrt(jnp.mean(features * features, axis=-1, keepdims=True) + EPS)


def rms_backward(features, inverse, gain_vec, grad_normed):
    scaled = gain_vec * grad_normed
    grad_rows = inverse * scaled - features * inverse**3 * jnp.mean(
        features * scaled, axis=-1, keepdims=True
    )
    grad_gain = jnp.sum(features * inverse * grad_normed, axis=0)
    return (grad_rows, grad_gain)


def apply_rotary(features, cosine_table, sine_table):
    half_width = features.shape[-1] // 2
    low_half = features[..., :half_width]
    high_half = features[..., half_width:]
    return jnp.concatenate(
        [
            low_half * cosine_table - high_half * sine_table,
            high_half * cosine_table + low_half * sine_table,
        ],
        axis=-1,
    )


def unrotate(gradient, cosine_table, sine_table):
    half_width = gradient.shape[-1] // 2
    low_half = gradient[..., :half_width]
    high_half = gradient[..., half_width:]
    return jnp.concatenate(
        [
            low_half * cosine_table + high_half * sine_table,
            high_half * cosine_table - low_half * sine_table,
        ],
        axis=-1,
    )


def split_keys(key_piece, seg_all):
    key_rows, value_rows = key_piece
    row_total = key_rows.shape[0]
    block_rows = math.gcd(row_total, 512)
    block_count = row_total // block_rows
    positions = jnp.arange(row_total, dtype=jnp.int32)
    return (
        key_rows.reshape(block_count, block_rows, -1),
        value_rows.reshape(block_count, block_rows, -1),
        positions.reshape(block_count, block_rows),
        seg_all.reshape(block_count, block_rows),
    )


def body(
    tokens,
    seg_ids,
    routes,
    gain_attn,
    query_key_value_weight,
    w_out,
    gain_moe,
    w_router,
    w_gate_up,
    w_down,
    cotangent,
):
    token_count = tokens.shape[1]
    n_expert = lax.axis_size("expert")
    experts_all = EXP_DEV * n_expert
    capacity = (7 * token_count * TOP // (4 * experts_all) + 7) // 8 * 8
    seq_length = token_count * n_expert
    group_count = QUERY_HEADS // KEY_VALUE_HEADS
    query_total_width = QUERY_HEADS * HEAD_SIZE
    key_value_width = KEY_VALUE_HEADS * HEAD_SIZE
    score_scale = 1.0 / math.sqrt(HEAD_SIZE)
    inputs = tokens[0].astype(jnp.float32)
    seg_all = seg_ids[0]
    chosen = routes[0]
    upstream = cotangent[0].astype(jnp.float32)
    first_pos = lax.axis_index("expert") * token_count
    query_pos = first_pos + jnp.arange(token_count, dtype=jnp.int32)
    query_seg = lax.dynamic_slice_in_dim(seg_all, first_pos, token_count)
    full_qkv, full_out, full_router, full_gain_a, full_gain_m = (
        lax.all_gather(query_key_value_weight, "fsdp", axis=0, tiled=True),
        lax.all_gather(w_out, "fsdp", axis=0, tiled=True),
        lax.all_gather(w_router, "fsdp", axis=0, tiled=True),
        lax.all_gather(gain_attn, "fsdp", axis=0, tiled=True),
        lax.all_gather(gain_moe, "fsdp", axis=0, tiled=True),
    )
    gain_one = full_gain_a.astype(jnp.float32)
    gain_two = full_gain_m.astype(jnp.float32)
    inverse_one = rms_inverse(inputs)
    normed_one = (inputs * inverse_one * gain_one).astype(jnp.bfloat16)
    projected_rows = jnp.dot(normed_one, full_qkv, preferred_element_type=jnp.float32)
    inv_freq = THETA ** (-jnp.arange(0, HEAD_SIZE, 2, dtype=jnp.float32) / HEAD_SIZE)
    angles = query_pos.astype(jnp.float32)[:, None] * inv_freq[None, :]
    cosine_table = jnp.cos(angles)[:, None, :]
    sine_table = jnp.sin(angles)[:, None, :]
    query_rows = apply_rotary(
        projected_rows[:, :query_total_width].reshape(token_count, QUERY_HEADS, HEAD_SIZE),
        cosine_table,
        sine_table,
    ).astype(jnp.bfloat16)
    keys_mine = (
        apply_rotary(
            projected_rows[:, query_total_width : query_total_width + key_value_width].reshape(
                token_count, KEY_VALUE_HEADS, HEAD_SIZE
            ),
            cosine_table,
            sine_table,
        )
        .astype(jnp.bfloat16)
        .reshape(token_count, key_value_width)
    )
    values_mine = projected_rows[:, query_total_width + key_value_width :].astype(jnp.bfloat16)
    grouped_queries = query_rows.reshape(token_count, KEY_VALUE_HEADS, group_count, HEAD_SIZE)

    def visible_mask(key_pos, key_seg):
        return (key_pos[None, :] <= query_pos[:, None]) & (key_seg[None, :] == query_seg[:, None])

    def forward_block(carried, block_item):
        run_max, run_sum, accumulated = carried
        key_tile, value_tile, key_pos, key_seg = block_item
        scores = (
            jnp.einsum(
                "qkgd,skd->kgqs",
                grouped_queries,
                key_tile.reshape(-1, KEY_VALUE_HEADS, HEAD_SIZE),
                preferred_element_type=jnp.float32,
            )
            * score_scale
        )
        visible = visible_mask(key_pos, key_seg)
        masked = jnp.where(visible, scores, LARGE_NEGATIVE)
        new_max = jnp.maximum(run_max, jnp.max(masked, axis=-1))
        factor = jnp.exp(run_max - new_max)
        weights = jnp.where(visible, jnp.exp(masked - new_max[..., None]), 0.0)
        run_sum = run_sum * factor + jnp.sum(weights, axis=-1)
        accumulated = accumulated * factor[..., None] + jnp.einsum(
            "kgqs,skd->kgqd",
            weights.astype(jnp.bfloat16),
            value_tile.reshape(-1, KEY_VALUE_HEADS, HEAD_SIZE),
            preferred_element_type=jnp.float32,
        )
        return ((new_max, run_sum, accumulated), None)

    start_state = (
        jnp.full((KEY_VALUE_HEADS, group_count, token_count), LARGE_NEGATIVE, jnp.float32),
        jnp.zeros((KEY_VALUE_HEADS, group_count, token_count), jnp.float32),
        jnp.zeros((KEY_VALUE_HEADS, group_count, token_count, HEAD_SIZE), jnp.float32),
    )
    carried = start_state
    carried, unused = lax.scan(
        forward_block,
        carried,
        split_keys(
            (
                lax.all_gather(keys_mine, "expert", axis=0, tiled=True),
                lax.all_gather(values_mine, "expert", axis=0, tiled=True),
            ),
            seg_all,
        ),
    )
    final_max, final_sum, accumulated = carried
    attended_g = jnp.transpose(accumulated / final_sum[..., None], (2, 0, 1, 3))
    attended_low = attended_g.reshape(token_count, query_total_width).astype(jnp.bfloat16)
    resid = inputs + jnp.dot(attended_low, full_out, preferred_element_type=jnp.float32)
    inverse_two = rms_inverse(resid)
    normed_two = (resid * inverse_two * gain_two).astype(jnp.bfloat16)
    logits = jnp.dot(normed_two, full_router, preferred_element_type=jnp.float32)
    route_hot = chosen[:, :, None] == jnp.arange(experts_all, dtype=jnp.int32)
    picked = jnp.sum(jnp.where(route_hot, logits[:, None, :], 0.0), axis=-1)
    gates = jax.nn.softmax(picked, axis=-1)
    flat_ids = chosen.reshape(-1)
    id_hot = (flat_ids[:, None] == jnp.arange(experts_all, dtype=jnp.int32)).astype(jnp.int32)
    ranks = jnp.sum((jnp.cumsum(id_hot, axis=0) - id_hot) * id_hot, axis=1)
    position = flat_ids * capacity + ranks
    slots_total = experts_all * capacity

    def dispatch_rows(routed_rows):
        placed = (
            jnp.zeros((slots_total, routed_rows.shape[1]), jnp.bfloat16)
            .at[position]
            .set(routed_rows)
        )
        return placed.reshape(n_expert, EXP_DEV * capacity, -1)

    received = lax.all_to_all(
        dispatch_rows(jnp.repeat(normed_two, TOP, axis=0)),
        "expert",
        split_axis=0,
        concat_axis=0,
        tiled=True,
    )
    received = received.reshape(n_expert, EXP_DEV, capacity, -1)
    gate_up_full, down_full = (
        lax.all_gather(w_gate_up, "fsdp", axis=1, tiled=True),
        lax.all_gather(w_down, "fsdp", axis=1, tiled=True),
    )
    pre_act = jnp.einsum(
        "secd,edf->secf", received, gate_up_full, preferred_element_type=jnp.float32
    )
    gate_part = pre_act[..., :FFE]
    up_part = pre_act[..., FFE:]
    sigmoid_gate = jax.nn.sigmoid(gate_part)
    silu_gate = gate_part * sigmoid_gate
    hidden = (silu_gate * up_part).astype(jnp.bfloat16)
    expert_out = jnp.einsum(
        "secf,efd->secd", hidden, down_full, preferred_element_type=jnp.float32
    ).astype(jnp.bfloat16)
    returned = lax.all_to_all(
        expert_out.reshape(n_expert, EXP_DEV * capacity, -1),
        "expert",
        split_axis=0,
        concat_axis=0,
        tiled=True,
    )
    routed_out = (
        returned.reshape(slots_total, -1)[position]
        .reshape(token_count, TOP, -1)
        .astype(jnp.float32)
    )
    output = (resid + jnp.sum(gates[:, :, None] * routed_out, axis=1)).astype(jnp.bfloat16)
    grad_gates = jnp.sum(routed_out * upstream[:, None, :], axis=-1)
    grad_routed_out = (
        (gates[:, :, None] * upstream[:, None, :])
        .astype(jnp.bfloat16)
        .reshape(token_count * TOP, -1)
    )
    grad_received = lax.all_to_all(
        dispatch_rows(grad_routed_out), "expert", split_axis=0, concat_axis=0, tiled=True
    )
    grad_received = grad_received.reshape(n_expert, EXP_DEV, capacity, -1)
    grad_down = jnp.einsum(
        "secf,secd->efd", hidden, grad_received, preferred_element_type=jnp.float32
    )
    grad_hidden = jnp.einsum(
        "secd,efd->secf", grad_received, down_full, preferred_element_type=jnp.float32
    )
    grad_pre = jnp.concatenate(
        [
            grad_hidden * up_part * sigmoid_gate * (1.0 + gate_part * (1.0 - sigmoid_gate)),
            grad_hidden * silu_gate,
        ],
        axis=-1,
    ).astype(jnp.bfloat16)
    grad_sent = jnp.einsum(
        "secf,edf->secd", grad_pre, gate_up_full, preferred_element_type=jnp.float32
    ).astype(jnp.bfloat16)
    grad_back = lax.all_to_all(
        grad_sent.reshape(n_expert, EXP_DEV * capacity, -1),
        "expert",
        split_axis=0,
        concat_axis=0,
        tiled=True,
    )
    grad_routes = jnp.sum(
        grad_back.reshape(slots_total, -1)[position]
        .reshape(token_count, TOP, -1)
        .astype(jnp.float32),
        axis=1,
    )
    grad_gate_up = jnp.einsum(
        "secd,secf->edf", received, grad_pre, preferred_element_type=jnp.float32
    )
    shard_gate_up, shard_down = (
        lax.psum_scatter(
            grad_gate_up.astype(jnp.bfloat16), "fsdp", scatter_dimension=1, tiled=True
        ).astype(jnp.float32),
        lax.psum_scatter(
            grad_down.astype(jnp.bfloat16), "fsdp", scatter_dimension=1, tiled=True
        ).astype(jnp.float32),
    )
    grad_picked = gates * (grad_gates - jnp.sum(gates * grad_gates, axis=-1, keepdims=True))
    grad_logits = jnp.sum(jnp.where(route_hot, grad_picked[:, :, None], 0.0), axis=1).astype(
        jnp.bfloat16
    )
    grad_router_local = jnp.dot(normed_two.T, grad_logits, preferred_element_type=jnp.float32)
    grad_normed_two = (
        jnp.dot(grad_logits, full_router.T, preferred_element_type=jnp.float32) + grad_routes
    )
    grad_resid_norm, grad_gain_m = rms_backward(resid, inverse_two, gain_two, grad_normed_two)
    grad_resid = upstream + grad_resid_norm
    grad_branch = grad_resid.astype(jnp.bfloat16)
    grad_out_local = jnp.dot(attended_low.T, grad_branch, preferred_element_type=jnp.float32)
    attended_gradient = jnp.dot(grad_branch, full_out.T, preferred_element_type=jnp.float32).astype(
        jnp.bfloat16
    )
    grad_attended_grouped = attended_gradient.reshape(
        token_count, KEY_VALUE_HEADS, group_count, HEAD_SIZE
    )
    grad_att_f = grad_attended_grouped.astype(jnp.float32)
    delta = jnp.transpose(jnp.sum(grad_att_f * attended_g, axis=-1), (1, 2, 0))

    def backward_block(carried, block_item):
        grad_query_acc, grad_kv_rows = carried
        key_tile, value_tile, key_pos, key_seg = block_item
        key_head_rows = key_tile.reshape(-1, KEY_VALUE_HEADS, HEAD_SIZE)
        value_head_rows = value_tile.reshape(-1, KEY_VALUE_HEADS, HEAD_SIZE)
        scores = (
            jnp.einsum(
                "qkgd,skd->kgqs", grouped_queries, key_head_rows, preferred_element_type=jnp.float32
            )
            * score_scale
        )
        visible = visible_mask(key_pos, key_seg)
        soft = jnp.where(
            visible,
            jnp.exp(jnp.where(visible, scores, LARGE_NEGATIVE) - final_max[..., None])
            / final_sum[..., None],
            0.0,
        )
        grad_probs = jnp.einsum(
            "qkgd,skd->kgqs",
            grad_attended_grouped,
            value_head_rows,
            preferred_element_type=jnp.float32,
        )
        grad_scores = (soft * (grad_probs - delta[..., None])).astype(jnp.bfloat16)
        grad_query_acc = (
            grad_query_acc
            + jnp.einsum(
                "kgqs,skd->qkgd", grad_scores, key_head_rows, preferred_element_type=jnp.float32
            )
            * score_scale
        )
        grad_key_blk = (
            jnp.einsum(
                "kgqs,qkgd->skd", grad_scores, grouped_queries, preferred_element_type=jnp.float32
            )
            * score_scale
        )
        grad_value_blk = jnp.einsum(
            "kgqs,qkgd->skd",
            soft.astype(jnp.bfloat16),
            grad_attended_grouped,
            preferred_element_type=jnp.float32,
        )
        rows_here = key_tile.shape[0]
        update = jnp.concatenate(
            [grad_key_blk.reshape(rows_here, -1), grad_value_blk.reshape(rows_here, -1)], axis=1
        )
        grad_kv_rows = lax.dynamic_update_slice(grad_kv_rows, update, (key_pos[0], 0))
        return ((grad_query_acc, grad_kv_rows), None)

    grad_start = (
        jnp.zeros((token_count, KEY_VALUE_HEADS, group_count, HEAD_SIZE), jnp.float32),
        jnp.zeros((seq_length, 2 * key_value_width), jnp.float32),
    )
    carried = grad_start
    carried, unused = lax.scan(
        backward_block,
        carried,
        split_keys(
            (
                lax.all_gather(keys_mine, "expert", axis=0, tiled=True),
                lax.all_gather(values_mine, "expert", axis=0, tiled=True),
            ),
            seg_all,
        ),
    )
    grad_query_acc, grad_kv_rows = carried
    local_key_value_grad = lax.psum_scatter(
        grad_kv_rows.astype(jnp.bfloat16), "expert", scatter_dimension=0, tiled=True
    ).astype(jnp.float32)
    key_gradient = local_key_value_grad[:, :key_value_width].reshape(
        token_count, KEY_VALUE_HEADS, HEAD_SIZE
    )
    grad_values = local_key_value_grad[:, key_value_width:]
    grad_queries = grad_query_acc.reshape(token_count, QUERY_HEADS, HEAD_SIZE)
    grad_proj = jnp.concatenate(
        [
            unrotate(grad_queries, cosine_table, sine_table).reshape(token_count, -1),
            unrotate(key_gradient, cosine_table, sine_table).reshape(token_count, -1),
            grad_values,
        ],
        axis=1,
    ).astype(jnp.bfloat16)
    grad_qkv_local = jnp.dot(normed_one.T, grad_proj, preferred_element_type=jnp.float32)
    grad_normed_one = jnp.dot(grad_proj, full_qkv.T, preferred_element_type=jnp.float32)
    grad_in_norm, grad_gain_a = rms_backward(inputs, inverse_one, gain_one, grad_normed_one)
    grad_tokens = (grad_resid + grad_in_norm).astype(jnp.bfloat16)[None]
    shards = (
        lax.psum_scatter(
            grad_qkv_local.astype(jnp.bfloat16), "fsdp", scatter_dimension=0, tiled=True
        ).astype(jnp.float32),
        lax.psum_scatter(
            grad_out_local.astype(jnp.bfloat16), "fsdp", scatter_dimension=0, tiled=True
        ).astype(jnp.float32),
        lax.psum_scatter(
            grad_router_local.astype(jnp.bfloat16), "fsdp", scatter_dimension=0, tiled=True
        ).astype(jnp.float32),
        lax.psum_scatter(
            grad_gain_a.astype(jnp.bfloat16), "fsdp", scatter_dimension=0, tiled=True
        ).astype(jnp.float32),
        lax.psum_scatter(
            grad_gain_m.astype(jnp.bfloat16), "fsdp", scatter_dimension=0, tiled=True
        ).astype(jnp.float32),
    )
    totals = (
        lax.psum(shards[0].astype(jnp.bfloat16), "expert").astype(jnp.float32),
        lax.psum(shards[1].astype(jnp.bfloat16), "expert").astype(jnp.float32),
        lax.psum(shards[2].astype(jnp.bfloat16), "expert").astype(jnp.float32),
        lax.psum(shards[3].astype(jnp.bfloat16), "expert").astype(jnp.float32),
        lax.psum(shards[4].astype(jnp.bfloat16), "expert").astype(jnp.float32),
    )
    return (
        output[None],
        grad_tokens,
        totals[3],
        totals[0],
        totals[1],
        totals[4],
        totals[2],
        shard_gate_up,
        shard_down,
    )


def solution(mesh):
    in_specs = (
        P("fsdp", "expert", None),
        P("fsdp", None),
        P("fsdp", "expert", None),
        P("fsdp"),
        P("fsdp", None),
        P("fsdp", None),
        P("fsdp"),
        P("fsdp", None),
        P("expert", "fsdp", None),
        P("expert", "fsdp", None),
        P("fsdp", "expert", None),
    )
    out_specs = (
        P("fsdp", "expert", None),
        P("fsdp", "expert", None),
        P("fsdp"),
        P("fsdp", None),
        P("fsdp", None),
        P("fsdp"),
        P("fsdp", None),
        P("expert", "fsdp", None),
        P("expert", "fsdp", None),
    )
    return jax.shard_map(body, mesh=mesh, in_specs=in_specs, out_specs=out_specs, check_vma=False)
```

profile of v0, /device:TPU:1, one launch (start us, length us, event | category | flops | bytes accessed | tf_op | source)
XLA Modules:
  0.0 1454.2 jit_solution(7900213093014796547)
XLA Ops:
  11.7 35.7 %all-reduce.5 = (bf16[1536]{0:T(1024)(128)(2,1)S(1)}, bf16[1536]{0:T(1024)(128)(2,1)S(1)}) all-reduce(bf16[1536]{0:T(1024)(128)(2,1)S(1)} %dynamic-update-slice, bf16[1536]{0:T(1024)(128)(2,1)S(1)} %dynamic-update-slice.1), channel_id=1, replica_groups=mesh['expert'=8,'fsdp'=16] {'fsdp'}, use_global_device_ids=true, to_apply=%add | all-reduce | flops 3072 | bytes 12288
  49.4 35.9 %all-gather.8.cloned.1.call-done = bf16[1536,2560]{1,0:T(8,128)(2,1)} async-done(((bf16[96,2560]{1,0:T(8,128)(2,1)}), bf16[1536,2560]{1,0:T(8,128)(2,1)}) %all-gather.8.cloned.1.call-update) | async-done | bytes 7864336 | tf_op jit(solution)/shard_map/all_gather | solution.py:104
  85.2 4.7 fusion.87
  96.7 11.3 reduce-window.6
  109.8 15.9 %all-gather.10.cloned.1.call-done = bf16[1024,512]{0,1:T(8,128)(2,1)} async-done(((bf16[128,512]{0,1:T(8,128)(2,1)}), bf16[1024,512]{0,1:T(8,128)(2,1)}) %all-gather.10.cloned.1.call-update) | async-done | bytes 1048592 | tf_op jit(solution)/shard_map/all_gather | solution.py:178
  128.6 40.9 %all-gather.12.cloned.1.call-done = bf16[1024,512]{1,0:T(8,128)(2,1)} async-done(((bf16[128,512]{1,0:T(8,128)(2,1)}), bf16[1024,512]{1,0:T(8,128)(2,1)}) %all-gather.12.cloned.1.call-update) | async-done | bytes 1048592 | tf_op jit(solution)/shard_map/all_gather | solution.py:179
  171.8 29.9 %while.28 = (s32[]{:T(128)}, f32[8,3,128]{2,1,0:T(4,128)S(1)}, f32[8,3,128]{2,1,0:T(4,128)}, f32[8,3,128,64]{2,3,1,0:T(8,128)S(1)}, s32[2,512]{1,0:T(2,128)}, /*...) while((s32[]{:T(128)}, f32[8,3,128]{2,1,0:T(4,128)S(1)}, ...), condition=%wide.region_4.5_spmd.clone, body=%wide.region_1.4_spmd.clone.sunk | while | flops 423902336 | bytes 49624760 | solution.py:173
  174.7 4.8 fusion.152
  189.2 4.8 fusion.152
  194.0 4.5 fusion.153
  202.5 31.9 %all-gather.14.cloned.1.call-done = bf16[1536,1536]{1,0:T(8,128)(2,1)} async-done(((bf16[96,1536]{1,0:T(8,128)(2,1)}), bf16[1536,1536]{1,0:T(8,128)(2,1)}) %all-gather.14.cloned.1.call-update) | async-done | bytes 4718608 | tf_op jit(solution)/shard_map/all_gather | solution.py:105
  238.3 9.3 scatter_custom_fusion
  247.6 4.9 all-to-all-start
  252.5 86.5 %all-gather = bf16[16,96,40]{1,2,0:T(8,128)(2,1)S(1)} all-gather(bf16[1,96,40]{1,2,0:T(8,128)(2,1)S(1)} %bitcast.336), channel_id=1, replica_groups=mesh['expert'=8,'fsdp'=16] {'fsdp'}, dimensions={0}, use_global_device_ids=true | all-gather | bytes 130560 | tf_op jit(solution)/shard_map/all_gather | solution.py:106
  340.5 9.4 scatter_custom_fusion.1
  349.9 5.4 all-to-all-start.2
  355.3 102.4 %all-gather.16.cloned.1.call-done = bf16[5,1536,1024]{2,1,0:T(8,128)(2,1)} async-done(((bf16[5,96,1024]{2,1,0:T(8,128)(2,1)}), bf16[5,1536,1024]{2,1,0:T(8,128)(2,1)}) %all-gather.16.cloned.1.call-update) | async-done | bytes 15728656 | tf_op jit(solution)/shard_map/all_gather | solution.py:217
  457.7 13.4 fusion.58
  471.1 57.6 %all-gather.18.cloned.1.call-done = bf16[5,512,1536]{2,1,0:T(8,128)(2,1)} async-done(((bf16[5,32,1536]{2,1,0:T(8,128)(2,1)}), bf16[5,512,1536]{2,1,0:T(8,128)(2,1)}) %all-gather.18.cloned.1.call-update) | async-done | bytes 7864336 | tf_op jit(solution)/shard_map/all_gather | solution.py:218
  528.7 12.9 fusion.48
  541.5 12.6 convert_bitcast_fusion
  554.1 5.6 copy.137
  559.8 4.7 all-to-all-start.3
  564.5 7.0 convert_bitcast_fusion.1
  574.5 72.3 %all-to-all-done.3 = bf16[8,240,1536]{2,1,0:T(8,128)(2,1)} async-done(((bf16[8,240,1536]{2,1,0:T(8,128)(2,1)}), bf16[8,240,1536]{2,1,0:T(8,128)(2,1)}, u32[]{:S(2)}, u32[]{:S(2)}) %all-to-all-start.3) | async-done | bytes 5898272 | tf_op jit(solution)/shard_map/all_to_all | solution.py:270
  646.7 4.7 all-to-all-start.1
  651.7 10.7 gather_fusion.1
  662.4 4.8 convert_reduce_fusion
  667.3 65.8 %all-to-all-done.1 = bf16[8,240,1536]{2,1,0:T(8,128)(2,1)} async-done(((bf16[8,240,1536]{2,1,0:T(8,128)(2,1)}), bf16[8,240,1536]{2,1,0:T(8,128)(2,1)}, u32[]{:S(2)}, u32[]{:S(2)}) %all-to-all-start.1) | async-done | bytes 5898272 | tf_op jit(solution)/shard_map/all_to_all | solution.py:231
  733.1 10.7 gather_fusion
  743.8 4.6 fusion.37
  763.7 55.7 %while.29 = (s32[]{:T(128)}, f32[128,8,3,64]{0,3,2,1:T(8,128)}, bf16[1024,1024]{1,0:T(8,128)(2,1)}, bf16[2,512,512]{1,2,0:T(8,128)(2,1)}, s32[2,512]{1,0:T(2,128...) while((s32[]{:T(128)}, f32[128,8,3,64]{0,3,2,1:T(8,128)}, ...), condition=%wide.region_22.23_spmd.clone, body=%wide.region_21.22_spmd.clone.sunk | while | flops 1024196736 | bytes 69961536 | solution.py:371
  785.7 6.1 dynamic_update_slice.5
  813.9 5.5 dynamic_update_slice.5
  819.5 4.8 convolution_convert_fusion.1
  824.6 42.8 %reduce-scatter.19.cloned.1.call-done = bf16[128,1024]{1,0:T(8,128)(2,1)} async-done(((bf16[1024,1024]{1,0:T(8,128)(2,1)}), bf16[128,1024]{1,0:T(8,128)(2,1)}) %reduce-scatter.19.cloned.1.call-update) | async-done | bytes 262160
  868.8 5.4 convolution_convert_fusion
  876.6 10.7 bitcast_convert_fusion.1
  887.4 67.4 %reduce-scatter.13.cloned.1.call-done = bf16[96,1536]{1,0:T(8,128)(2,1)} async-done(((bf16[1536,1536]{1,0:T(8,128)(2,1)}), bf16[96,1536]{1,0:T(8,128)(2,1)}) %reduce-scatter.13.cloned.1.call-update) | async-done | bytes 294928 | tf_op jit(solution)/shard_map/reduce_scatter | solution.py:407
  954.9 100.2 %reduce-scatter.11.cloned.1.call-done = bf16[96,2560]{1,0:T(8,128)(2,1)} async-done(((bf16[1536,2560]{1,0:T(8,128)(2,1)}), bf16[96,2560]{1,0:T(8,128)(2,1)}) %reduce-scatter.11.cloned.1.call-update) | async-done | bytes 491536 | tf_op jit(solution)/shard_map/reduce_scatter | solution.py:404
  1055.1 14.7 %bitcast_convert_fusion = bf16[5,1536,1024]{2,1,0:T(8,128)(2,1)} fusion(bf16[8,5,48,1536]{3,2,1,0:T(8,128)(2,1)} %bitcast.21, bf16[8,5,48,512]{3,2,0,1:T(8,128)(2,1)} %get-tuple-element.436, bf16[8,5,48,512]{3,2,0,1:T(8,128)(2,1)} %get-tuple-element.435), kind=kOutput, calls=%fused_computation.51 | convolution fusion | flops 6055526400 | bytes 25559040 | tf_op jit(solution)/shard_map/secd,secf->edf/dot_general | solution.py:283
  1070.6 52.4 %reduce-scatter.21.cloned.1.call-done = bf16[96,40]{1,0:T(8,128)(2,1)} async-done(((bf16[1536,40]{1,0:T(8,128)(2,1)}), bf16[96,40]{1,0:T(8,128)(2,1)}) %reduce-scatter.21.cloned.1.call-update) | async-done | bytes 7696
  1123.8 6.1 fusion.69
  1129.9 35.6 %all-reduce.4 = (bf16[1536]{0:T(1024)(128)(2,1)S(1)}, bf16[1536]{0:T(1024)(128)(2,1)S(1)}) all-reduce(bf16[1536]{0:T(1024)(128)(2,1)S(1)} %get-tuple-element.362, bf16[1536]{0:T(1024)(128)(2,1)S(1)} %copy-done.28), channel_id=3, replica_groups=mesh['expert'=8,'fsdp'=16] {'fsdp'}, use_global_device_ids=true, to_apply=%region_26.27.clone | all-reduce | flops 3072 | bytes 12288
  1165.7 27.6 %all-reduce.6 = (bf16[96]{0:T(256)(128)(2,1)S(1)}, bf16[96]{0:T(256)(128)(2,1)S(1)}, bf16[96,40]{0,1:T(8,128)(2,1)S(1)}) all-reduce(bf16[96]{0:T(256)(128)(2,1)S(1)} %dynamic-slice.4, bf16[96]{0:T(256)(128)(2,1)S(1)} %dynamic-slice.6, bf16[96,40]{0,1:T(8,128)(2,1)S(1)} %copy.159), channel_id=1, replica_groups=mesh['expert'=8,'fsdp'=16] {'expert'}, use_global_device_ids=true, to_apply=%region_27.28 | all-reduce | flops 4032 | bytes 16128 | tf_op jit(solution)/shard_map/psum | solution.py:424
  1196.0 29.1 %reduce-scatter.17.cloned.1.call-done = bf16[5,32,1536]{2,1,0:T(8,128)(2,1)} async-done(((bf16[5,512,1536]{2,1,0:T(8,128)(2,1)}), bf16[5,32,1536]{2,1,0:T(8,128)(2,1)}) %reduce-scatter.17.cloned.1.call-update) | async-done | bytes 491536 | tf_op jit(solution)/shard_map/reduce_scatter | solution.py:290
  1227.2 71.5 %all-reduce.10.cloned.1.call-done = (bf16[96,2560]{1,0:T(8,128)(2,1)}, bf16[96,1536]{1,0:T(8,128)(2,1)}) async-done(((bf16[96,2560]{1,0:T(8,128)(2,1)}, bf16[96,1536]{1,0:T(8,128)(2,1)}), (bf16[96,2560]{1,0:T(8,128)(2,1)}, bf16[96,1536]{1,0:T(8,128)(2,1)})) %all-reduce.10.cloned.1.call-update) | async-done | bytes 786448 | tf_op jit(solution)/shard_map/psum | solution.py:421
  1302.6 142.1 %reduce-scatter.15.cloned.1.call-done = bf16[5,96,1024]{2,1,0:T(8,128)(2,1)} async-done(((bf16[5,1536,1024]{2,1,0:T(8,128)(2,1)}), bf16[5,96,1024]{2,1,0:T(8,128)(2,1)}) %reduce-scatter.15.cloned.1.call-update) | async-done | bytes 983056 | tf_op jit(solution)/shard_map/reduce_scatter | solution.py:287
  (252 shorter events, 115.8 us)
Async XLA Ops:
  7.2 78.1 %all-gather.8.cloned.1.call-start = ((), (), s32[]{:S(2)}) async-start(), calls=%async_computation.10 | async-start | bytes 8355840 | tf_op jit(solution)/shard_map/all_gather | solution.py:104
  7.9 117.8 %all-gather.10.cloned.1.call-start = ((), (), s32[]{:S(2)}) async-start(), calls=%async_computation.11 | async-start | bytes 1179648 | tf_op jit(solution)/shard_map/all_gather | solution.py:178
  47.4 37.8 %copy-start.20 = (f32[1536]{0:T(1024)}, f32[1536]{0:T(1024)S(1)}, u32[]{:S(2)}) copy-start(f32[1536]{0:T(1024)S(1)} %convert_element_type.178) | copy-start | bytes 18436
  49.2 36.0 %copy-start.32 = (f32[128]{0:T(128)}, f32[128]{0:T(128)S(1)}, u32[]{:S(2)}) copy-start(f32[128]{0:T(128)S(1)} %get-tuple-element.455) | copy-start | bytes 1540
  49.3 59.6 %copy-start.16 = (f32[128,32]{0,1:T(8,128)}, f32[128,32]{0,1:T(8,128)S(1)}, u32[]{:S(2)}) copy-start(f32[128,32]{0,1:T(8,128)S(1)} %get-tuple-element.450) | copy-start | bytes 49156
  49.3 59.6 %copy-start.18 = (f32[128,32]{0,1:T(8,128)}, f32[128,32]{0,1:T(8,128)S(1)}, u32[]{:S(2)}) copy-start(f32[128,32]{0,1:T(8,128)S(1)} %get-tuple-element.451) | copy-start | bytes 49156
  85.2 8.7 copy-start.26
  85.2 9.5 copy-start.37
  90.8 78.7 %all-gather.12.cloned.1.call-start = ((), (), s32[]{:S(2)}) async-start(), calls=%async_computation.12 | async-start | bytes 1179648 | tf_op jit(solution)/shard_map/all_gather | solution.py:179
  91.6 142.8 %all-gather.14.cloned.1.call-start = ((), (), s32[]{:S(2)}) async-start(), calls=%async_computation.13 | async-start | bytes 5013504 | tf_op jit(solution)/shard_map/all_gather | solution.py:105
  92.1 365.5 %all-gather.16.cloned.1.call-start = ((), (), s32[]{:S(2)}) async-start(), calls=%async_computation.14 | async-start | bytes 16711680 | tf_op jit(solution)/shard_map/all_gather | solution.py:217
  92.7 435.9 %all-gather.18.cloned.1.call-start = ((), (), s32[]{:S(2)}) async-start(), calls=%async_computation.15 | async-start | bytes 8355840 | tf_op jit(solution)/shard_map/all_gather | solution.py:218
  96.5 141.6 %copy-start.23 = (f32[1536]{0:T(1024)}, f32[1536]{0:T(1024)S(1)}, u32[]{:S(2)}) copy-start(f32[1536]{0:T(1024)S(1)} %convert_element_type.184) | copy-start | bytes 18436
  108.6 129.7 %copy-start.29 = (s32[1024,1]{0,1:T(1,128)}, s32[1024,1]{0,1:T(1,128)S(1)}, u32[]{:S(2)}) copy-start(s32[1024,1]{0,1:T(1,128)S(1)} %compare_select_fusion) | copy-start | bytes 12292
  171.8 62.6 %copy-start.4 = (bf16[1,128,1536]{2,1,0:T(8,128)(2,1)S(1)}, bf16[1,128,1536]{2,1,0:T(8,128)(2,1)}, u32[]{:S(2)}) copy-start(bf16[1,128,1536]{2,1,0:T(8,128)(2,1)} %param.15) | copy-start | bytes 1179652
  179.4 5.1 copy-start
  194.0 5.8 copy-start
  202.5 45.1 %copy-start.10 = (bf16[128,8,3,64]{0,3,2,1:T(8,128)(2,1)}, bf16[128,8,3,64]{0,3,2,1:T(8,128)(2,1)S(1)}, u32[]{:S(2)}) copy-start(bf16[128,8,3,64]{0,3,2,1:T(8,128)(2,1)S(1)} %bitcast_convert_fusion.2) | copy-start | bytes 1179652
  238.2 9.5 copy-start.36
  238.3 101.1 %copy-start.8 = (bf16[128,1536]{1,0:T(8,128)(2,1)}, bf16[128,1536]{1,0:T(8,128)(2,1)S(1)}, u32[]{:S(2)}) copy-start(bf16[128,1536]{1,0:T(8,128)(2,1)S(1)} %multiply_convert_fusion.1) | copy-start | bytes 1179652
  247.6 91.7 %copy-start.11 = (bf16[1,128,1536]{2,1,0:T(8,128)(2,1)S(1)}, bf16[1,128,1536]{2,1,0:T(8,128)(2,1)}, u32[]{:S(2)}) copy-start(bf16[1,128,1536]{2,1,0:T(8,128)(2,1)} %param.25) | copy-start | bytes 1179652
  247.6 92.0 %copy-start.27 = (s32[1,128,8]{1,2,0:T(8,128)S(1)}, s32[1,128,8]{1,2,0:T(8,128)}, u32[]{:S(2)}) copy-start(s32[1,128,8]{1,2,0:T(8,128)} %param.17) | copy-start | bytes 12292
  247.6 92.8 %copy-start.30 = (s32[1024,1]{0,1:T(1,128)S(1)}, s32[1024,1]{0,1:T(1,128)}, u32[]{:S(2)}) copy-start(s32[1024,1]{0,1:T(1,128)} %copy-done.29) | copy-start | bytes 12292
  247.6 102.2 %all-to-all-start = ((bf16[8,240,1536]{2,1,0:T(8,128)(2,1)}), bf16[8,240,1536]{2,1,0:T(8,128)(2,1)}, u32[]{:S(2)}, u32[]{:S(2)}) async-start(bf16[8,240,1536]{2,1,0:T(8,128)(2,1)} %bitcast.304), calls=%async_computation | async-start | bytes 11796480 | tf_op jit(solution)/shard_map/all_to_all | solution.py:208
  339.3 10.6 copy-start.13
  339.7 10.2 copy-start.31
  340.2 9.6 copy-start.35
  340.3 9.5 copy-start.15
  349.9 178.8 %all-to-all-start.2 = ((bf16[8,240,1536]{2,1,0:T(8,128)(2,1)}), bf16[8,240,1536]{2,1,0:T(8,128)(2,1)}, u32[]{:S(2)}, u32[]{:S(2)}) async-start(bf16[8,240,1536]{2,1,0:T(8,128)(2,1)} %bitcast.306), calls=%async_computation.2 | async-start | bytes 11796480 | tf_op jit(solution)/shard_map/all_to_all | solution.py:250
  559.8 87.0 %all-to-all-start.3 = ((bf16[8,240,1536]{2,1,0:T(8,128)(2,1)}), bf16[8,240,1536]{2,1,0:T(8,128)(2,1)}, u32[]{:S(2)}, u32[]{:S(2)}) async-start(bf16[8,240,1536]{2,1,0:T(8,128)(2,1)} %bitcast.307), calls=%async_computation.3 | async-start | bytes 11796480 | tf_op jit(solution)/shard_map/all_to_all | solution.py:270
  646.7 86.4 %all-to-all-start.1 = ((bf16[8,240,1536]{2,1,0:T(8,128)(2,1)}), bf16[8,240,1536]{2,1,0:T(8,128)(2,1)}, u32[]{:S(2)}, u32[]{:S(2)}) async-start(bf16[8,240,1536]{2,1,0:T(8,128)(2,1)} %bitcast.305), calls=%async_computation.1 | async-start | bytes 11796480 | tf_op jit(solution)/shard_map/all_to_all | solution.py:231
  651.5 215.9 %reduce-scatter.19.cloned.1.call-start = ((), (), s32[]{:S(2)}) async-start(), calls=%async_computation.20 | async-start | bytes 2359296
  743.8 9.9 copy-start.12
  766.7 5.6 copy-start.14
  794.7 5.6 copy-start.14
  819.4 5.0 copy-start.3
  819.4 135.4 %reduce-scatter.13.cloned.1.call-start = ((), (), s32[]{:S(2)}) async-start(), calls=%async_computation.17 | async-start | bytes 5013504 | tf_op jit(solution)/shard_map/reduce_scatter | solution.py:407
  824.3 44.4 %copy-start.5 = (bf16[1,128,1536]{2,1,0:T(8,128)(2,1)S(1)}, bf16[1,128,1536]{2,1,0:T(8,128)(2,1)}, u32[]{:S(2)}) copy-start(bf16[1,128,1536]{2,1,0:T(8,128)(2,1)} %param.15) | copy-start | bytes 1179652
  824.3 44.5 %copy-start.21 = (f32[1536]{0:T(1024)S(1)}, f32[1536]{0:T(1024)}, u32[]{:S(2)}) copy-start(f32[1536]{0:T(1024)} %copy-done.20) | copy-start | bytes 18436
  824.3 44.5 %copy-start.33 = (f32[128]{0:T(128)S(1)}, f32[128]{0:T(128)}, u32[]{:S(2)}) copy-start(f32[128]{0:T(128)} %copy-done.32) | copy-start | bytes 1540
  824.3 230.7 %reduce-scatter.11.cloned.1.call-start = ((), (), s32[]{:S(2)}) async-start(), calls=%async_computation.16 | async-start | bytes 8355840 | tf_op jit(solution)/shard_map/reduce_scatter | solution.py:404
  874.2 248.8 %reduce-scatter.21.cloned.1.call-start = ((), (), s32[]{:S(2)}) async-start(), calls=%async_computation.21 | async-start | bytes 417792
  876.3 348.8 %reduce-scatter.17.cloned.1.call-start = ((), (), s32[]{:S(2)}) async-start(), calls=%async_computation.19 | async-start | bytes 8355840 | tf_op jit(solution)/shard_map/reduce_scatter | solution.py:290
  887.4 411.3 %all-reduce.10.cloned.1.call-start = ((), (), s32[]{:S(2)}) async-start(), calls=%async_computation.22 | async-start | bytes 1572864 | tf_op jit(solution)/shard_map/psum | solution.py:421
  1055.1 389.6 %reduce-scatter.15.cloned.1.call-start = ((), (), s32[]{:S(2)}) async-start(), calls=%async_computation.18 | async-start | bytes 16711680 | tf_op jit(solution)/shard_map/reduce_scatter | solution.py:287
  1069.9 60.0 %copy-start.28 = (bf16[1536]{0:T(1024)(128)(2,1)S(1)}, bf16[1536]{0:T(1024)(128)(2,1)}, u32[]{:S(2)}) copy-start(bf16[1536]{0:T(1024)(128)(2,1)} %get-tuple-element.360) | copy-start | bytes 9220
  1069.9 125.1 %copy-start.7 = (f32[128,1536]{1,0:T(8,128)S(1)}, f32[128,1536]{1,0:T(8,128)}, u32[]{:S(2)}) copy-start(f32[128,1536]{1,0:T(8,128)} %copy-done.6) | copy-start | bytes 2359300
  1069.9 125.1 %copy-start.38 = (f32[128]{0:T(128)S(1)}, f32[128]{0:T(128)}, u32[]{:S(2)}) copy-start(f32[128]{0:T(128)} %get-tuple-element.454) | copy-start | bytes 1540
  (12 other events, 35.0 us)
Sparse Core Ops, SparseCore 0:
  10.4 74.7 all-gather.7
  90.9 34.7 all-gather.9
  128.0 41.4 all-gather.11
  171.7 62.6 all-gather.13
  236.7 220.9 all-gather.15
  460.0 68.5 all-gather.17
  819.5 47.8 reduce-scatter.18
  871.5 83.3 reduce-scatter.12
  959.7 95.2 reduce-scatter.10
  1059.6 63.3 reduce-scatter.20
  1127.9 97.1 reduce-scatter.16
  1227.7 70.9 all-reduce.9
  1303.1 141.5 reduce-scatter.14
where the time goes:
time: 1460 us; the launch traced here: 1450 us
  waiting for transfers between devices  930 us (64%)
  blocking collectives  185 us (13%)
  matrix products  141 us (10%)
  local copies, waits for them, and re-layouts  88 us (6%)
  other arithmetic  68.2 us (5%)
  starting transfers between devices  20.9 us (1%)
  between operations  16.3 us (1%)
    reduce_scatter x1, waiting for transfers between devices, body(): lax.psum_scatter(grad_gate_up.astype(jnp.bfloat16), 'fsdp', scatter_dimen...  142 us
    all_gather x1, waiting for transfers between devices, body(): lax.all_gather(w_gate_up, 'fsdp', axis=1, tiled=True)  102 us
    reduce_scatter x1, waiting for transfers between devices, body(): lax.psum_scatter(grad_qkv_local.astype(jnp.bfloat16), 'fsdp', scatter_dim...  100 us
    unnamed x15, waiting for transfers between devices  97.5 us
    all_gather x1, blocking collectives, body(): lax.all_gather(w_router, 'fsdp', axis=0, tiled=True)  86.5 us
    all_to_all x1, waiting for transfers between devices, body(): lax.all_to_all(grad_sent.reshape(n_expert, EXP_DEV * capacity, -1), 'expe...  72.3 us
    psum x1, waiting for transfers between devices, body(): lax.psum(shards[0].astype(jnp.bfloat16), 'expert').astype(jnp.float32)  71.5 us
    unnamed x2, blocking collectives  71.3 us
  transfers between devices with their start and end apart: 17, of which 15 were waited for; matrix products, arithmetic and copies ran while one was open for 12% of the time, Pallas kernels for 0%

commit v1 on v0

v1 whole, which is shorter than its diff:
```python
import math

import jax
import jax.numpy as jnp
from jax import lax
from jax.sharding import Mesh, PartitionSpec as P

QUERY_HEADS = 24
KEY_VALUE_HEADS = 8
HEAD_SIZE = 64
GROUP = QUERY_HEADS // KEY_VALUE_HEADS
FFE = 512
EXP_DEV = 5
EXPERTS = 40
WIDTH = 1536
TOK = 128
SEQ = 1024
CAP = 48
BLOCKS = 16
N_EXP = 8
N_FSDP = 16
N_YZ = 8
HALF_FFE = FFE // 2
HEAD_COLS = GROUP * HEAD_SIZE
QKV_COLS = HEAD_COLS + 2 * HEAD_SIZE
PACK = 384
SIDE = 128

EPS = 1e-06
THETA = 10000.0
LARGE_NEGATIVE = -1e30

EXP = ("x", "zl")
FSDP = ("y", "zh", "c")
YZ = ("y", "zh")
SWAP = ((0, 1), (1, 0))
BF = jnp.bfloat16
F32 = jnp.float32


def dot(a, b):
    return jnp.dot(a, b, preferred_element_type=F32)


def ein(spec, *args):
    return jnp.einsum(spec, *args, preferred_element_type=F32)


def core_swap(value):
    return lax.ppermute(value, "c", SWAP)


def to_all(value, axes, count):
    spread = jnp.broadcast_to(value[None], (count, *value.shape))
    return lax.all_to_all(spread, axes, 0, 0, tiled=True)


def exchange(value, axes):
    return lax.all_to_all(value, axes, 0, 0, tiled=True)


def rms_inverse(features):
    return lax.rsqrt(jnp.mean(features * features, axis=-1, keepdims=True) + EPS)


def rms_backward(features, inverse, gain_vec, grad_normed):
    scaled = gain_vec * grad_normed
    grad_rows = inverse * scaled - features * inverse**3 * jnp.mean(
        features * scaled, axis=-1, keepdims=True
    )
    grad_gain = jnp.sum(features * inverse * grad_normed, axis=0)
    return grad_rows, grad_gain


def rotate(features, cosine_table, sine_table):
    half = features.shape[-1] // 2
    low, high = features[..., :half], features[..., half:]
    return jnp.concatenate(
        [low * cosine_table - high * sine_table, high * cosine_table + low * sine_table], axis=-1
    )


def parity_matrix(parity):
    rows = jnp.arange(2 * FFE, dtype=jnp.int32)[:, None]
    cols = jnp.arange(FFE, dtype=jnp.int32)[None, :]
    part, rest = cols // HALF_FFE, cols % HALF_FFE
    source = part * FFE + (2 * (rest // 32) + parity) * 32 + rest % 32
    return (rows == source).astype(BF)


def split_pair(value):
    high = value.astype(BF)
    return high, (value - high.astype(F32)).astype(BF)


def body(tokens, seg_ids, routes, gain_attn, w_qkv, w_out, gain_moe, w_router, w_gate_up, w_down, cotangent):
    e = lax.axis_index(EXP)
    c = lax.axis_index("c")
    scale = 1.0 / math.sqrt(HEAD_SIZE)

    def own_columns(start, width):
        return lax.dynamic_slice_in_dim(w_qkv, start + e * width, width, axis=1)

    packet = jnp.concatenate(
        [
            own_columns(0, HEAD_COLS),
            own_columns(WIDTH, HEAD_SIZE),
            own_columns(WIDTH + KEY_VALUE_HEADS * HEAD_SIZE, HEAD_SIZE),
            w_router,
            gain_attn[:, None],
            gain_moe[:, None],
            jnp.zeros((w_qkv.shape[0], PACK - QKV_COLS - EXPERTS - 2), BF),
        ],
        axis=1,
    )
    packed = lax.all_gather(packet, FSDP, axis=0, tiled=True)
    qkv_cols = packed[:, :QKV_COLS]
    router = packed[:, QKV_COLS : QKV_COLS + EXPERTS]
    gain_one = packed[:, QKV_COLS + EXPERTS].astype(F32)
    gain_two = packed[:, QKV_COLS + EXPERTS + 1].astype(F32)
    full_out = lax.all_gather(w_out, FSDP, axis=0, tiled=True)

    mine_matrix, other_matrix = parity_matrix(c), parity_matrix(1 - c)
    flat_gu = w_gate_up.reshape(EXP_DEV * 96, 2 * FFE)
    gu_mine = dot(flat_gu, mine_matrix).astype(BF).reshape(EXP_DEV, 96, FFE)
    gu_other = dot(flat_gu, other_matrix).astype(BF).reshape(EXP_DEV, 96, FFE)
    gu_recv = core_swap(gu_other)
    gu_rows = jnp.where(
        c == 0,
        jnp.concatenate([gu_mine, gu_recv], axis=1),
        jnp.concatenate([gu_recv, gu_mine], axis=1),
    )
    gu_full = lax.all_gather(gu_rows, YZ, axis=1, tiled=True)
    dn_full = lax.all_gather(w_down, YZ, axis=1, tiled=True)

    tok_all = to_all(tokens[0], EXP, N_EXP).reshape(SEQ, WIDTH).astype(F32)
    cot_packet = jnp.concatenate(
        [cotangent[0], routes[0].astype(BF), jnp.zeros((TOK, SIDE - routes.shape[-1]), BF)], axis=1
    )
    cot_all = to_all(cot_packet, EXP, N_EXP).reshape(SEQ, WIDTH + SIDE)
    cot_pair = jnp.stack([cot_all, core_swap(cot_all)])

    inv_one = rms_inverse(tok_all)
    normed_one = (tok_all * inv_one * gain_one).astype(BF)
    projected = dot(normed_one, qkv_cols)
    positions = jnp.arange(SEQ, dtype=jnp.int32)
    inv_freq = THETA ** (-jnp.arange(0, HEAD_SIZE, 2, dtype=F32) / HEAD_SIZE)
    angles = positions.astype(F32)[:, None] * inv_freq[None, :]
    cosine, sine = jnp.cos(angles), jnp.sin(angles)
    queries = rotate(
        jnp.transpose(projected[:, :HEAD_COLS].reshape(SEQ, GROUP, HEAD_SIZE), (1, 0, 2)), cosine, sine
    ).astype(BF)
    keys = rotate(projected[:, HEAD_COLS : HEAD_COLS + HEAD_SIZE], cosine, sine).astype(BF)
    values = projected[:, HEAD_COLS + HEAD_SIZE :].astype(BF)
    seg = seg_ids[0]
    visible = (positions[None, :] <= positions[:, None]) & (seg[None, :] == seg[:, None])

    def softmax_rows(row_max=None, row_sum=None):
        scores = jnp.where(visible, ein("hqd,kd->hqk", queries, keys) * scale, LARGE_NEGATIVE)
        if row_max is None:
            row_max = jnp.max(scores, axis=-1, keepdims=True)
        weights = jnp.where(visible, jnp.exp(scores - row_max), 0.0)
        if row_sum is None:
            row_sum = jnp.sum(weights, axis=-1, keepdims=True)
        return weights / row_sum, row_max, row_sum

    soft, row_max, row_sum = softmax_rows()
    attended = ein("hqk,kd->hqd", soft.astype(BF), values)
    attended_low = jnp.transpose(attended, (1, 0, 2)).reshape(SEQ, HEAD_COLS).astype(BF)
    attended_all = to_all(attended_low, EXP, N_EXP)

    resid = tok_all + ein("etk,ekn->tn", attended_all, full_out.reshape(N_EXP, HEAD_COLS, WIDTH))
    inv_two = rms_inverse(resid)
    normed_two = (resid * inv_two * gain_two).astype(BF)

    normed_pair = jnp.stack([normed_two, core_swap(normed_two)])
    logits = dot(normed_pair.reshape(2 * SEQ, WIDTH), router)
    routes_pair = cot_pair[:, :, WIDTH : WIDTH + routes.shape[-1]].reshape(2 * SEQ, -1).astype(jnp.int32)
    chosen = jnp.any(routes_pair[:, :, None] == jnp.arange(EXPERTS, dtype=jnp.int32), axis=1)
    masked = jnp.where(chosen, logits, LARGE_NEGATIVE)
    exps = jnp.where(chosen, jnp.exp(masked - jnp.max(masked, axis=-1, keepdims=True)), 0.0)
    gates = exps / jnp.sum(exps, axis=-1, keepdims=True)
    gates_own = lax.dynamic_slice_in_dim(gates, e * EXP_DEV, EXP_DEV, axis=1).reshape(BLOCKS, TOK, EXP_DEV)
    hit = lax.dynamic_slice_in_dim(chosen, e * EXP_DEV, EXP_DEV, axis=1).reshape(BLOCKS, TOK, EXP_DEV)
    before = (jnp.arange(TOK)[:, None] > jnp.arange(TOK)[None, :]).astype(BF)
    ranks = ein("ts,bsj->bjt", before, hit.astype(BF)).astype(jnp.int32)
    hit_t = jnp.transpose(hit, (0, 2, 1))
    taken = (ranks[:, :, None, :] == jnp.arange(CAP, dtype=jnp.int32)[:, None]) & hit_t[:, :, None, :]
    one_hot = taken.astype(BF)
    slot_gates = jnp.sum(
        jnp.where(taken, jnp.transpose(gates_own, (0, 2, 1))[:, :, None, :], 0.0), axis=-1
    )
    slot_gates = jnp.transpose(slot_gates, (1, 0, 2)).reshape(EXP_DEV, BLOCKS * CAP)[:, :, None]

    def dispatch(rows):
        placed = ein("bjct,btd->jbcd", one_hot, rows.reshape(BLOCKS, TOK, WIDTH)).astype(BF)
        return placed.reshape(EXP_DEV, BLOCKS * CAP, WIDTH)

    def combine(rows):
        return ein(
            "bjct,jbcd->btd", one_hot, rows.reshape(EXP_DEV, BLOCKS, CAP, -1)
        ).reshape(2, SEQ, -1)

    received = dispatch(normed_pair)
    upstream_slots = dispatch(cot_pair[:, :, :WIDTH])
    pre_act = ein("jrd,jdf->jrf", received, gu_full)
    gate_part, up_part = pre_act[..., :HALF_FFE], pre_act[..., HALF_FFE:]
    sigmoid_gate = jax.nn.sigmoid(gate_part)
    silu_gate = gate_part * sigmoid_gate
    hidden = (silu_gate * up_part).astype(BF)
    hidden_gated = (hidden.astype(F32) * slot_gates).astype(BF)
    grad_plain = ein("jrd,jfd->jrf", upstream_slots, dn_full)
    gate_grad_slots = jnp.sum(hidden.astype(F32) * grad_plain, axis=-1)
    grad_down = ein("jrf,jrd->jfd", hidden_gated, upstream_slots).astype(BF)
    out_slots = ein("jrf,jfd->jrd", hidden_gated, dn_full).astype(BF)
    grad_hidden = grad_plain * slot_gates
    grad_pre = jnp.concatenate(
        [
            grad_hidden * up_part * sigmoid_gate * (1.0 + gate_part * (1.0 - sigmoid_gate)),
            grad_hidden * silu_gate,
        ],
        axis=-1,
    ).astype(BF)
    grad_sent = ein("jrf,jdf->jrd", grad_pre, gu_full).astype(BF)
    grad_gate_up = ein("jrd,jrf->jdf", received, grad_pre).astype(BF)

    routed_grad = combine(grad_sent)
    gate_grads = jnp.sum(
        jnp.where(
            taken,
            jnp.transpose(gate_grad_slots.reshape(EXP_DEV, BLOCKS, CAP), (1, 0, 2))[..., None],
            0.0,
        ),
        axis=2,
    )
    gate_grads = jnp.transpose(gate_grads, (0, 2, 1)).reshape(2, SEQ, EXP_DEV)

    def with_side(main, side):
        high, low = split_pair(side)
        zeros = jnp.zeros((*side.shape[:-1], SIDE - 2 * EXP_DEV), BF)
        return jnp.concatenate([main.astype(BF), high, low, zeros], axis=-1)

    def read_side(block):
        block = block.astype(F32)
        return block[..., WIDTH : WIDTH + EXP_DEV] + block[..., WIDTH + EXP_DEV : WIDTH + 2 * EXP_DEV]

    from_core = core_swap(with_side(routed_grad[1], gate_grads[1]))
    routed_sum = routed_grad[0] + from_core[:, :WIDTH].astype(F32)
    gate_sum = gate_grads[0] + read_side(from_core)
    routed_back = exchange(with_side(routed_sum, gate_sum).reshape(N_EXP, TOK, WIDTH + SIDE), EXP)
    routed_total = jnp.sum(routed_back[..., :WIDTH].astype(F32), axis=0)
    grad_gates = jnp.transpose(read_side(routed_back), (1, 0, 2)).reshape(TOK, EXPERTS)

    out_part = combine(out_slots)
    out_sum = out_part[0] + core_swap(out_part[1].astype(BF)).astype(F32)
    out_back = exchange(out_sum.astype(BF).reshape(N_EXP, TOK, WIDTH), EXP)

    def own_rows(value):
        return lax.dynamic_slice_in_dim(value, e * TOK, TOK, axis=0)

    resid_own, inv_two_own, normed_two_own = own_rows(resid), own_rows(inv_two), own_rows(normed_two)
    output = (resid_own + jnp.sum(out_back.astype(F32), axis=0)).astype(BF)
    gates_tok = own_rows(gates)
    upstream = cotangent[0].astype(F32)
    grad_logits = (
        gates_tok * (grad_gates - jnp.sum(gates_tok * grad_gates, axis=-1, keepdims=True))
    ).astype(BF)
    router_part = dot(normed_two_own.T, grad_logits)
    grad_normed_two = dot(grad_logits, router.T) + routed_total
    grad_rows, gain_two_part = rms_backward(resid_own, inv_two_own, gain_two, grad_normed_two)
    grad_resid = upstream + grad_rows
    grad_branch = grad_resid.astype(BF)
    grad_attended_own = ein("tn,ekn->etk", grad_branch, full_out.reshape(N_EXP, HEAD_COLS, WIDTH)).astype(BF)
    branch_blocks = jnp.transpose(grad_branch.reshape(TOK, N_EXP, HEAD_COLS), (1, 0, 2))
    back = exchange(jnp.concatenate([grad_attended_own, branch_blocks], axis=-1), EXP)
    grad_attended = jnp.transpose(back[..., :HEAD_COLS].reshape(SEQ, GROUP, HEAD_SIZE), (1, 0, 2))
    branch_cols = back[..., HEAD_COLS:].reshape(SEQ, HEAD_COLS)
    out_grad_part = ein("etk,tn->ekn", attended_all, branch_cols).reshape(WIDTH, HEAD_COLS)

    def reduce_over_all(parts):
        sent = parts.astype(BF).reshape(N_FSDP, WIDTH // N_FSDP, -1)
        summed = jnp.sum(exchange(sent, FSDP).astype(F32), axis=0).astype(BF)
        return to_all(summed, EXP, N_EXP).astype(F32)

    first_totals = reduce_over_all(
        jnp.concatenate(
            [
                out_grad_part,
                router_part,
                gain_two_part[:, None],
                jnp.zeros((WIDTH, 256 - HEAD_COLS - EXPERTS - 1), F32),
            ],
            axis=1,
        )
    )
    total_out = jnp.transpose(first_totals[..., :HEAD_COLS], (1, 0, 2)).reshape(-1, WIDTH)
    shared = jnp.sum(first_totals[..., HEAD_COLS : HEAD_COLS + EXPERTS + 1], axis=0)

    soft, _, _ = softmax_rows(row_max, row_sum)
    delta = jnp.sum(grad_attended.astype(F32) * attended, axis=-1, keepdims=True)
    grad_probs = ein("hqd,kd->hqk", grad_attended, values)
    grad_scores = (soft * (grad_probs - delta)).astype(BF)
    grad_values = ein("hqk,hqd->kd", soft.astype(BF), grad_attended)
    grad_queries = ein("hqk,kd->hqd", grad_scores, keys) * scale
    grad_keys = ein("hqk,hqd->kd", grad_scores, queries) * scale
    grad_projected = jnp.concatenate(
        [
            jnp.transpose(rotate(grad_queries, cosine, -sine), (1, 0, 2)).reshape(SEQ, HEAD_COLS),
            rotate(grad_keys, cosine, -sine),
            grad_values,
        ],
        axis=1,
    ).astype(BF)
    normed_grad_part = dot(grad_projected, qkv_cols.T).astype(BF)
    normed_back = exchange(normed_grad_part.reshape(N_EXP, TOK, WIDTH), EXP)
    grad_normed_one = jnp.sum(normed_back.astype(F32), axis=0)
    grad_in, gain_one_part = rms_backward(
        tokens[0].astype(F32), own_rows(inv_one), gain_one, grad_normed_one
    )
    grad_tokens = (grad_resid + grad_in).astype(BF)
    qkv_grad_part = dot(normed_one.T, grad_projected)
    last_totals = reduce_over_all(
        jnp.concatenate(
            [qkv_grad_part, gain_one_part[:, None], jnp.zeros((WIDTH, PACK - QKV_COLS - 1), F32)], axis=1
        )
    )

    def head_columns(start, width):
        return jnp.transpose(last_totals[..., start : start + width], (1, 0, 2)).reshape(-1, N_EXP * width)

    total_qkv = jnp.concatenate(
        [
            head_columns(0, HEAD_COLS),
            head_columns(HEAD_COLS, HEAD_SIZE),
            head_columns(HEAD_COLS + HEAD_SIZE, HEAD_SIZE),
        ],
        axis=1,
    )
    total_gain_one = jnp.sum(last_totals[..., QKV_COLS], axis=0)

    down_sent = jnp.transpose(grad_down.reshape(EXP_DEV, N_YZ, 32, WIDTH), (1, 0, 2, 3))
    total_down = jnp.sum(exchange(down_sent, YZ).astype(F32), axis=0)
    gu_sent = jnp.transpose(grad_gate_up.reshape(EXP_DEV, N_YZ, 192, FFE), (1, 0, 2, 3))
    gu_sum = jnp.sum(exchange(gu_sent, YZ).astype(F32), axis=0).astype(BF)
    first_rows, second_rows = gu_sum[:, :96], gu_sum[:, 96:]
    keep = jnp.where(c == 0, first_rows, second_rows).reshape(-1, FFE)
    arrived = core_swap(jnp.where(c == 0, second_rows, first_rows)).reshape(-1, FFE)
    total_gu = (dot(keep, mine_matrix.T) + dot(arrived, other_matrix.T)).reshape(EXP_DEV, 96, 2 * FFE)

    return (
        output[None],
        grad_tokens[None],
        total_gain_one,
        total_qkv,
        total_out,
        shared[:, EXPERTS],
        shared[:, :EXPERTS],
        total_gu,
        total_down,
    )


def solution(mesh):
    fine = Mesh(mesh.devices.reshape(4, 2, 4, 2, 2), ("x", "zl", "y", "zh", "c"))
    rows = P(FSDP, EXP, None)
    weight = P(FSDP, None)
    expert_weight = P(EXP, FSDP, None)
    in_specs = (
        rows,
        P(FSDP, None),
        rows,
        P(FSDP),
        weight,
        weight,
        P(FSDP),
        weight,
        expert_weight,
        expert_weight,
        rows,
    )
    out_specs = (rows, rows, P(FSDP), weight, weight, P(FSDP), weight, expert_weight, expert_weight)
    return jax.shard_map(body, mesh=fine, in_specs=in_specs, out_specs=out_specs, check_vma=False)
```

time: 1460 us -> 899 us (0.62)
  waiting for transfers between devices: 930 us -> 416 us
  blocking collectives: 185 us -> 0 us
  local copies, waits for them, and re-layouts: 88 us -> 139 us
  starting transfers between devices: 20.9 us -> 69.6 us
  other arithmetic: 68.2 us -> 92 us
  matrix products: 141 us -> 160 us
    reduce_scatter x4 -> x0, waiting for transfers between devices: 339 us -> none  [the longest x1 142 us: body(): lax.psum_scatter(grad_gate_up.astype(jnp.bfloat16), 'fsdp', scatter_dimen...]
    all_gather x6 -> x4, waiting for transfers between devices: 285 us -> 145 us  [the longest x1 53.7 us: body(): dn_full = lax.all_gather(w_down, YZ, axis=1, tiled=True)]
    all_to_all x4 -> x13, waiting for transfers between devices: 138 us -> 269 us  [the longest x8 202 us: exchange(): return lax.all_to_all(value, axes, 0, 0, tiled=True)]
    unnamed x15 -> x4, waiting for transfers between devices: 97.5 us -> 0.75 us
    all_gather x1 -> x0, blocking collectives: 86.5 us -> none  [body(): lax.all_gather(w_router, 'fsdp', axis=0, tiled=True)]
    psum x1 -> x0, waiting for transfers between devices: 71.5 us -> none  [body(): lax.psum(shards[0].astype(jnp.bfloat16), 'expert').astype(jnp.float32)]
    unnamed x2 -> x0, blocking collectives: 71.3 us -> none
    concatenate x0 -> x9, local copies, waits for them, and re-layouts: none -> 44.4 us  [the longest x3 41.2 us: with_side(): return jnp.concatenate([main.astype(BF), high, low, zeros], axis=-1)]
  transfers between devices with their start and end apart: 17 -> 23, of which waited for: 15 -> 16; matrix products, arithmetic and copies ran while one was open for 12% -> 37% of each run, Pallas kernels for 0% -> 0%
where the time goes in v1:
time: 899 us; the launch traced here: 891 us
  waiting for transfers between devices  416 us (46%)
  matrix products  160 us (18%)
  local copies, waits for them, and re-layouts  139 us (15%)
  other arithmetic  92 us (10%)
  starting transfers between devices  69.6 us (8%)
  between operations  15.4 us (2%)
    all_to_all x8, waiting for transfers between devices, exchange(): return lax.all_to_all(value, axes, 0, 0, tiled=True)  202 us
    dot_general x19, matrix products, ein(): return jnp.einsum(spec, *args, preferred_element_type=F32)  131 us
    all_to_all x5, waiting for transfers between devices, to_all(): return lax.all_to_all(spread, axes, 0, 0, tiled=True)  67.7 us
    all_gather x1, waiting for transfers between devices, body(): dn_full = lax.all_gather(w_down, YZ, axis=1, tiled=True)  53.7 us
    all_gather x1, waiting for transfers between devices, body(): packed = lax.all_gather(packet, FSDP, axis=0, tiled=True)  52.3 us
    all_to_all x8, starting transfers between devices, exchange(): return lax.all_to_all(value, axes, 0, 0, tiled=True)  41.8 us
    concatenate x3, local copies, waits for them, and re-layouts, with_side(): return jnp.concatenate([main.astype(BF), high, low, zeros], axis=-1)  41.2 us
    all_gather x1, waiting for transfers between devices, body(): gu_full = lax.all_gather(gu_rows, YZ, axis=1, tiled=True)  34.7 us
  transfers between devices with their start and end apart: 23, of which 16 were waited for; matrix products, arithmetic and copies ran while one was open for 37% of the time, Pallas kernels for 0%

profile of v1, /device:TPU:1, one launch (start us, length us, event | category | flops | bytes accessed | tf_op | source)
XLA Modules:
  0.0 891.4 jit_solution(977132794807971333)
XLA Ops:
  20.3 5.6 all-to-all-start
  26.8 52.3 %all-gather.5.cloned.1.call-done = bf16[1536,384]{1,0:T(8,128)(2,1)} async-done(((bf16[96,384]{1,0:T(8,128)(2,1)}), bf16[1536,384]{1,0:T(8,128)(2,1)}) %all-gather.5.cloned.1.call-update) | async-done | bytes 1179664 | tf_op jit(solution)/shard_map/all_gather | solution.py:116
  82.7 5.0 all-to-all-start.2
  97.5 8.9 %fusion.138 = (f32[3,1024]{1,0:T(4,128)S(1)}, f32[3,1024,1024]{1,2,0:T(8,128)}) fusion(pred[1024,1024]{0,1:T(8,128)(4,1)S(1)} %fusion.22, bf16[3,1024,32]{1,2,0:T(8,128)(2,1)} %get-tuple-element.64, bf16[3,1024,32]{1,2,0:T(8,128)(2,1)S(1)} %get-tuple-element.63, bf16[1024,32]{0,1:T(8,128)(2,1)S(1)} %get-tuple-element.75, ...), kind=kOutput, calls=%fused_computation.248 | convolution fusion | flops 419431424 | bytes 14168064 | tf_op jit(solution)/shard_map/sub | solution.py:162
  107.1 9.2 %fusion.21 = bf16[3,1024,1024]{1,2,0:T(8,128)(2,1)} fusion(f32[3,1024,1024]{1,2,0:T(8,128)} %get-tuple-element.83, f32[3,1024]{1,0:T(4,128)S(1)} %get-tuple-element.82), kind=kLoop, calls=%fused_computation.42 | loop fusion | flops 6291456 | bytes 18886656 | tf_op jit(solution)/shard_map/convert_element_type | solution.py:168
  116.3 5.0 fusion.139
  121.2 15.4 %all-to-all-done.2 = bf16[8,128,1664]{2,1,0:T(8,128)(2,1)} async-done(((bf16[8,128,1664]{2,1,0:T(8,128)(2,1)}), bf16[8,128,1664]{2,1,0:T(8,128)(2,1)}, u32[]{:S(2)}, u32[]{:S(2)}) %all-to-all-start.2) | async-done | bytes 3407904 | tf_op jit(solution)/shard_map/all_to_all | solution.py:55
  144.4 43.5 %all-to-all-done.1 = bf16[8,1024,192]{1,2,0:T(8,128)(2,1)} async-done(((bf16[8,1024,192]{1,2,0:T(8,128)(2,1)}), bf16[8,1024,192]{1,2,0:T(8,128)(2,1)}, u32[]{:S(2)}, u32[]{:S(2)}) %all-to-all-start.1) | async-done | bytes 3145760 | tf_op jit(solution)/shard_map/all_to_all | solution.py:55
  192.2 9.3 %multiply_reduce_fusion = (f32[1024]{0:T(1024)S(1)}, f32[1024,1536]{1,0:T(8,128)S(1)}) fusion(bf16[8,1024,192]{1,2,0:T(8,128)(2,1)} %all-to-all-done.1, bf16[8,192,1536]{2,1,0:T(8,128)(2,1)} %bitcast.262, bf16[8,128,1536]{2,1,0:T(8,128)(2,1)} %all-to-all-done), kind=kOutput, calls=%fused_computation.36 | convolution fusion | flops 4838128640 | bytes 17305600 | tf_op jit(solution)/shard_map/etk,ekn->tn/dot_general | solution.py:46
  208.0 6.0 pad_maximum_fusion
  213.9 9.0 %fusion.6 = bf16[5,16,48,1536]{3,2,0,1:T(8,128)(2,1)} fusion(bf16[16,128,1536,1]{2,1,3,0:T(8,128)(2,1)} %bitcast.251, s32[16,5,128]{2,1,0:T(8,128)S(1)} %copy.156, pred[16,5,128]{2,1,0:T(8,128)(4,1)S(1)} %copy.157), kind=kOutput, calls=%fused_computation.13 | convolution fusion | flops 1516830720 | bytes 18139136 | tf_op jit(solution)/shard_map/bjct,btd->jbcd/dot_general | solution.py:46
  223.0 10.4 %copy.162 = bf16[5,16,48,1536]{3,2,1,0:T(8,128)(2,1)} copy(bf16[5,16,48,1536]{3,2,0,1:T(8,128)(2,1)} %fusion.6) | data formatting | bytes 23592960 | tf_op jit(solution)/shard_map/convert_element_type | solution.py:196
  234.0 5.4 pad_maximum_fusion.1
  239.4 9.0 %fusion.5 = bf16[5,16,48,1536]{3,2,0,1:T(8,128)(2,1)} fusion(bf16[16,128,1536,1]{2,1,3,0:T(8,128)(2,1)} %bitcast.242, s32[16,5,128]{2,1,0:T(8,128)S(1)} %copy.156, pred[16,5,128]{2,1,0:T(8,128)(4,1)S(1)} %copy.157), kind=kOutput, calls=%fused_computation.12 | convolution fusion | flops 1516830720 | bytes 18139136 | tf_op jit(solution)/shard_map/bjct,btd->jbcd/dot_general | solution.py:46
  248.4 10.4 %copy.158 = bf16[5,16,48,1536]{3,2,1,0:T(8,128)(2,1)} copy(bf16[5,16,48,1536]{3,2,0,1:T(8,128)(2,1)} %fusion.5) | data formatting | bytes 23592960 | tf_op jit(solution)/shard_map/convert_element_type | solution.py:196
  261.1 34.7 %all-gather.9.cloned.1.call-done = bf16[5,1536,512]{2,1,0:T(8,128)(2,1)} async-done(((bf16[5,192,512]{2,1,0:T(8,128)(2,1)}), bf16[5,1536,512]{2,1,0:T(8,128)(2,1)}) %all-gather.9.cloned.1.call-update) | async-done | bytes 7864336 | tf_op jit(solution)/shard_map/all_gather | solution.py:133
  295.8 15.6 %fusion.141 = f32[5,768,512]{1,2,0:T(8,128)} fusion(bf16[5,768,1536]{2,1,0:T(8,128)(2,1)} %bitcast.257, bf16[5,1536,512]{2,1,0:T(8,128)(2,1)} %all-gather.9.cloned.1.call-done), kind=kOutput, calls=%fused_computation.251 | convolution fusion | flops 6039797760 | bytes 27525120 | tf_op jit(solution)/shard_map/jrd,jdf->jrf/dot_general | solution.py:46
  311.4 53.7 %all-gather.11.cloned.1.call-done = bf16[5,256,1536]{2,1,0:T(8,128)(2,1)} async-done(((bf16[5,32,1536]{2,1,0:T(8,128)(2,1)}), bf16[5,256,1536]{2,1,0:T(8,128)(2,1)}) %all-gather.11.cloned.1.call-update) | async-done | bytes 3932176 | tf_op jit(solution)/shard_map/all_gather | solution.py:134
  365.1 11.5 %fusion.24 = (f32[5,768]{1,0:T(8,128)S(1)}, bf16[5,768,256]{1,2,0:T(8,128)(2,1)S(1)}, f32[5,768,256]{1,2,0:T(8,128)}) fusion(f32[5,768,512]{1,2,0:T(8,128)} %fusion.141, bf16[5,768,1536]{2,1,0:T(8,128)(2,1)} %bitcast.259, bf16[5,256,1536]{2,1,0:T(8,128)(2,1)} %all-gather.11.cloned.1.call-done), kind=kOutput, calls=%fused_computation.49 | convolution fusion | flops 3028742400 | bytes 29506560 | tf_op jit(solution)/shard_map/jrd,jfd->jrf/dot_general | solution.py:46
  378.3 6.9 multiply_convert_fusion.3
  385.2 6.0 convolution_convert_fusion.1
  391.2 5.5 fusion.8
  404.4 13.2 %convolution_convert_fusion = bf16[5,768,1536]{2,1,0:T(8,128)(2,1)} fusion(bf16[5,1536,512]{2,1,0:T(8,128)(2,1)} %all-gather.9.cloned.1.call-done, bf16[5,768,256]{1,2,0:T(8,128)(2,1)} %get-tuple-element.55, bf16[5,768,256]{1,2,0:T(8,128)(2,1)} %get-tuple-element.54), kind=kOutput, calls=%fused_computation.1 | convolution fusion | flops 6053560320 | bytes 23592960 | tf_op jit(solution)/shard_map/jrf,jdf->jrd/dot_general | solution.py:46
  417.6 5.5 fusion.11
  434.4 17.8 %concatenate.67 = bf16[1024,1664]{0,1:T(8,128)(2,1)} concatenate(bf16[1024,1536]{0,1:T(8,128)(2,1)} %copy.166, bf16[1024,5]{0,1:T(8,128)(2,1)S(1)} %get-tuple-element.51, bf16[1024,5]{0,1:T(8,128)(2,1)S(1)} %get-tuple-element.50, bf16[1024,118]{0,1:T(8,128)(2,1)S(1)} %broadcast.409), dimensions={1} | concatenate | bytes 6815744 | tf_op jit(solution)/shard_map/concatenate | solution.py:241
  455.0 5.1 fusion.14
  464.6 5.8 slice.194
  470.5 6.6 copy.167
  480.8 4.8 add_convert_fusion
  485.6 17.8 %concatenate.68 = bf16[1024,1664]{0,1:T(8,128)(2,1)} concatenate(bf16[1024,1536]{0,1:T(8,128)(2,1)} %add_convert_fusion, bf16[1024,5]{0,1:T(8,128)(2,1)S(1)} %get-tuple-element.49, bf16[1024,5]{0,1:T(8,128)(2,1)S(1)} %get-tuple-element.48, bf16[1024,118]{0,1:T(8,128)(2,1)S(1)} %broadcast.409), dimensions={1} | concatenate | bytes 6815744 | tf_op jit(solution)/shard_map/concatenate | solution.py:241
  503.4 5.6 copy.168
  515.0 7.9 convolution_convert_fusion.5
  524.9 38.4 %all-to-all-done.4 = bf16[8,128,1664]{2,1,0:T(8,128)(2,1)} async-done(((bf16[8,128,1664]{2,1,0:T(8,128)(2,1)}), bf16[8,128,1664]{2,1,0:T(8,128)(2,1)}, u32[]{:S(2)}, u32[]{:S(2)}) %all-to-all-start.4) | async-done | bytes 3407904 | tf_op jit(solution)/shard_map/all_to_all | solution.py:59
  584.9 38.1 %all-to-all-done.12 = bf16[8,5,32,1536]{3,2,1,0:T(8,128)(2,1)} async-done(((bf16[8,5,32,1536]{3,2,1,0:T(8,128)(2,1)}), bf16[8,5,32,1536]{3,2,1,0:T(8,128)(2,1)}, u32[]{:S(2)}, u32[]{:S(2)}) %all-to-all-start.12) | async-done | bytes 3932192 | tf_op jit(solution)/shard_map/all_to_all | solution.py:59
  626.5 12.9 %convolution_convert_fusion.4 = bf16[5,1536,512]{2,1,0:T(8,128)(2,1)} fusion(bf16[5,768,1536]{2,1,0:T(8,128)(2,1)} %bitcast.258, bf16[5,768,256]{1,2,0:T(8,128)(2,1)} %get-tuple-element.55, bf16[5,768,256]{1,2,0:T(8,128)(2,1)} %get-tuple-element.54), kind=kOutput, calls=%fused_computation.41 | convolution fusion | flops 6051594240 | bytes 23592960 | tf_op jit(solution)/shard_map/jrd,jrf->jdf/dot_general | solution.py:46
  639.5 7.2 copy.225
  646.7 5.1 all-to-all-start.11
  658.4 6.0 multiply_convert_fusion
  673.6 85.8 %all-to-all-done.11 = bf16[8,5,192,512]{3,2,1,0:T(8,128)(2,1)} async-done(((bf16[8,5,192,512]{3,2,1,0:T(8,128)(2,1)}), bf16[8,5,192,512]{3,2,1,0:T(8,128)(2,1)}, u32[]{:S(2)}, u32[]{:S(2)}) %all-to-all-start.11) | async-done | bytes 7864352 | tf_op jit(solution)/shard_map/all_to_all | solution.py:59
  759.4 6.6 all-to-all-start.9
  766.0 4.8 fusion.45
  774.4 5.8 all-to-all-done.9
  780.2 5.2 all-to-all-start.6
  785.5 4.7 copy.176
  805.3 24.7 %all-to-all-done.6 = bf16[8,128,1536]{2,1,0:T(8,128)(2,1)} async-done(((bf16[8,128,1536]{2,1,0:T(8,128)(2,1)}), bf16[8,128,1536]{2,1,0:T(8,128)(2,1)}, u32[]{:S(2)}, u32[]{:S(2)}) %all-to-all-start.6) | async-done | bytes 3145760 | tf_op jit(solution)/shard_map/all_to_all | solution.py:59
  840.5 7.7 all-to-all-start.7
  859.3 7.5 all-to-all-done.7
  873.6 7.4 all-to-all-done.8
  (264 shorter events, 179.8 us)
Async XLA Ops:
  7.2 6.0 copy-start
  7.2 71.9 %all-gather.5.cloned.1.call-start = ((), (), s32[]{:S(2)}) async-start(), calls=%async_computation.13 | async-start | bytes 1253376 | tf_op jit(solution)/shard_map/all_gather | solution.py:116
  12.3 179.9 %all-gather.7.cloned.1.call-start = ((), (), s32[]{:S(2)}) async-start(), calls=%async_computation.14 | async-start | bytes 5013504 | tf_op jit(solution)/shard_map/all_gather | solution.py:121
  13.0 282.7 %all-gather.9.cloned.1.call-start = ((), (), s32[]{:S(2)}) async-start(), calls=%async_computation.15 | async-start | bytes 8847360 | tf_op jit(solution)/shard_map/all_gather | solution.py:133
  13.9 3.0 collective-permute-start.2
  20.3 60.5 %all-to-all-start = ((bf16[8,128,1536]{2,1,0:T(8,128)(2,1)}), bf16[8,128,1536]{2,1,0:T(8,128)(2,1)}, u32[]{:S(2)}, u32[]{:S(2)}) async-start(bf16[8,128,1536]{2,1,0:T(8,128)(2,1)} %broadcast_in_dim.74), calls=%async_computation | async-start | bytes 6291456 | tf_op jit(solution)/shard_map/all_to_all | solution.py:55
  26.1 69.3 %copy-start.44 = (f32[32]{0:T(128)}, f32[32]{0:T(128)S(1)}, u32[]{:S(2)}) copy-start(f32[32]{0:T(128)S(1)} %multiply_power_fusion) | copy-start | bytes 388
  26.2 69.3 %copy-start.34 = (f32[1024]{0:T(1024)}, f32[1024]{0:T(1024)S(1)}, u32[]{:S(2)}) copy-start(f32[1024]{0:T(1024)S(1)} %iota_convert_fusion) | copy-start | bytes 12292
  80.8 10.2 %copy-start.31 = (f32[1536]{0:T(1024)}, f32[1536]{0:T(1024)S(1)}, u32[]{:S(2)}) copy-start(f32[1536]{0:T(1024)S(1)} %get-tuple-element.41) | copy-start | bytes 18436
  82.7 53.9 %all-to-all-start.2 = ((bf16[8,128,1664]{2,1,0:T(8,128)(2,1)}), bf16[8,128,1664]{2,1,0:T(8,128)(2,1)}, u32[]{:S(2)}, u32[]{:S(2)}) async-start(bf16[8,128,1664]{2,1,0:T(8,128)(2,1)} %broadcast_in_dim.83), calls=%async_computation.2 | async-start | bytes 6815744 | tf_op jit(solution)/shard_map/all_to_all | solution.py:55
  96.7 9.7 %copy-start.18 = (f32[1024,32]{0,1:T(8,128)}, f32[1024,32]{0,1:T(8,128)S(1)}, u32[]{:S(2)}) copy-start(f32[1024,32]{0,1:T(8,128)S(1)} %get-tuple-element.77) | copy-start | bytes 393220
  96.7 9.7 %copy-start.27 = (bf16[1024,32]{0,1:T(8,128)(2,1)}, bf16[1024,32]{0,1:T(8,128)(2,1)S(1)}, u32[]{:S(2)}) copy-start(bf16[1024,32]{0,1:T(8,128)(2,1)S(1)} %get-tuple-element.75) | copy-start | bytes 196612
  96.7 9.7 %copy-start.29 = (bf16[1024,32]{0,1:T(8,128)(2,1)}, bf16[1024,32]{0,1:T(8,128)(2,1)S(1)}, u32[]{:S(2)}) copy-start(bf16[1024,32]{0,1:T(8,128)(2,1)S(1)} %get-tuple-element.76) | copy-start | bytes 196612
  97.5 8.9 %copy-start.20 = (bf16[3,1024,32]{1,2,0:T(8,128)(2,1)}, bf16[3,1024,32]{1,2,0:T(8,128)(2,1)S(1)}, u32[]{:S(2)}) copy-start(bf16[3,1024,32]{1,2,0:T(8,128)(2,1)S(1)} %get-tuple-element.63) | copy-start | bytes 589828
  138.7 49.2 %all-to-all-start.1 = ((bf16[8,1024,192]{1,2,0:T(8,128)(2,1)}), bf16[8,1024,192]{1,2,0:T(8,128)(2,1)}, u32[]{:S(2)}, u32[]{:S(2)}) async-start(bf16[8,1024,192]{1,2,0:T(8,128)(2,1)} %broadcast_in_dim.81), calls=%async_computation.1 | async-start | bytes 6291456 | tf_op jit(solution)/shard_map/all_to_all | solution.py:55
  143.2 221.9 %all-gather.11.cloned.1.call-start = ((), (), s32[]{:S(2)}) async-start(), calls=%async_computation.16 | async-start | bytes 4423680 | tf_op jit(solution)/shard_map/all_gather | solution.py:134
  143.2 62.5 %collective-permute-start = (bf16[1024,1664]{1,0:T(8,128)(2,1)}, bf16[1024,1664]{1,0:T(8,128)(2,1)}, u32[]{:S(2)}, u32[]{:S(2)}) collective-permute-start(bf16[1024,1664]{1,0:T(8,128)(2,1)} %bitcast.18), channel_id=1, source_target_pairs={{0,1},{1,0},{2,3},{3,2},{4,5},{5,4},{6,7},{7,6},{8,9},{9,8},{10,11... | collective-permute-start | bytes 10223624 | tf_op jit(solution)/shard_map/ppermute | solution.py:50
  205.3 28.7 %collective-permute-start.1 = (bf16[1024,1536]{1,0:T(8,128)(2,1)}, bf16[1024,1536]{1,0:T(8,128)(2,1)}, u32[]{:S(2)}, u32[]{:S(2)}) collective-permute-start(bf16[1024,1536]{1,0:T(8,128)(2,1)} %multiply_convert_fusion.1), channel_id=1, source_target_pairs={{0,1},{1,0},{2,3},{3,2},{4,5},{5,4},{6,7},{7,6},{8,9},{9,8},{10,11... | collective-permute-start | bytes 9437192 | tf_op jit(solution)/shard_map/ppermute | solution.py:50
  213.9 19.4 %slice-start.3 = ((s8[6291456]{0:T(1024)(128)(4,1)}), s8[2097152]{0:T(1024)(128)(4,1)S(1)}, s32[]{:S(2)}) async-start(s8[6291456]{0:T(1024)(128)(4,1)} %bitcast.246), calls=%async_computation.20 | async-start | bytes 4194304
  223.0 10.4 %slice-start.4 = ((s8[6291456]{0:T(1024)(128)(4,1)}), s8[4194304]{0:T(1024)(128)(4,1)S(1)}, s32[]{:S(2)}) async-start(s8[6291456]{0:T(1024)(128)(4,1)} %bitcast.246), calls=%async_computation.21 | async-start | bytes 8388608
  239.4 19.4 %slice-start = ((s8[6291456]{0:T(1024)(128)(4,1)}), s8[2097152]{0:T(1024)(128)(4,1)S(1)}, s32[]{:S(2)}) async-start(s8[6291456]{0:T(1024)(128)(4,1)} %bitcast.243), calls=%async_computation.17 | async-start | bytes 4194304
  248.4 10.4 %slice-start.1 = ((s8[6291456]{0:T(1024)(128)(4,1)}), s8[4194304]{0:T(1024)(128)(4,1)S(1)}, s32[]{:S(2)}) async-start(s8[6291456]{0:T(1024)(128)(4,1)} %bitcast.243), calls=%async_computation.18 | async-start | bytes 8388608
  261.1 312.2 %copy-start.23 = (f32[2048,40]{0,1:T(8,128)}, f32[2048,40]{0,1:T(8,128)S(1)}, u32[]{:S(2)}) copy-start(f32[2048,40]{0,1:T(8,128)S(1)} %fusion.78) | copy-start | bytes 983044
  378.3 6.9 copy-start.7
  403.3 49.0 %collective-permute-start.3 = (bf16[1024,1536]{1,0:T(8,128)(2,1)}, bf16[1024,1536]{1,0:T(8,128)(2,1)}, u32[]{:S(2)}, u32[]{:S(2)}) collective-permute-start(bf16[1024,1536]{1,0:T(8,128)(2,1)} %bitcast.44), channel_id=1, source_target_pairs={{0,1},{1,0},{2,3},{3,2},{4,5},{5,4},{6,7},{7,6},{8,9},{9,8},{10,11... | collective-permute-start | bytes 9437192 | tf_op jit(solution)/shard_map/ppermute | solution.py:50
  452.3 24.8 %collective-permute-start.4 = (bf16[1024,1664]{0,1:T(8,128)(2,1)}, bf16[1024,1664]{0,1:T(8,128)(2,1)}, u32[]{:S(2)}, u32[]{:S(2)}) collective-permute-start(bf16[1024,1664]{0,1:T(8,128)(2,1)} %concatenate.67), channel_id=1, source_target_pairs={{0,1},{1,0},{2,3},{3,2},{4,5},{5,4},{6,7},{7,6},{8,9},{9,8},{10,11... | collective-permute-start | bytes 10223624 | tf_op jit(solution)/shard_map/ppermute | solution.py:50
  460.2 50.1 %all-to-all-start.3 = ((bf16[8,128,1536]{2,1,0:T(8,128)(2,1)}), bf16[8,128,1536]{2,1,0:T(8,128)(2,1)}, u32[]{:S(2)}, u32[]{:S(2)}) async-start(bf16[8,128,1536]{2,1,0:T(8,128)(2,1)} %bitcast.256), calls=%async_computation.3 | async-start | bytes 6291456 | tf_op jit(solution)/shard_map/all_to_all | solution.py:59
  510.3 53.1 %all-to-all-start.4 = ((bf16[8,128,1664]{2,1,0:T(8,128)(2,1)}), bf16[8,128,1664]{2,1,0:T(8,128)(2,1)}, u32[]{:S(2)}, u32[]{:S(2)}) async-start(bf16[8,128,1664]{2,1,0:T(8,128)(2,1)} %bitcast.253), calls=%async_computation.4 | async-start | bytes 6815744 | tf_op jit(solution)/shard_map/all_to_all | solution.py:59
  563.4 59.6 %all-to-all-start.12 = ((bf16[8,5,32,1536]{3,2,1,0:T(8,128)(2,1)}), bf16[8,5,32,1536]{3,2,1,0:T(8,128)(2,1)}, u32[]{:S(2)}, u32[]{:S(2)}) async-start(bf16[8,5,32,1536]{3,2,1,0:T(8,128)(2,1)} %bitcast.252), calls=%async_computation.12 | async-start | bytes 7864320 | tf_op jit(solution)/shard_map/all_to_all | solution.py:59
  623.0 23.7 %all-to-all-start.5 = ((bf16[8,128,384]{1,2,0:T(8,128)(2,1)}), bf16[8,128,384]{1,2,0:T(8,128)(2,1)S(1)}, u32[]{:S(2)}, u32[]{:S(2)}) async-start(bf16[8,128,384]{1,2,0:T(8,128)(2,1)} %pad_maximum_fusion.6), calls=%async_computation.5 | async-start | bytes 1572864 | tf_op jit(solution)/shard_map/all_to_all | solution.py:59
  646.7 112.6 %all-to-all-start.11 = ((bf16[8,5,192,512]{3,2,1,0:T(8,128)(2,1)}), bf16[8,5,192,512]{3,2,1,0:T(8,128)(2,1)}, u32[]{:S(2)}, u32[]{:S(2)}) async-start(bf16[8,5,192,512]{3,2,1,0:T(8,128)(2,1)} %bitcast.248), calls=%async_computation.11 | async-start | bytes 15728640 | tf_op jit(solution)/shard_map/all_to_all | solution.py:59
  651.8 6.5 copy-start.10
  651.8 6.6 copy-start.38
  658.4 6.0 copy-start.28
  658.4 6.0 copy-start.30
  669.3 101.6 %copy-start.33 = (bf16[1024,32]{0,1:T(8,128)(2,1)}, bf16[1024,32]{0,1:T(8,128)(2,1)S(1)}, u32[]{:S(2)}) copy-start(bf16[1024,32]{0,1:T(8,128)(2,1)S(1)} %get-tuple-element.72) | copy-start | bytes 196612
  673.5 97.3 %copy-start.25 = (bf16[3,1024,64]{1,2,0:T(8,128)(2,1)S(1)}, bf16[3,1024,64]{1,2,0:T(8,128)(2,1)}, u32[]{:S(2)}) copy-start(bf16[3,1024,64]{1,2,0:T(8,128)(2,1)} %pad_maximum_fusion.10) | copy-start | bytes 1179652
  759.4 20.8 %all-to-all-start.9 = ((bf16[16,96,256]{2,1,0:T(8,128)(2,1)}), bf16[16,96,256]{2,1,0:T(8,128)(2,1)S(1)}, u32[]{:S(2)}, u32[]{:S(2)}) async-start(bf16[16,96,256]{2,1,0:T(8,128)(2,1)} %maximum_maximum_fusion.1), calls=%async_computation.9 | async-start | bytes 1572864 | tf_op jit(solution)/shard_map/all_to_all | solution.py:59
  780.2 49.8 %all-to-all-start.6 = ((bf16[8,128,1536]{2,1,0:T(8,128)(2,1)}), bf16[8,128,1536]{2,1,0:T(8,128)(2,1)}, u32[]{:S(2)}, u32[]{:S(2)}) async-start(bf16[8,128,1536]{2,1,0:T(8,128)(2,1)} %bitcast.266), calls=%async_computation.6 | async-start | bytes 6291456 | tf_op jit(solution)/shard_map/all_to_all | solution.py:59
  800.0 50.0 %collective-permute-start.5 = (bf16[5,96,512]{2,1,0:T(8,128)(2,1)}, bf16[5,96,512]{2,1,0:T(8,128)(2,1)}, u32[]{:S(2)}, u32[]{:S(2)}) collective-permute-start(bf16[5,96,512]{2,1,0:T(8,128)(2,1)} %get-tuple-element.65), channel_id=1, source_target_pairs={{0,1},{1,0},{2,3},{3,2},{4,5},{5,4},{6,7},{7,6},{8,9},{9,8},{10,11... | collective-permute-start | bytes 1474568 | tf_op jit(solution)/shard_map/ppermute | solution.py:50
  805.1 31.5 %copy-start.9 = (bf16[1,128,1536]{2,1,0:T(8,128)(2,1)S(1)}, bf16[1,128,1536]{2,1,0:T(8,128)(2,1)}, u32[]{:S(2)}) copy-start(bf16[1,128,1536]{2,1,0:T(8,128)(2,1)} %param.11) | copy-start | bytes 1179652
  805.2 31.5 %copy-start.32 = (f32[1536]{0:T(1024)S(1)}, f32[1536]{0:T(1024)}, u32[]{:S(2)}) copy-start(f32[1536]{0:T(1024)} %copy-done.31) | copy-start | bytes 18436
  830.8 9.8 %all-to-all-start.10 = ((bf16[8,96,256]{2,1,0:T(8,128)(2,1)}), bf16[8,96,256]{2,1,0:T(8,128)(2,1)S(1)}, u32[]{:S(2)}, u32[]{:S(2)}) async-start(bf16[8,96,256]{2,1,0:T(8,128)(2,1)} %broadcast_in_dim.161), calls=%async_computation.10 | async-start | bytes 786432 | tf_op jit(solution)/shard_map/all_to_all | solution.py:55
  836.6 11.6 %copy-start.43 = (s32[512]{0:T(512)S(1)}, s32[512]{0:T(512)}, u32[]{:S(2)}) copy-start(s32[512]{0:T(512)} %copy-done.42) | copy-start | bytes 6148
  837.6 12.4 %copy-start.40 = (s32[512]{0:T(512)S(1)}, s32[512]{0:T(512)}, u32[]{:S(2)}) copy-start(s32[512]{0:T(512)} %copy-done.39) | copy-start | bytes 6148
  840.5 9.5 %copy-start.14 = (bf16[8,96,256]{2,1,0:T(8,128)(2,1)}, bf16[8,96,256]{2,1,0:T(8,128)(2,1)S(1)}, u32[]{:S(2)}) copy-start(bf16[8,96,256]{2,1,0:T(8,128)(2,1)S(1)} %all-to-all-done.10) | copy-start | bytes 1179652
  840.5 26.3 %all-to-all-start.7 = ((bf16[16,96,384]{2,1,0:T(8,128)(2,1)}), bf16[16,96,384]{2,1,0:T(8,128)(2,1)S(1)}, u32[]{:S(2)}, u32[]{:S(2)}) async-start(bf16[16,96,384]{2,1,0:T(8,128)(2,1)} %maximum_maximum_fusion), calls=%async_computation.7 | async-start | bytes 2359296 | tf_op jit(solution)/shard_map/all_to_all | solution.py:59
  867.9 13.2 %all-to-all-start.8 = ((bf16[8,96,384]{2,1,0:T(8,128)(2,1)}), bf16[8,96,384]{2,1,0:T(8,128)(2,1)S(1)}, u32[]{:S(2)}, u32[]{:S(2)}) async-start(bf16[8,96,384]{2,1,0:T(8,128)(2,1)} %broadcast_in_dim.159), calls=%async_computation.8 | async-start | bytes 1179648 | tf_op jit(solution)/shard_map/all_to_all | solution.py:55
  (26 other events, 83.1 us)
Sparse Core Ops, SparseCore 0:
  12.4 66.5 all-gather.4
  81.4 110.6 all-gather.6
  195.1 100.6 all-gather.8
  298.0 67.0 all-gather.10

commit v2 on v1

v2 whole, which is shorter than its diff:
```python
import math

import jax
import jax.numpy as jnp
from jax import lax
from jax.experimental import pallas as pl
from jax.experimental.pallas import tpu as pltpu
from jax.sharding import Mesh, PartitionSpec as P

QUERY_HEADS = 24
KEY_VALUE_HEADS = 8
HEAD_SIZE = 64
GROUP = QUERY_HEADS // KEY_VALUE_HEADS
FFE = 512
EXP_DEV = 5
EXPERTS = 40
WIDTH = 1536
TOK = 128
SEQ = 1024
CAP = 48
BLOCKS = 16
N_EXP = 8
N_FSDP = 16
N_YZ = 8
HALF_FFE = FFE // 2
HEAD_COLS = GROUP * HEAD_SIZE
QKV_COLS = HEAD_COLS + 2 * HEAD_SIZE
PACK = 384
SIDE = 128
SLOTS = EXP_DEV * CAP
ROWS = BLOCKS * CAP
CHUNK = 256
PARTS = 2
STEPS = BLOCKS // PARTS
GU_ROWS = WIDTH // N_YZ
MIX_ROWS = GU_ROWS + 32 * WIDTH // FFE
TILE = 256
TILES = SEQ // TILE
QK_COLS = HEAD_COLS + HEAD_SIZE
SCALE = 1.0 / math.sqrt(HEAD_SIZE)

EPS = 1e-06
THETA = 10000.0
LARGE_NEGATIVE = -1e30

EXP = ("x", "zl")
FSDP = ("y", "zh", "c")
YZ = ("y", "zh")
SWAP = ((0, 1), (1, 0))
BF = jnp.bfloat16
F32 = jnp.float32


def dot(a, b):
    return jnp.dot(a, b, preferred_element_type=F32)


def ein(spec, *args):
    return jnp.einsum(spec, *args, preferred_element_type=F32)


def core_swap(value):
    return lax.ppermute(value, "c", SWAP)


def to_all(value, axes, count):
    spread = jnp.broadcast_to(value[None], (count, *value.shape))
    return lax.all_to_all(spread, axes, 0, 0, tiled=True)


def exchange(value, axes):
    return lax.all_to_all(value, axes, 0, 0, tiled=True)


def rms_inverse(features):
    return lax.rsqrt(jnp.mean(features * features, axis=-1, keepdims=True) + EPS)


def rms_backward(features, inverse, gain_vec, grad_normed):
    scaled = gain_vec * grad_normed
    grad_rows = inverse * scaled - features * inverse**3 * jnp.mean(
        features * scaled, axis=-1, keepdims=True
    )
    grad_gain = jnp.sum(features * inverse * grad_normed, axis=0)
    return grad_rows, grad_gain


def parity_matrix(parity):
    rows = jnp.arange(2 * FFE, dtype=jnp.int32)[:, None]
    cols = jnp.arange(FFE, dtype=jnp.int32)[None, :]
    part, rest = cols // HALF_FFE, cols % HALF_FFE
    source = part * FFE + (2 * (rest // 32) + parity) * 32 + rest % 32
    return (rows == source).astype(BF)


def contract(a, b, dims):
    return lax.dot_general(a, b, (dims, ((), ())), preferred_element_type=F32)


def expert_kernel(
    n_own, n_par, g_own, g_par, chosen, router, weights,
    out_own, out_par, back_own, back_par, grads,
    x_slots, g_slots, side_slots, gate_slots, sum_gate_up, sum_down,
):
    step = pl.program_id(0)
    token = lax.broadcasted_iota(jnp.int32, (TOK, TOK), 0)
    other = lax.broadcasted_iota(jnp.int32, (TOK, TOK), 1)

    @pl.when(step < STEPS)
    def dispatch():
        def place(n_ref, g_ref, part):
            here = slice(part * TOK, (part + 1) * TOK)
            rows = n_ref[here, :]
            picks = chosen[here, :]
            logits = jnp.dot(rows, router[...], preferred_element_type=F32)
            keep = picks > 0
            masked = jnp.where(keep, logits, LARGE_NEGATIVE)
            exps = jnp.where(keep, jnp.exp(masked - jnp.max(masked, axis=-1, keepdims=True)), 0.0)
            gates = exps / jnp.sum(exps, axis=-1, keepdims=True)
            ranks = contract(picks, (token < other).astype(BF), ((0,), (0,)))
            named = contract(picks, (token == other).astype(BF), ((0,), (0,)))
            ranks = jnp.where(named > 0, ranks, -1.0).astype(jnp.int32)
            slot = lax.broadcasted_iota(jnp.int32, (CAP, TOK), 0)
            one_hot = jnp.concatenate(
                [(slot == ranks[j : j + 1, :]).astype(F32) for j in range(EXP_DEV)], axis=0
            ).astype(BF)
            high = gates.astype(BF)
            rest = gates - high.astype(F32)
            middle = rest.astype(BF)
            low = (rest - middle.astype(F32)).astype(BF)
            spread = (
                jnp.dot(one_hot, high, preferred_element_type=F32)
                + jnp.dot(one_hot, middle, preferred_element_type=F32)
                + jnp.dot(one_hot, low, preferred_element_type=F32)
            )
            lane = lax.broadcasted_iota(jnp.int32, (CAP, TOK), 1)
            x = jnp.dot(one_hot, rows, preferred_element_type=F32).astype(BF)
            g = jnp.dot(one_hot, g_ref[here, :], preferred_element_type=F32).astype(BF)
            start = pl.multiple_of((step * PARTS + part) * CAP, 16)
            for j in range(EXP_DEV):
                piece = slice(j * CAP, (j + 1) * CAP)
                x_slots[j, pl.ds(start, CAP), :] = x[piece]
                g_slots[j, pl.ds(start, CAP), :] = g[piece]
                gate_slots[j, pl.ds(start, CAP), :] = jnp.sum(
                    jnp.where(lane == j, spread[piece], 0.0), axis=-1, keepdims=True
                )

        @pl.when(step < STEPS // 2)
        def _():
            for part in range(PARTS):
                place(n_own, g_own, part)

        @pl.when(step >= STEPS // 2)
        def _():
            for part in range(PARTS):
                place(n_par, g_par, part)

    @pl.when((step >= STEPS) & (step < STEPS + EXP_DEV))
    def experts():
        j = step - STEPS
        gate_up = weights[:, 0, :GU_ROWS, :].reshape(WIDTH, FFE)
        down = jnp.concatenate(
            [
                weights[:, 0, GU_ROWS + 32 * p : GU_ROWS + 32 * (p + 1), :].reshape(HALF_FFE, FFE)
                for p in range(WIDTH // FFE)
            ],
            axis=1,
        )
        sum_gate_up[...] = jnp.zeros_like(sum_gate_up)
        sum_down[...] = jnp.zeros_like(sum_down)

        @pl.loop(0, ROWS // CHUNK)
        def _(part):
            here = pl.ds(pl.multiple_of(part * CHUNK, CHUNK), CHUNK)
            x = x_slots[j, here, :]
            g = g_slots[j, here, :]
            gates = gate_slots[j, here, :]
            pre = jnp.dot(x, gate_up, preferred_element_type=F32)
            plain = contract(g, down, ((1,), (1,)))
            gate, up = pre[:, :HALF_FFE], pre[:, HALF_FFE:]
            sigmoid = jax.nn.sigmoid(gate)
            silu = gate * sigmoid
            hidden = (silu * up).astype(BF).astype(F32)
            gated = (hidden * gates).astype(BF)
            slope = jnp.sum(hidden * plain, axis=-1, keepdims=True)
            high = slope.astype(BF).astype(F32)
            lane = lax.broadcasted_iota(jnp.int32, (CHUNK, SIDE), 1)
            row = lax.broadcasted_iota(jnp.int32, (CHUNK, SIDE), 0) + part * CHUNK
            lane = jnp.where(row < ROWS // 2, lane, lane - 2 * EXP_DEV)
            side_slots[j, here, :] = jnp.where(
                lane == j, high, jnp.where(lane == j + EXP_DEV, slope - high, 0.0)
            ).astype(BF)
            grad_hidden = plain * gates
            grad_pre = jnp.concatenate(
                [grad_hidden * up * sigmoid * (1.0 + gate * (1.0 - sigmoid)), grad_hidden * silu], axis=-1
            ).astype(BF)
            sum_down[...] += contract(gated, g, ((0,), (0,)))
            sum_gate_up[...] += contract(x, grad_pre, ((0,), (0,)))
            g_slots[j, here, :] = jnp.dot(gated, down, preferred_element_type=F32).astype(BF)
            x_slots[j, here, :] = contract(grad_pre, gate_up, ((1,), (1,))).astype(BF)

        grads[:, 0, :GU_ROWS, :] = sum_gate_up[...].astype(BF).reshape(N_YZ, GU_ROWS, FFE)
        for p in range(WIDTH // FFE):
            grads[:, 0, GU_ROWS + 32 * p : GU_ROWS + 32 * (p + 1), :] = (
                sum_down[:, p * FFE : (p + 1) * FFE].astype(BF).reshape(N_YZ, 32, FFE)
            )

    @pl.when(step >= STEPS + EXP_DEV)
    def combine():
        block = step - STEPS - EXP_DEV

        def write(out_ref, back_ref, part):
            here = slice(part * TOK, (part + 1) * TOK)
            start = pl.multiple_of((block * PARTS + part) * CAP, 16)
            picks = chosen[here, :]
            ranks = jnp.dot((token > other).astype(BF), picks, preferred_element_type=F32).astype(jnp.int32)
            lane = lax.broadcasted_iota(jnp.int32, (TOK, SLOTS), 1)
            hot = jnp.zeros((TOK, SLOTS), F32)
            for j in range(EXP_DEV):
                hit = (picks[:, j : j + 1] > 0) & (lane == ranks[:, j : j + 1] + j * CAP)
                hot = jnp.where(hit, 1.0, hot)
            hot = hot.astype(BF)

            def rows_of(ref):
                return jnp.concatenate([ref[j, pl.ds(start, CAP), :] for j in range(EXP_DEV)], axis=0)

            out_ref[here, :] = jnp.dot(hot, rows_of(g_slots), preferred_element_type=F32).astype(BF)
            back_ref[here, :WIDTH] = jnp.dot(hot, rows_of(x_slots), preferred_element_type=F32).astype(BF)
            back_ref[here, WIDTH:] = jnp.dot(hot, rows_of(side_slots), preferred_element_type=F32).astype(BF)

        @pl.when(block < STEPS // 2)
        def _():
            for part in range(PARTS):
                write(out_own, back_own, part)

        @pl.when(block >= STEPS // 2)
        def _():
            for part in range(PARTS):
                write(out_par, back_par, part)


def experts_call(n_own, n_par, g_own, g_par, chosen, router, weights):
    half = STEPS // 2
    last = STEPS + EXP_DEV
    span = PARTS * TOK

    def first(i):
        return (jnp.clip(i, 0, half - 1), 0)

    def second(i):
        return (jnp.clip(i - half, 0, half - 1), 0)

    def any_block(i):
        return (jnp.where(i < last, jnp.clip(i, 0, STEPS - 1), i - last), 0)

    def grad(i):
        return (0, jnp.clip(i - STEPS, 0, EXP_DEV - 1), 0, 0)

    def out_first(i):
        return (jnp.clip(i - last, 0, half - 1), 0)

    def out_second(i):
        return (jnp.clip(i - last - half, 0, half - 1), 0)

    shape = jax.ShapeDtypeStruct
    return pl.pallas_call(
        expert_kernel,
        grid=(2 * STEPS + EXP_DEV,),
        in_specs=[
            pl.BlockSpec((span, WIDTH), first),
            pl.BlockSpec((span, WIDTH), second),
            pl.BlockSpec((span, WIDTH), first),
            pl.BlockSpec((span, WIDTH), second),
            pl.BlockSpec((span, SIDE), any_block),
            pl.BlockSpec((WIDTH, SIDE), lambda i: (0, 0)),
            pl.BlockSpec((N_YZ, 1, MIX_ROWS, FFE), grad),
        ],
        out_specs=[
            pl.BlockSpec((span, WIDTH), out_first),
            pl.BlockSpec((span, WIDTH), out_second),
            pl.BlockSpec((span, WIDTH + SIDE), out_first),
            pl.BlockSpec((span, WIDTH + SIDE), out_second),
            pl.BlockSpec((N_YZ, 1, MIX_ROWS, FFE), grad),
        ],
        out_shape=[
            shape((SEQ, WIDTH), BF),
            shape((SEQ, WIDTH), BF),
            shape((SEQ, WIDTH + SIDE), BF),
            shape((SEQ, WIDTH + SIDE), BF),
            shape((N_YZ, EXP_DEV, MIX_ROWS, FFE), BF),
        ],
        scratch_shapes=[
            pltpu.VMEM((EXP_DEV, ROWS, WIDTH), BF),
            pltpu.VMEM((EXP_DEV, ROWS, WIDTH), BF),
            pltpu.VMEM((EXP_DEV, ROWS, SIDE), BF),
            pltpu.VMEM((EXP_DEV, ROWS, 1), F32),
            pltpu.VMEM((WIDTH, FFE), F32),
            pltpu.VMEM((HALF_FFE, WIDTH), F32),
        ],
        compiler_params=pltpu.CompilerParams(
            dimension_semantics=("arbitrary",), vmem_limit_bytes=60 * 1024 * 1024
        ),
        cost_estimate=pl.CostEstimate(flops=40_000_000_000, bytes_accessed=60_000_000, transcendentals=1_000_000),
        name="experts",
    )(n_own, n_par, g_own, g_par, chosen, router, weights)


def swap_halves(value):
    width = value.shape[-1]
    lane = lax.broadcasted_iota(jnp.int32, value.shape, 1)
    return jnp.where(
        lane % HEAD_SIZE < HEAD_SIZE // 2,
        pltpu.roll(value, width - HEAD_SIZE // 2, 1),
        pltpu.roll(value, HEAD_SIZE // 2, 1),
    )


def visible_tile(tile, count, seg_rows, seg_cols):
    row = lax.broadcasted_iota(jnp.int32, (TILE, count), 0) + tile * TILE
    col = lax.broadcasted_iota(jnp.int32, (TILE, count), 1)
    return (col <= row) & (seg_rows[...] == seg_cols[:, :count])


def attend_kernel(
    tokens, packed, gain, cosine, sine, seg_rows, seg_cols,
    normed, heads, attended, attended_low, stats, keys, values,
):
    step = pl.program_id(0)
    features = tokens[...].astype(F32)
    inverse = lax.rsqrt(jnp.mean(features * features, axis=-1, keepdims=True) + EPS)
    rows = (features * inverse * gain[...]).astype(BF)
    normed[...] = rows
    projected = jnp.dot(rows, packed[...], preferred_element_type=F32)
    turned = projected[:, :QK_COLS]
    turned = (turned * cosine[...] + swap_halves(turned) * sine[...]).astype(BF)
    value_rows = projected[:, QK_COLS:QKV_COLS].astype(BF)
    heads[:, :QK_COLS] = turned
    heads[:, QK_COLS:] = jnp.concatenate([value_rows, jnp.zeros_like(value_rows)], axis=1)
    here = pl.ds(pl.multiple_of(step * TILE, TILE), TILE)
    keys[here, :] = turned[:, HEAD_COLS:]
    values[here, :] = value_rows

    for tile in range(TILES):

        @pl.when(step == tile)
        def _(tile=tile):
            count = (tile + 1) * TILE
            visible = visible_tile(tile, count, seg_rows, seg_cols)
            key_rows, value_all = keys[:count, :], values[:count, :]
            parts = []
            for h in range(GROUP):
                query = turned[:, h * HEAD_SIZE : (h + 1) * HEAD_SIZE]
                scores = contract(query, key_rows, ((1,), (1,))) * SCALE
                scores = jnp.where(visible, scores, LARGE_NEGATIVE)
                top = jnp.max(scores, axis=-1, keepdims=True)
                weights = jnp.where(visible, jnp.exp(scores - top), 0.0)
                total = jnp.sum(weights, axis=-1, keepdims=True)
                soft = (weights / total).astype(BF)
                parts.append(jnp.dot(soft, value_all, preferred_element_type=F32))
                stats[:, 2 * h : 2 * h + 1] = top
                stats[:, 2 * h + 1 : 2 * h + 2] = total
            result = jnp.concatenate(parts, axis=1)
            attended[...] = result
            attended_low[...] = result.astype(BF)


def attend_call(tokens, packed, gain, cosine, sine, seg_rows, seg_cols):
    def rows(i):
        return (i, 0)

    def whole(i):
        return (0, 0)

    shape = jax.ShapeDtypeStruct
    return pl.pallas_call(
        attend_kernel,
        grid=(TILES,),
        in_specs=[
            pl.BlockSpec((TILE, WIDTH), rows),
            pl.BlockSpec((WIDTH, PACK), whole),
            pl.BlockSpec((1, WIDTH), whole),
            pl.BlockSpec((TILE, QK_COLS), rows),
            pl.BlockSpec((TILE, QK_COLS), rows),
            pl.BlockSpec((TILE, 1), rows),
            pl.BlockSpec((1, SEQ), whole),
        ],
        out_specs=[
            pl.BlockSpec((TILE, WIDTH), rows),
            pl.BlockSpec((TILE, PACK), rows),
            pl.BlockSpec((TILE, HEAD_COLS), rows),
            pl.BlockSpec((TILE, HEAD_COLS), rows),
            pl.BlockSpec((TILE, 8), rows),
        ],
        out_shape=[
            shape((SEQ, WIDTH), BF),
            shape((SEQ, PACK), BF),
            shape((SEQ, HEAD_COLS), F32),
            shape((SEQ, HEAD_COLS), BF),
            shape((SEQ, 8), F32),
        ],
        scratch_shapes=[pltpu.VMEM((SEQ, HEAD_SIZE), BF), pltpu.VMEM((SEQ, HEAD_SIZE), BF)],
        compiler_params=pltpu.CompilerParams(
            dimension_semantics=("arbitrary",), vmem_limit_bytes=48 * 1024 * 1024
        ),
        cost_estimate=pl.CostEstimate(flops=3_000_000_000, bytes_accessed=12_000_000, transcendentals=3_000_000),
        name="attend",
    )(tokens, packed, gain, cosine, sine, seg_rows, seg_cols)


def attend_back_kernel(
    upstream, heads, attended, stats, all_heads, cosine, sine, all_cosine, all_sine, seg_rows, seg_cols,
    grads, grad_keys, grad_values,
):
    step = pl.program_id(0)

    @pl.when(step == 0)
    def _():
        grad_keys[...] = jnp.zeros_like(grad_keys)
        grad_values[...] = jnp.zeros_like(grad_values)

    for tile in range(TILES):

        @pl.when(step == tile)
        def _(tile=tile):
            count = (tile + 1) * TILE
            visible = visible_tile(tile, count, seg_rows, seg_cols)
            key_rows = all_heads[:count, HEAD_COLS:QK_COLS]
            value_rows = all_heads[:count, QK_COLS:QKV_COLS]
            parts = []
            sum_keys, sum_values = 0.0, 0.0
            for h in range(GROUP):
                columns = slice(h * HEAD_SIZE, (h + 1) * HEAD_SIZE)
                query, grad = heads[:, columns], upstream[:, columns]
                scores = contract(query, key_rows, ((1,), (1,))) * SCALE
                scores = jnp.where(visible, scores, LARGE_NEGATIVE)
                top, total = stats[:, 2 * h : 2 * h + 1], stats[:, 2 * h + 1 : 2 * h + 2]
                soft = jnp.where(visible, jnp.exp(scores - top), 0.0) / total
                delta = jnp.sum(grad.astype(F32) * attended[:, columns], axis=-1, keepdims=True)
                grad_probs = contract(grad, value_rows, ((1,), (1,)))
                grad_scores = (soft * (grad_probs - delta)).astype(BF)
                parts.append(jnp.dot(grad_scores, key_rows, preferred_element_type=F32) * SCALE)
                sum_keys = sum_keys + contract(grad_scores, query, ((0,), (0,)))
                sum_values = sum_values + contract(soft.astype(BF), grad, ((0,), (0,)))
            grad_keys[:count, :] += sum_keys * SCALE
            grad_values[:count, :] += sum_values
            turned = jnp.concatenate([*parts, jnp.zeros_like(parts[0])], axis=1)
            turned = turned * cosine[...] - swap_halves(turned) * sine[...]
            grads[tile * TILE : count, :HEAD_COLS] = turned[:, :HEAD_COLS].astype(BF)

    @pl.when(step == TILES - 1)
    def _():
        both = jnp.concatenate([grad_keys[...], grad_values[...]], axis=1)
        turned = both * all_cosine[...] - swap_halves(both) * all_sine[...]
        lane = lax.broadcasted_iota(jnp.int32, both.shape, 1)
        both = jnp.where(lane < HEAD_SIZE, turned, both)
        grads[:, HEAD_COLS:] = jnp.concatenate([both, jnp.zeros((SEQ, HEAD_SIZE), F32)], axis=1).astype(BF)


def attend_back_call(upstream, heads, attended, stats, cosine, sine, seg_rows, seg_cols):
    def rows(i):
        return (i, 0)

    def whole(i):
        return (0, 0)

    return pl.pallas_call(
        attend_back_kernel,
        grid=(TILES,),
        in_specs=[
            pl.BlockSpec((TILE, HEAD_COLS), rows),
            pl.BlockSpec((TILE, PACK), rows),
            pl.BlockSpec((TILE, HEAD_COLS), rows),
            pl.BlockSpec((TILE, 8), rows),
            pl.BlockSpec((SEQ, PACK), whole),
            pl.BlockSpec((TILE, QK_COLS), rows),
            pl.BlockSpec((TILE, QK_COLS), rows),
            pl.BlockSpec((SEQ, 2 * HEAD_SIZE), whole),
            pl.BlockSpec((SEQ, 2 * HEAD_SIZE), whole),
            pl.BlockSpec((TILE, 1), rows),
            pl.BlockSpec((1, SEQ), whole),
        ],
        out_specs=pl.BlockSpec((SEQ, PACK), whole),
        out_shape=jax.ShapeDtypeStruct((SEQ, PACK), BF),
        scratch_shapes=[pltpu.VMEM((SEQ, HEAD_SIZE), F32), pltpu.VMEM((SEQ, HEAD_SIZE), F32)],
        compiler_params=pltpu.CompilerParams(
            dimension_semantics=("arbitrary",), vmem_limit_bytes=48 * 1024 * 1024
        ),
        cost_estimate=pl.CostEstimate(flops=4_000_000_000, bytes_accessed=8_000_000, transcendentals=3_000_000),
        name="attend_back",
    )(upstream, heads, attended, stats, heads, cosine, sine, cosine, sine, seg_rows, seg_cols)


def ring_of_four(block, axis):
    half = block.shape[0] // 2
    ahead = [(i, (i + 1) % 4) for i in range(4)]
    back = [(i, (i + 3) % 4) for i in range(4)]
    before = lax.ppermute(block, axis, ahead)
    after = lax.ppermute(block, axis, back)
    far_low = lax.ppermute(before[:half], axis, ahead)
    far_high = lax.ppermute(after[half:], axis, back)
    return [block, after, jnp.concatenate([far_low, far_high]), before]


def in_order(blocks, start):
    count = len(blocks)
    twice = jnp.stack([*blocks, *blocks])
    return lax.dynamic_slice_in_dim(twice, lax.rem(count - start, count), count, axis=0)


def body(tokens, seg_ids, routes, gain_attn, w_qkv, w_out, gain_moe, w_router, w_gate_up, w_down, cotangent):
    e = lax.axis_index(EXP)
    c = lax.axis_index("c")
    y = lax.axis_index("y")

    mine_matrix, other_matrix = parity_matrix(c), parity_matrix(1 - c)
    flat_gu = w_gate_up.reshape(EXP_DEV * 96, 2 * FFE)
    gu_other = dot(flat_gu, other_matrix).astype(BF).reshape(EXP_DEV, 96, FFE)
    gu_recv = core_swap(gu_other)
    gu_mine = dot(flat_gu, mine_matrix).astype(BF).reshape(EXP_DEV, 96, FFE)
    mixed = jnp.concatenate(
        [
            jnp.where(c == 0, gu_mine, gu_recv),
            jnp.where(c == 0, gu_recv, gu_mine),
            *(w_down[:, :, p * FFE : (p + 1) * FFE] for p in range(WIDTH // FFE)),
        ],
        axis=1,
    )
    weights = lax.all_gather(mixed, YZ, axis=0, tiled=False)

    def own_columns(start, width):
        return lax.dynamic_slice_in_dim(w_qkv, start + e * width, width, axis=1)

    packet = jnp.concatenate(
        [
            own_columns(0, HEAD_COLS),
            own_columns(WIDTH, HEAD_SIZE),
            own_columns(WIDTH + KEY_VALUE_HEADS * HEAD_SIZE, HEAD_SIZE),
            w_router,
            gain_attn[:, None],
            gain_moe[:, None],
            jnp.zeros((w_qkv.shape[0], PACK - QKV_COLS - EXPERTS - 2), BF),
        ],
        axis=1,
    )
    packed = to_all(packet, FSDP, N_FSDP).reshape(WIDTH, PACK)
    router = packed[:, QKV_COLS : QKV_COLS + EXPERTS]
    gain_one = packed[:, QKV_COLS + EXPERTS].astype(F32)
    gain_two = packed[:, QKV_COLS + EXPERTS + 1].astype(F32)
    tok_all = to_all(tokens[0], EXP, N_EXP).reshape(SEQ, WIDTH)

    row_of_z = [w_out, lax.ppermute(w_out, "zh", SWAP)]
    rings = [in_order(ring_of_four(block, "y"), y) for block in row_of_z]
    near, far = rings
    zh = lax.axis_index("zh")
    out_mine = jnp.stack([jnp.where(zh == 0, near, far), jnp.where(zh == 0, far, near)], axis=1)
    out_other = core_swap(out_mine)
    full_out = jnp.stack(
        [jnp.where(c == 0, out_mine, out_other), jnp.where(c == 0, out_other, out_mine)], axis=2
    ).reshape(N_EXP, HEAD_COLS, WIDTH)

    cot_packet = jnp.concatenate(
        [cotangent[0], routes[0].astype(BF), jnp.zeros((TOK, SIDE - routes.shape[-1]), BF)], axis=1
    )
    cot_packet, tok_all = lax.optimization_barrier((cot_packet, tok_all))
    cot_all = to_all(cot_packet, EXP, N_EXP).reshape(SEQ, WIDTH + SIDE)
    cot_other = core_swap(cot_all)

    lanes = jnp.arange(QK_COLS, dtype=jnp.int32)
    inv_freq = THETA ** (-2.0 * (lanes % (HEAD_SIZE // 2)).astype(F32) / HEAD_SIZE)
    angles = jnp.arange(SEQ, dtype=jnp.int32).astype(F32)[:, None] * inv_freq[None, :]
    cosine = jnp.cos(angles)
    sine = jnp.sin(angles) * jnp.where(lanes % HEAD_SIZE < HEAD_SIZE // 2, -1.0, 1.0)
    seg_rows, seg_cols = seg_ids[0][:, None], seg_ids
    normed_one, heads, attended, attended_low, stats = attend_call(
        tok_all, packed, gain_one[None], cosine, sine, seg_rows, seg_cols
    )
    attended_all = to_all(attended_low, EXP, N_EXP)

    resid = tok_all.astype(F32) + ein("etk,ekn->tn", attended_all, full_out)
    inv_two = rms_inverse(resid)
    normed_two = (resid * inv_two * gain_two).astype(BF)

    def own_first(value):
        return lax.dynamic_slice_in_dim(
            jnp.concatenate([value, value], axis=1), e * EXP_DEV, EXPERTS, axis=1
        )

    router_turned = jnp.pad(own_first(router), ((0, 0), (0, SIDE - EXPERTS)))
    routes_pair = jnp.concatenate(
        [side[:, WIDTH : WIDTH + routes.shape[-1]] for side in (cot_all, cot_other)]
    ).astype(jnp.int32)
    routes_turned = (routes_pair + (EXPERTS - e * EXP_DEV)) % EXPERTS
    chosen = jnp.any(routes_turned[:, :, None] == jnp.arange(SIDE, dtype=jnp.int32), axis=1).astype(BF)
    out_own, out_par, back_own, back_par, grad_weights = experts_call(
        normed_two, core_swap(normed_two), cot_all, cot_other, chosen, router_turned, weights
    )
    shard_weights = lax.psum_scatter(grad_weights, YZ, scatter_dimension=0, tiled=False)

    def both_cores(own, par):
        return (own.astype(F32) + core_swap(par).astype(F32)).astype(BF).reshape(N_EXP, TOK, -1)

    routed_back = exchange(both_cores(back_own, back_par), EXP)
    routed_total = jnp.sum(routed_back[..., :WIDTH].astype(F32), axis=0)
    sides = routed_back[..., WIDTH : WIDTH + 4 * EXP_DEV].astype(F32).reshape(N_EXP, TOK, 4, EXP_DEV)
    grad_gates = jnp.transpose(jnp.sum(sides, axis=2), (1, 0, 2)).reshape(TOK, EXPERTS)

    def own_rows(value):
        return lax.dynamic_slice_in_dim(value, e * TOK, TOK, axis=0)

    resid_own, inv_two_own, normed_two_own = own_rows(resid), own_rows(inv_two), own_rows(normed_two)
    logits = dot(normed_two_own, router)
    picked = jnp.any(routes[0][:, :, None] == jnp.arange(EXPERTS, dtype=jnp.int32), axis=1)
    masked = jnp.where(picked, logits, LARGE_NEGATIVE)
    exps = jnp.where(picked, jnp.exp(masked - jnp.max(masked, axis=-1, keepdims=True)), 0.0)
    gates = exps / jnp.sum(exps, axis=-1, keepdims=True)
    upstream = cotangent[0].astype(F32)
    grad_logits = (
        gates * (grad_gates - jnp.sum(gates * grad_gates, axis=-1, keepdims=True))
    ).astype(BF)
    router_part = dot(normed_two_own.T, grad_logits)
    grad_normed_two = dot(grad_logits, router.T) + routed_total
    grad_rows, gain_two_part = rms_backward(resid_own, inv_two_own, gain_two, grad_normed_two)
    grad_resid = upstream + grad_rows
    grad_branch = grad_resid.astype(BF)
    grad_attended_own = ein("tn,ekn->etk", grad_branch, full_out).astype(BF)
    branch_blocks = jnp.transpose(grad_branch.reshape(TOK, N_EXP, HEAD_COLS), (1, 0, 2))
    back = exchange(jnp.concatenate([grad_attended_own, branch_blocks], axis=-1), EXP)
    back = back.reshape(SEQ, 2 * HEAD_COLS)
    grad_attended, branch_cols = back[:, :HEAD_COLS], back[:, HEAD_COLS:]

    grad_projected = attend_back_call(
        grad_attended, heads, attended, stats, cosine, sine, seg_rows, seg_cols
    )
    normed_grad_part = contract(grad_projected, packed, ((1,), (1,))).astype(BF)

    out_part, out_back_in = lax.optimization_barrier((both_cores(out_own, out_par), back))
    out_back = exchange(out_part, EXP)
    output = (resid_own + jnp.sum(out_back.astype(F32), axis=0)).astype(BF)

    normed_back = exchange(normed_grad_part.reshape(N_EXP, TOK, WIDTH), EXP)

    def reduce_over_all(parts):
        sent = parts.astype(BF).reshape(N_FSDP, WIDTH // N_FSDP, -1)
        summed = jnp.sum(exchange(sent, FSDP).astype(F32), axis=0).astype(BF)
        return to_all(summed, EXP, N_EXP).astype(F32)

    out_grad_part = ein("etk,tn->ekn", attended_all, branch_cols).reshape(WIDTH, HEAD_COLS)
    first_totals = reduce_over_all(
        jnp.concatenate(
            [
                out_grad_part,
                router_part,
                gain_two_part[:, None],
                jnp.zeros((WIDTH, 256 - HEAD_COLS - EXPERTS - 1), F32),
            ],
            axis=1,
        )
    )
    total_out = jnp.transpose(first_totals[..., :HEAD_COLS], (1, 0, 2)).reshape(-1, WIDTH)
    shared = jnp.sum(first_totals[..., HEAD_COLS : HEAD_COLS + EXPERTS + 1], axis=0)

    grad_normed_one = jnp.sum(normed_back.astype(F32), axis=0)
    own_tokens = tokens[0].astype(F32)
    grad_in, gain_one_part = rms_backward(own_tokens, rms_inverse(own_tokens), gain_one, grad_normed_one)
    grad_tokens = (grad_resid + grad_in).astype(BF)
    qkv_grad_part = contract(normed_one, grad_projected, ((0,), (0,)))[:, :QKV_COLS]
    last_totals = reduce_over_all(
        jnp.concatenate(
            [qkv_grad_part, gain_one_part[:, None], jnp.zeros((WIDTH, PACK - QKV_COLS - 1), F32)], axis=1
        )
    )

    def head_columns(start, width):
        return jnp.transpose(last_totals[..., start : start + width], (1, 0, 2)).reshape(-1, N_EXP * width)

    total_qkv = jnp.concatenate(
        [
            head_columns(0, HEAD_COLS),
            head_columns(HEAD_COLS, HEAD_SIZE),
            head_columns(HEAD_COLS + HEAD_SIZE, HEAD_SIZE),
        ],
        axis=1,
    )
    total_gain_one = jnp.sum(last_totals[..., QKV_COLS], axis=0)

    first_rows, second_rows = shard_weights[:, :96], shard_weights[:, 96:GU_ROWS]
    keep = jnp.where(c == 0, first_rows, second_rows).reshape(-1, FFE)
    arrived = core_swap(jnp.where(c == 0, second_rows, first_rows)).reshape(-1, FFE)
    total_gu = (dot(keep, mine_matrix.T) + dot(arrived, other_matrix.T)).reshape(EXP_DEV, 96, 2 * FFE)
    total_down = jnp.concatenate(
        [shard_weights[:, GU_ROWS + 32 * p : GU_ROWS + 32 * (p + 1)] for p in range(WIDTH // FFE)], axis=2
    ).astype(F32)

    return (
        output[None],
        grad_tokens[None],
        total_gain_one,
        total_qkv,
        total_out,
        shared[:, EXPERTS],
        shared[:, :EXPERTS],
        total_gu,
        total_down,
    )


def solution(mesh):
    fine = Mesh(mesh.devices.reshape(4, 2, 4, 2, 2), ("x", "zl", "y", "zh", "c"))
    rows = P(FSDP, EXP, None)
    weight = P(FSDP, None)
    expert_weight = P(EXP, FSDP, None)
    in_specs = (
        rows,
        P(FSDP, None),
        rows,
        P(FSDP),
        weight,
        weight,
        P(FSDP),
        weight,
        expert_weight,
        expert_weight,
        rows,
    )
    out_specs = (rows, rows, P(FSDP), weight, weight, P(FSDP), weight, expert_weight, expert_weight)
    return jax.shard_map(body, mesh=fine, in_specs=in_specs, out_specs=out_specs, check_vma=False)
```

time: 899 us -> 653 us (0.73)
  waiting for transfers between devices: 416 us -> 288 us
  matrix products: 160 us -> 33.4 us
  Pallas kernels: 0 us -> 95.5 us
  local copies, waits for them, and re-layouts: 139 us -> 63.2 us
  other arithmetic: 92 us -> 65.9 us
  starting transfers between devices: 69.6 us -> 83.7 us
    all_gather x4 -> x1, waiting for transfers between devices: 145 us -> 24.7 us  [body(): weights = lax.all_gather(mixed, YZ, axis=0, tiled=False)]
    dot_general x19 -> x3, matrix products: 131 us -> 16.3 us  [ein(): return jnp.einsum(spec, *args, preferred_element_type=F32)]
    pallas_call x0 -> x3, Pallas kernels: none -> 95.5 us  [the longest x1 71.6 us: experts_call(): pl.pallas_call(expert_kernel, grid=(2 * STEPS + EXP_DEV,), in_specs=[pl.B...]
    all_to_all x8 -> x6, waiting for transfers between devices: 202 us -> 137 us  [exchange(): return lax.all_to_all(value, axes, 0, 0, tiled=True)]
    concatenate x3 -> x1, local copies, waits for them, and re-layouts: 41.2 us -> 0.01 us  [body(): jnp.concatenate([jnp.where(c == 0, gu_mine, gu_recv), jnp.where(c == 0, g...]
    all_to_all x5 -> x6, waiting for transfers between devices: 67.7 us -> 93.9 us  [to_all(): return lax.all_to_all(spread, axes, 0, 0, tiled=True)]
    convert_element_type x5 -> x1, local copies, waits for them, and re-layouts: 25.8 us -> 0.01 us  [body(): gain_one = packed[:, QKV_COLS + EXPERTS].astype(F32)]
    ppermute x0 -> x9, waiting for transfers between devices: none -> 25.6 us  [the longest x2 25.6 us: ring_of_four(): far_low = lax.ppermute(before[:half], axis, ahead)]
  transfers between devices with their start and end apart: 23 -> 30, of which waited for: 16 -> 16; matrix products, arithmetic and copies ran while one was open for 37% -> 23% of each run, Pallas kernels for 0% -> 4%
where the time goes in v2:
time: 653 us; the launch traced here: 645 us
  waiting for transfers between devices  288 us (44%)
  Pallas kernels  95.5 us (15%)
  starting transfers between devices  83.7 us (13%)
  other arithmetic  65.9 us (10%)
  local copies, waits for them, and re-layouts  63.2 us (10%)
  matrix products  33.4 us (5%)
  between operations  15.3 us (2%)
    all_to_all x6, waiting for transfers between devices, exchange(): return lax.all_to_all(value, axes, 0, 0, tiled=True)  137 us
    all_to_all x6, waiting for transfers between devices, to_all(): return lax.all_to_all(spread, axes, 0, 0, tiled=True)  93.9 us
    pallas_call x1, Pallas kernels, experts_call(): pl.pallas_call(expert_kernel, grid=(2 * STEPS + EXP_DEV,), in_specs=[pl.B...  71.6 us
    all_to_all x6, starting transfers between devices, exchange(): return lax.all_to_all(value, axes, 0, 0, tiled=True)  33.2 us
    all_to_all x6, starting transfers between devices, to_all(): return lax.all_to_all(spread, axes, 0, 0, tiled=True)  26.5 us
    ppermute x2, waiting for transfers between devices, ring_of_four(): far_low = lax.ppermute(before[:half], axis, ahead)  25.6 us
    all_gather x1, waiting for transfers between devices, body(): weights = lax.all_gather(mixed, YZ, axis=0, tiled=False)  24.7 us
    unnamed x80, local copies, waits for them, and re-layouts  19.3 us
  transfers between devices with their start and end apart: 30, of which 16 were waited for; matrix products, arithmetic and copies ran while one was open for 23% of the time, Pallas kernels for 4%

profile of v2, /device:TPU:1, one launch (start us, length us, event | category | flops | bytes accessed | tf_op | source)
XLA Modules:
  0.0 644.7 jit_solution(16816561445268062892)
XLA Ops:
  13.6 3.8 collective-permute-start.4
  22.1 4.6 all-to-all-start
  31.2 2.7 collective-permute-start.3
  37.9 3.0 collective-permute-done.2
  44.6 26.8 %all-to-all-done = bf16[8,128,1536]{2,1,0:T(8,128)(2,1)} async-done(((bf16[8,128,1536]{2,1,0:T(8,128)(2,1)}), bf16[8,128,1536]{2,1,0:T(8,128)(2,1)}, u32[]{:S(2)}, u32[]{:S(2)}) %all-to-all-start) | async-done | bytes 3145760 | tf_op jit(solution)/shard_map/all_to_all | solution.py:68
  72.5 5.7 all-to-all-start.1
  82.6 22.6 %collective-permute-done.7 = bf16[48,1536]{1,0:T(8,128)(2,1)S(1)} collective-permute-done((bf16[48,1536]{1,0:T(8,128)(2,1)S(1)}, bf16[48,1536]{1,0:T(8,128)(2,1)S(1)}, u32[]{:S(2)}, u32[]{:S(2)}) %collective-permute-start.7) | collective-permute-done | bytes 147488 | tf_op jit(solution)/shard_map/ppermute | solution.py:499
  106.0 3.3 broadcast_in_dim.55
  109.3 4.6 all-to-all-start.3
  123.2 3.7 fusion.9
  127.5 13.2 %attend.1 = (bf16[1024,1536]{1,0:T(8,128)(2,1)}, bf16[1024,384]{1,0:T(8,128)(2,1)S(1)}, f32[1024,192]{1,0:T(8,128)S(1)}, bf16[1024,192]{1,0:T(8,128)(2,1)S(1)}, f32[1024,8]{1,0:T(8,128)S(1)}) custom-call(bf16[1024,1536]{1,0:T(8,128)(2,1)} %bitcast.3.tokens, bf16[1536,384]{1,0:T(8,128)(2,1)} %bitcast.132, f32[1,1536]{1,0:T(1,128)S(1)} %reshape.371.gain, ...), custom_call_target="tpu_custom_call" | custom-call | flops 3000000000 | bytes 12000000 | tf_op jit(solution)/shard_map/attend/pallas_call | solution.py:375
  143.6 18.9 %all-to-all-done.3 = bf16[8,128,1664]{2,1,0:T(8,128)(2,1)} async-done(((bf16[8,128,1664]{2,1,0:T(8,128)(2,1)}), bf16[8,128,1664]{2,1,0:T(8,128)(2,1)}, u32[]{:S(2)}, u32[]{:S(2)}) %all-to-all-start.3) | async-done | bytes 3407904 | tf_op jit(solution)/shard_map/all_to_all | solution.py:68
  164.6 4.6 all-to-all-start.2
  172.4 2.4 copy.133
  176.2 37.6 %all-to-all-done.2 = bf16[8,1024,192]{1,2,0:T(8,128)(2,1)} async-done(((bf16[8,1024,192]{1,2,0:T(8,128)(2,1)}), bf16[8,1024,192]{1,2,0:T(8,128)(2,1)}, u32[]{:S(2)}, u32[]{:S(2)}) %all-to-all-start.2) | async-done | bytes 3145760 | tf_op jit(solution)/shard_map/all_to_all | solution.py:68
  213.8 9.3 %multiply_reduce_fusion = (f32[1024]{0:T(1024)S(1)}, f32[1024,1536]{1,0:T(8,128)S(1)}) fusion(bf16[8,1024,192]{1,2,0:T(8,128)(2,1)} %all-to-all-done.2, bf16[8,192,1536]{2,1,0:T(8,128)(2,1)} %bitcast.139, bf16[1024,1536]{1,0:T(8,128)(2,1)} %bitcast.3.tokens), kind=kOutput, calls=%fused_computation.9 | convolution fusion | flops 4838128640 | bytes 17305600 | tf_op jit(solution)/shard_map/etk,ekn->tn/dot_general | solution.py:59
  223.1 2.4 multiply_convert_fusion.n_own
  233.8 12.4 %fusion = pred[2048,128]{1,0:T(8,128)(4,1)S(1)} fusion(s32[2048,8]{1,0:T(8,128)} %copy.136), kind=kLoop, calls=%fused_computation.1 | loop fusion | flops 3932160 | bytes 327680 | tf_op jit(solution)/shard_map/reduce_or | solution.py:593
  247.1 24.7 %all-gather.3.cloned.1.call-done = bf16[40,288,512]{2,1,0:T(8,128)(2,1)} async-done(((bf16[5,288,512]{2,1,0:T(8,128)(2,1)}), bf16[40,288,512]{2,1,0:T(8,128)(2,1)}) %all-gather.3.cloned.1.call-update) | async-done | bytes 11796496 | tf_op jit(solution)/shard_map/all_gather | solution.py:528
  271.9 71.6 %experts.1 = (bf16[1024,1536]{1,0:T(8,128)(2,1)}, bf16[1024,1536]{1,0:T(8,128)(2,1)}, bf16[1024,1664]{1,0:T(8,128)(2,1)}, bf16[1024,1664]{1,0:T(8,128)(2,1)}, bf16[8,5,288,512]{3,2,1,0:T(8,128)(2,1)}) custom-call(bf16[1024,1536]{1,0:T(8,128)(2,1)} %multiply_convert_fusion.n_own, bf16[1024,1536]{1,0:T(8,128)(2,1)} %collective-permute-done.10.n_par, ...), custom_call_target="tpu_custom_call" | custom-call | flops 40000000000 | bytes 60000000 | tf_op jit(solution)/shard_map/experts/pallas_call | solution.py:266
  344.8 5.9 collective-permute-done.14
  350.7 5.5 add_convert_fusion
  356.1 5.6 copy.138
  361.7 4.5 all-to-all-start.4
  367.9 47.0 %all-to-all-done.4 = bf16[8,128,1664]{1,2,0:T(8,128)(2,1)} async-done(((bf16[8,128,1664]{1,2,0:T(8,128)(2,1)}), bf16[8,128,1664]{1,2,0:T(8,128)(2,1)}, u32[]{:S(2)}, u32[]{:S(2)}) %all-to-all-start.4) | async-done | bytes 3407904 | tf_op jit(solution)/shard_map/all_to_all | solution.py:72
  415.8 3.3 convert_reduce_fusion.2
  423.5 2.3 fusion.55
  426.0 3.9 fusion.8
  430.8 3.5 all-to-all-start.5
  439.4 7.7 %all-to-all-done.5 = bf16[8,128,384]{1,2,0:T(8,128)(2,1)S(1)} async-done(((bf16[8,128,384]{1,2,0:T(8,128)(2,1)}), bf16[8,128,384]{1,2,0:T(8,128)(2,1)S(1)}, u32[]{:S(2)}, u32[]{:S(2)}) %all-to-all-start.5) | async-done | bytes 786464 | tf_op jit(solution)/shard_map/all_to_all | solution.py:72
  448.4 3.2 convolution_convert_fusion.2
  452.9 6.6 %all-to-all-start.10 = ((bf16[16,96,256]{2,1,0:T(8,128)(2,1)}), bf16[16,96,256]{2,1,0:T(8,128)(2,1)}, u32[]{:S(2)}, u32[]{:S(2)}) async-start(bf16[16,96,256]{2,1,0:T(8,128)(2,1)} %maximum_maximum_fusion.1), calls=%async_computation.10 | async-start | bytes 1572864 | tf_op jit(solution)/shard_map/all_to_all | solution.py:72
  461.9 10.8 %attend_back.1 = bf16[1024,384]{1,0:T(8,128)(2,1)S(1)} custom-call(bf16[1024,192]{1,0:T(8,128)(2,1)S(1)} %slice.132.upstream, bf16[1024,384]{1,0:T(8,128)(2,1)S(1)} %copy-done.7, f32[1024,192]{1,0:T(8,128)S(1)} %copy-done.5, f32[1024,8]{1,0:T(8,128)S(1)} %copy-done.9, bf16[1024,384]{1,0:T(8,128)(2,1)S(1)} %copy-done.7, ...), custom_call_target="tpu_custom_call" | custom-call | flops 4000000000 | bytes 8000000 | tf_op jit(solution)/shard_map/attend_back/pallas_call | solution.py:466
  475.7 3.5 all-to-all-start.11
  479.1 4.8 convolution_convert_fusion
  486.0 5.0 all-to-all-start.7
  491.0 5.4 add_convert_fusion.1
  496.5 39.1 %all-to-all-done.7 = bf16[8,128,1536]{2,1,0:T(8,128)(2,1)} async-done(((bf16[8,128,1536]{2,1,0:T(8,128)(2,1)}), bf16[8,128,1536]{2,1,0:T(8,128)(2,1)}, u32[]{:S(2)}, u32[]{:S(2)}) %all-to-all-start.7) | async-done | bytes 3145760 | tf_op jit(solution)/shard_map/all_to_all | solution.py:72
  535.6 4.7 all-to-all-start.6
  540.6 3.3 fusion.58
  545.8 2.7 convert_reduce_fusion
  550.2 2.4 maximum_maximum_fusion
  552.6 32.0 %all-to-all-done.6 = bf16[8,128,1536]{2,1,0:T(8,128)(2,1)} async-done(((bf16[8,128,1536]{2,1,0:T(8,128)(2,1)}), bf16[8,128,1536]{2,1,0:T(8,128)(2,1)}, u32[]{:S(2)}, u32[]{:S(2)}) %all-to-all-start.6) | async-done | bytes 3145760 | tf_op jit(solution)/shard_map/all_to_all | solution.py:72
  584.6 8.9 %all-to-all-start.8 = ((bf16[16,96,384]{2,1,0:T(8,128)(2,1)}), bf16[16,96,384]{2,1,0:T(8,128)(2,1)S(1)}, u32[]{:S(2)}, u32[]{:S(2)}) async-start(bf16[16,96,384]{2,1,0:T(8,128)(2,1)} %maximum_maximum_fusion), calls=%async_computation.8 | async-start | bytes 2359296 | tf_op jit(solution)/shard_map/all_to_all | solution.py:72
  597.7 2.4 convert_reduce_fusion.1
  602.2 9.9 %all-to-all-done.8 = bf16[16,96,384]{2,1,0:T(8,128)(2,1)S(1)} async-done(((bf16[16,96,384]{2,1,0:T(8,128)(2,1)}), bf16[16,96,384]{2,1,0:T(8,128)(2,1)S(1)}, u32[]{:S(2)}, u32[]{:S(2)}) %all-to-all-start.8) | async-done | bytes 1179680 | tf_op jit(solution)/shard_map/all_to_all | solution.py:72
  613.1 3.5 all-to-all-start.9
  617.8 8.5 %all-to-all-done.9 = bf16[8,96,384]{2,1,0:T(8,128)(2,1)S(1)} async-done(((bf16[8,96,384]{2,1,0:T(8,128)(2,1)}), bf16[8,96,384]{2,1,0:T(8,128)(2,1)S(1)}, u32[]{:S(2)}, u32[]{:S(2)}) %all-to-all-start.9) | async-done | bytes 589856 | tf_op jit(solution)/shard_map/all_to_all | solution.py:68
  (224 shorter events, 105.4 us)
Async XLA Ops:
  7.2 264.7 %all-gather.3.cloned.1.call-start = ((), (), s32[]{:S(2)}) async-start(), calls=%async_computation.14 | async-start | bytes 13271040 | tf_op jit(solution)/shard_map/all_gather | solution.py:528
  9.1 3.0 collective-permute-start.12
  12.1 8.0 %copy-start.16 = (bf16[1,128,1536]{2,1,0:T(8,128)(2,1)S(1)}, bf16[1,128,1536]{2,1,0:T(8,128)(2,1)}, u32[]{:S(2)}) copy-start(bf16[1,128,1536]{2,1,0:T(8,128)(2,1)} %param.11) | copy-start | bytes 1179652
  13.6 20.3 %collective-permute-start.4 = (bf16[96,1536]{1,0:T(8,128)(2,1)S(1)}, bf16[96,1536]{1,0:T(8,128)(2,1)}, u32[]{:S(2)}, u32[]{:S(2)}) collective-permute-start(bf16[96,1536]{1,0:T(8,128)(2,1)S(1)} %copy-done.25), channel_id=1, source_target_pairs={{0,2},{2,0},{1,3},{3,1},{4,6},{6,4},{5,7},{7,5},{8,10},{10,8},{9,1... | collective-permute-start | bytes 884744 | tf_op jit(solution)/shard_map/ppermute | solution.py:551
  17.4 13.7 %collective-permute-start.1 = (bf16[96,1536]{1,0:T(8,128)(2,1)S(1)}, bf16[96,1536]{1,0:T(8,128)(2,1)S(1)}, u32[]{:S(2)}, u32[]{:S(2)}) collective-permute-start(bf16[96,1536]{1,0:T(8,128)(2,1)S(1)} %copy-done.25), channel_id=1, source_target_pairs={{0,4},{4,8},{8,12},{12,0},{1,5},{5,9},{9,13},{13,1},{2,6},{6,10},{... | collective-permute-start | bytes 884744 | tf_op jit(solution)/shard_map/ppermute | solution.py:497
  18.7 12.5 %collective-permute-start = (bf16[96,1536]{1,0:T(8,128)(2,1)S(1)}, bf16[96,1536]{1,0:T(8,128)(2,1)S(1)}, u32[]{:S(2)}, u32[]{:S(2)}) collective-permute-start(bf16[96,1536]{1,0:T(8,128)(2,1)S(1)} %copy-done.25), channel_id=1, source_target_pairs={{0,12},{4,0},{8,4},{12,8},{1,13},{5,1},{9,5},{13,9},{2,14},{6,2},{... | collective-permute-start | bytes 884744 | tf_op jit(solution)/shard_map/ppermute | solution.py:498
  22.1 4.7 copy-start.29
  22.1 4.8 copy-start.30
  22.1 4.9 copy-start.31
  22.1 5.0 copy-start.28
  22.1 5.1 copy-start.3
  22.1 5.4 copy-start.23
  22.1 49.3 %all-to-all-start = ((bf16[8,128,1536]{2,1,0:T(8,128)(2,1)}), bf16[8,128,1536]{2,1,0:T(8,128)(2,1)}, u32[]{:S(2)}, u32[]{:S(2)}) async-start(bf16[8,128,1536]{2,1,0:T(8,128)(2,1)} %broadcast_in_dim.47), calls=%async_computation | async-start | bytes 6291456 | tf_op jit(solution)/shard_map/all_to_all | solution.py:68
  27.5 14.9 %copy-start.26 = (bf16[96,1536]{1,0:T(8,128)(2,1)S(1)}, bf16[96,1536]{1,0:T(8,128)(2,1)}, u32[]{:S(2)}) copy-start(bf16[96,1536]{1,0:T(8,128)(2,1)} %param.16) | copy-start | bytes 884740
  31.1 9.8 %collective-permute-start.2 = (bf16[48,1536]{1,0:T(8,128)(2,1)S(1)}, bf16[48,1536]{1,0:T(8,128)(2,1)S(1)}, u32[]{:S(2)}, u32[]{:S(2)}) collective-permute-start(bf16[48,1536]{1,0:T(8,128)(2,1)S(1)} %slice.122), channel_id=1, source_target_pairs={{0,4},{4,8},{8,12},{12,0},{1,5},{5,9},{9,13},{13,1},{2,6},{6,10},{... | collective-permute-start | bytes 442376 | tf_op jit(solution)/shard_map/ppermute | solution.py:499
  31.2 9.7 %collective-permute-start.3 = (bf16[48,1536]{1,0:T(8,128)(2,1)S(1)}, bf16[48,1536]{1,0:T(8,128)(2,1)S(1)}, u32[]{:S(2)}, u32[]{:S(2)}) collective-permute-start(bf16[48,1536]{1,0:T(8,128)(2,1)S(1)} %slice.123), channel_id=1, source_target_pairs={{0,12},{4,0},{8,4},{12,8},{1,13},{5,1},{9,5},{13,9},{2,14},{6,2},{... | collective-permute-start | bytes 442376 | tf_op jit(solution)/shard_map/ppermute | solution.py:500
  34.0 46.5 %collective-permute-start.5 = (bf16[96,1536]{1,0:T(8,128)(2,1)}, bf16[96,1536]{1,0:T(8,128)(2,1)S(1)}, u32[]{:S(2)}, u32[]{:S(2)}) collective-permute-start(bf16[96,1536]{1,0:T(8,128)(2,1)} %collective-permute-done.4), channel_id=1, source_target_pairs={{0,12},{4,0},{8,4},{12,8},{1,13},{5,1},{9,5},{13,9},{2,14},{6,2},{... | collective-permute-start | bytes 884744 | tf_op jit(solution)/shard_map/ppermute | solution.py:498
  34.2 44.8 %collective-permute-start.6 = (bf16[96,1536]{1,0:T(8,128)(2,1)}, bf16[96,1536]{1,0:T(8,128)(2,1)S(1)}, u32[]{:S(2)}, u32[]{:S(2)}) collective-permute-start(bf16[96,1536]{1,0:T(8,128)(2,1)} %collective-permute-done.4), channel_id=1, source_target_pairs={{0,4},{4,8},{8,12},{12,0},{1,5},{5,9},{9,13},{13,1},{2,6},{6,10},{... | collective-permute-start | bytes 884744 | tf_op jit(solution)/shard_map/ppermute | solution.py:497
  72.5 33.4 %all-to-all-start.1 = ((bf16[16,96,384]{2,1,0:T(8,128)(2,1)}), bf16[16,96,384]{2,1,0:T(8,128)(2,1)S(1)}, u32[]{:S(2)}, u32[]{:S(2)}) async-start(bf16[16,96,384]{2,1,0:T(8,128)(2,1)} %broadcast_in_dim.51), calls=%async_computation.1 | async-start | bytes 2359296 | tf_op jit(solution)/shard_map/all_to_all | solution.py:68
  79.0 26.2 %collective-permute-start.7 = (bf16[48,1536]{1,0:T(8,128)(2,1)S(1)}, bf16[48,1536]{1,0:T(8,128)(2,1)S(1)}, u32[]{:S(2)}, u32[]{:S(2)}) collective-permute-start(bf16[48,1536]{1,0:T(8,128)(2,1)S(1)} %slice.124), channel_id=1, source_target_pairs={{0,4},{4,8},{8,12},{12,0},{1,5},{5,9},{9,13},{13,1},{2,6},{6,10},{... | collective-permute-start | bytes 442376 | tf_op jit(solution)/shard_map/ppermute | solution.py:499
  80.5 24.8 %collective-permute-start.8 = (bf16[48,1536]{1,0:T(8,128)(2,1)S(1)}, bf16[48,1536]{1,0:T(8,128)(2,1)S(1)}, u32[]{:S(2)}, u32[]{:S(2)}) collective-permute-start(bf16[48,1536]{1,0:T(8,128)(2,1)S(1)} %slice.125), channel_id=1, source_target_pairs={{0,12},{4,0},{8,4},{12,8},{1,13},{5,1},{9,5},{13,9},{2,14},{6,2},{... | collective-permute-start | bytes 442376 | tf_op jit(solution)/shard_map/ppermute | solution.py:500
  106.0 21.0 %copy-start.14 = (bf16[16,96,384]{2,1,0:T(8,128)(2,1)}, bf16[16,96,384]{2,1,0:T(8,128)(2,1)S(1)}, u32[]{:S(2)}) copy-start(bf16[16,96,384]{2,1,0:T(8,128)(2,1)S(1)} %all-to-all-done.1) | copy-start | bytes 3538948
  109.3 53.2 %all-to-all-start.3 = ((bf16[8,128,1664]{2,1,0:T(8,128)(2,1)}), bf16[8,128,1664]{2,1,0:T(8,128)(2,1)}, u32[]{:S(2)}, u32[]{:S(2)}) async-start(bf16[8,128,1664]{2,1,0:T(8,128)(2,1)} %broadcast_in_dim.55), calls=%async_computation.3 | async-start | bytes 6815744 | tf_op jit(solution)/shard_map/all_to_all | solution.py:68
  122.5 47.1 %collective-permute-start.9 = (bf16[4,2,96,1536]{3,2,0,1:T(8,128)(2,1)}, bf16[4,2,96,1536]{3,2,0,1:T(8,128)(2,1)}, u32[]{:S(2)}, u32[]{:S(2)}) collective-permute-start(bf16[4,2,96,1536]{3,2,0,1:T(8,128)(2,1)} %pad_maximum_fusion.1), channel_id=1, source_target_pairs={{0,1},{1,0},{2,3},{3,2},{4,5},{5,4},{6,7},{7,6},{8,9},{9,8},{10,11... | collective-permute-start | bytes 7077896 | tf_op jit(solution)/shard_map/ppermute | solution.py:63
  127.0 13.8 %copy-start.2 = (f32[1024,256]{1,0:T(8,128)}, f32[1024,256]{1,0:T(8,128)S(1)}, u32[]{:S(2)}) copy-start(f32[1024,256]{1,0:T(8,128)S(1)} %get-tuple-element.85.sine.all_sine) | copy-start | bytes 3145732
  164.6 5.1 copy-start.12
  164.6 49.2 %all-to-all-start.2 = ((bf16[8,1024,192]{1,2,0:T(8,128)(2,1)}), bf16[8,1024,192]{1,2,0:T(8,128)(2,1)}, u32[]{:S(2)}, u32[]{:S(2)}) async-start(bf16[8,1024,192]{1,2,0:T(8,128)(2,1)} %broadcast_in_dim.54), calls=%async_computation.2 | async-start | bytes 6291456 | tf_op jit(solution)/shard_map/all_to_all | solution.py:68
  169.2 460.6 %reduce-scatter.2.cloned.1.call-start = ((), (), s32[]{:S(2)}) async-start(), calls=%async_computation.13 | async-start | bytes 13271040 | tf_op jit(solution)/shard_map/reduce_scatter | solution.py:597
  174.8 56.5 %collective-permute-start.11 = (bf16[1024,1664]{1,0:T(8,128)(2,1)}, bf16[1024,1664]{1,0:T(8,128)(2,1)}, u32[]{:S(2)}, u32[]{:S(2)}) collective-permute-start(bf16[1024,1664]{1,0:T(8,128)(2,1)} %bitcast.22.g_own), channel_id=1, source_target_pairs={{0,1},{1,0},{2,3},{3,2},{4,5},{5,4},{6,7},{7,6},{8,9},{9,8},{10,11... | collective-permute-start | bytes 10223624 | tf_op jit(solution)/shard_map/ppermute | solution.py:63
  223.1 3.6 copy-start.10
  223.1 5.6 copy-start.15
  226.8 20.4 %collective-permute-start.10 = (bf16[1024,1536]{1,0:T(8,128)(2,1)}, bf16[1024,1536]{1,0:T(8,128)(2,1)}, u32[]{:S(2)}, u32[]{:S(2)}) collective-permute-start(bf16[1024,1536]{1,0:T(8,128)(2,1)} %multiply_convert_fusion.n_own), channel_id=1, source_target_pairs={{0,1},{1,0},{2,3},{3,2},{4,5},{5,4},{6,7},{7,6},{8,9},{9,8},{10,11... | collective-permute-start | bytes 9437192 | tf_op jit(solution)/shard_map/ppermute | solution.py:63
  343.5 7.2 %collective-permute-start.14 = (bf16[1024,1664]{1,0:T(8,128)(2,1)}, bf16[1024,1664]{1,0:T(8,128)(2,1)S(1)}, u32[]{:S(2)}, u32[]{:S(2)}) collective-permute-start(bf16[1024,1664]{1,0:T(8,128)(2,1)} %get-tuple-element.28), channel_id=1, source_target_pairs={{0,1},{1,0},{2,3},{3,2},{4,5},{5,4},{6,7},{7,6},{8,9},{9,8},{10,11... | collective-permute-start | bytes 10223624 | tf_op jit(solution)/shard_map/ppermute | solution.py:63
  361.7 53.2 %all-to-all-start.4 = ((bf16[8,128,1664]{1,2,0:T(8,128)(2,1)}), bf16[8,128,1664]{1,2,0:T(8,128)(2,1)}, u32[]{:S(2)}, u32[]{:S(2)}) async-start(bf16[8,128,1664]{1,2,0:T(8,128)(2,1)} %copy.138), calls=%async_computation.4 | async-start | bytes 6815744 | tf_op jit(solution)/shard_map/all_to_all | solution.py:72
  430.8 16.4 %all-to-all-start.5 = ((bf16[8,128,384]{1,2,0:T(8,128)(2,1)}), bf16[8,128,384]{1,2,0:T(8,128)(2,1)S(1)}, u32[]{:S(2)}, u32[]{:S(2)}) async-start(bf16[8,128,384]{1,2,0:T(8,128)(2,1)} %pad_maximum_fusion.3), calls=%async_computation.5 | async-start | bytes 1572864 | tf_op jit(solution)/shard_map/all_to_all | solution.py:72
  434.4 56.6 %collective-permute-start.13 = (bf16[1024,1536]{1,0:T(8,128)(2,1)}, bf16[1024,1536]{1,0:T(8,128)(2,1)}, u32[]{:S(2)}, u32[]{:S(2)}) collective-permute-start(bf16[1024,1536]{1,0:T(8,128)(2,1)} %get-tuple-element.26), channel_id=1, source_target_pairs={{0,1},{1,0},{2,3},{3,2},{4,5},{5,4},{6,7},{7,6},{8,9},{9,8},{10,11... | collective-permute-start | bytes 9437192 | tf_op jit(solution)/shard_map/ppermute | solution.py:63
  448.3 3.2 copy-start.21
  448.3 3.2 copy-start.22
  451.5 7.9 %copy-start.20 = (bf16[8,128,384]{2,1,0:T(8,128)(2,1)S(1)}, bf16[8,128,384]{2,1,0:T(8,128)(2,1)}, u32[]{:S(2)}) copy-start(bf16[8,128,384]{2,1,0:T(8,128)(2,1)} %copy.144) | copy-start | bytes 2359300
  451.5 7.9 %copy-start.9 = (f32[1024,8]{1,0:T(8,128)S(1)}, f32[1024,8]{1,0:T(8,128)}, u32[]{:S(2)}) copy-start(f32[1024,8]{1,0:T(8,128)} %copy-done.8) | copy-start | bytes 98308
  452.9 20.8 %all-to-all-start.10 = ((bf16[16,96,256]{2,1,0:T(8,128)(2,1)}), bf16[16,96,256]{2,1,0:T(8,128)(2,1)}, u32[]{:S(2)}, u32[]{:S(2)}) async-start(bf16[16,96,256]{2,1,0:T(8,128)(2,1)} %maximum_maximum_fusion.1), calls=%async_computation.10 | async-start | bytes 1572864 | tf_op jit(solution)/shard_map/all_to_all | solution.py:72
  475.7 10.3 %all-to-all-start.11 = ((bf16[8,96,256]{2,1,0:T(8,128)(2,1)}), bf16[8,96,256]{2,1,0:T(8,128)(2,1)S(1)}, u32[]{:S(2)}, u32[]{:S(2)}) async-start(bf16[8,96,256]{2,1,0:T(8,128)(2,1)} %broadcast_in_dim.117), calls=%async_computation.11 | async-start | bytes 786432 | tf_op jit(solution)/shard_map/all_to_all | solution.py:68
  486.0 49.6 %all-to-all-start.7 = ((bf16[8,128,1536]{2,1,0:T(8,128)(2,1)}), bf16[8,128,1536]{2,1,0:T(8,128)(2,1)}, u32[]{:S(2)}, u32[]{:S(2)}) async-start(bf16[8,128,1536]{2,1,0:T(8,128)(2,1)} %bitcast.141), calls=%async_computation.7 | async-start | bytes 6291456 | tf_op jit(solution)/shard_map/all_to_all | solution.py:72
  535.6 49.0 %all-to-all-start.6 = ((bf16[8,128,1536]{2,1,0:T(8,128)(2,1)}), bf16[8,128,1536]{2,1,0:T(8,128)(2,1)}, u32[]{:S(2)}, u32[]{:S(2)}) async-start(bf16[8,128,1536]{2,1,0:T(8,128)(2,1)} %bitcast.130), calls=%async_computation.6 | async-start | bytes 6291456 | tf_op jit(solution)/shard_map/all_to_all | solution.py:72
  584.6 27.5 %all-to-all-start.8 = ((bf16[16,96,384]{2,1,0:T(8,128)(2,1)}), bf16[16,96,384]{2,1,0:T(8,128)(2,1)S(1)}, u32[]{:S(2)}, u32[]{:S(2)}) async-start(bf16[16,96,384]{2,1,0:T(8,128)(2,1)} %maximum_maximum_fusion), calls=%async_computation.8 | async-start | bytes 2359296 | tf_op jit(solution)/shard_map/all_to_all | solution.py:72
  600.1 16.6 %copy-start.18 = (f32[128,1536]{1,0:T(8,128)S(1)}, f32[128,1536]{1,0:T(8,128)}, u32[]{:S(2)}) copy-start(f32[128,1536]{1,0:T(8,128)} %get-tuple-element.69) | copy-start | bytes 2359300
  613.1 13.2 %all-to-all-start.9 = ((bf16[8,96,384]{2,1,0:T(8,128)(2,1)}), bf16[8,96,384]{2,1,0:T(8,128)(2,1)S(1)}, u32[]{:S(2)}, u32[]{:S(2)}) async-start(bf16[8,96,384]{2,1,0:T(8,128)(2,1)} %broadcast_in_dim.115), calls=%async_computation.9 | async-start | bytes 1179648 | tf_op jit(solution)/shard_map/all_to_all | solution.py:68
  632.1 3.3 collective-permute-start.15
  (14 other events, 22.1 us)
Sparse Core Ops, SparseCore 0:
  13.7 258.1 all-gather.2
  343.6 215.6 reduce-scatter.1

commit v3 on v2

v3 whole, which is shorter than its diff:
```python
import math

import jax
import jax.numpy as jnp
from jax import lax
from jax.experimental import pallas as pl
from jax.experimental.pallas import tpu as pltpu
from jax.sharding import Mesh, PartitionSpec as P

QUERY_HEADS = 24
KEY_VALUE_HEADS = 8
HEAD_SIZE = 64
GROUP = QUERY_HEADS // KEY_VALUE_HEADS
FFE = 512
TOP = 8
EXP_DEV = 5
EXPERTS = 40
WIDTH = 1536
TOK = 128
SEQ = 1024
CAP = 48
BLOCKS = 16
N_EXP = 8
N_FSDP = 16
N_YZ = 8
HALF_FFE = FFE // 2
HEAD_COLS = GROUP * HEAD_SIZE
QKV_COLS = HEAD_COLS + 2 * HEAD_SIZE
PACK = 384
DENSE_COLS = 640
SIDE = 128
SLOTS = EXP_DEV * CAP
ROWS = BLOCKS * CAP
PARTS = 4
STEPS = BLOCKS // PARTS
GU_ROWS = WIDTH // N_YZ
MIX_ROWS = GU_ROWS + 32 * WIDTH // FFE
TILE = 256
TILES = SEQ // TILE
QK_COLS = HEAD_COLS + HEAD_SIZE
SCALE = 1.0 / math.sqrt(HEAD_SIZE)

EPS = 1e-06
THETA = 10000.0
LARGE_NEGATIVE = -1e30

EXP = ("x", "zl")
FSDP = ("y", "zh", "c")
YZ = ("y", "zh")
SWAP = ((0, 1), (1, 0))
BF = jnp.bfloat16
F32 = jnp.float32


def dot(a, b):
    return jnp.dot(a, b, preferred_element_type=F32)


def ein(spec, *args):
    return jnp.einsum(spec, *args, preferred_element_type=F32)


def core_swap(value):
    return lax.ppermute(value, "c", SWAP)


def to_all(value, axes, count):
    spread = jnp.broadcast_to(value[None], (count, *value.shape))
    return lax.all_to_all(spread, axes, 0, 0, tiled=True)


def exchange(value, axes):
    return lax.all_to_all(value, axes, 0, 0, tiled=True)


def rms_inverse(features):
    return lax.rsqrt(jnp.mean(features * features, axis=-1, keepdims=True) + EPS)


def rms_backward(features, inverse, gain_vec, grad_normed):
    scaled = gain_vec * grad_normed
    grad_rows = inverse * scaled - features * inverse**3 * jnp.mean(
        features * scaled, axis=-1, keepdims=True
    )
    grad_gain = jnp.sum(features * inverse * grad_normed, axis=0)
    return grad_rows, grad_gain


def parity_matrix(parity):
    rows = jnp.arange(2 * FFE, dtype=jnp.int32)[:, None]
    cols = jnp.arange(FFE, dtype=jnp.int32)[None, :]
    part, rest = cols // HALF_FFE, cols % HALF_FFE
    source = part * FFE + (2 * (rest // 32) + parity) * 32 + rest % 32
    return (rows == source).astype(BF)


def contract(a, b, dims):
    return lax.dot_general(a, b, (dims, ((), ())), preferred_element_type=F32)


def picked_lanes(routes):
    lane = lax.broadcasted_iota(jnp.int32, routes.shape, 1).astype(F32)
    numbers = routes.astype(F32)
    found = lane < 0
    for r in range(TOP):
        found = found | (lane == numbers[:, r : r + 1])
    return found.astype(F32).astype(BF)


def token_square():
    shape = (TOK, TOK)
    return lax.broadcasted_iota(jnp.int32, shape, 0), lax.broadcasted_iota(jnp.int32, shape, 1)


def slots_by_token(picks):
    token, other = token_square()
    ranks = contract(picks, (token < other).astype(BF), ((0,), (0,)))
    named = contract(picks, (token == other).astype(BF), ((0,), (0,)))
    ranks = jnp.where(named > 0, ranks, -1.0).astype(jnp.int32)
    slot = lax.broadcasted_iota(jnp.int32, (CAP, TOK), 0)
    hits = [(slot == ranks[j : j + 1, :]).astype(F32) for j in range(EXP_DEV)]
    return jnp.concatenate(hits, axis=0).astype(BF)


def tokens_by_slot(picks):
    token, other = token_square()
    ranks = jnp.dot((token > other).astype(BF), picks, preferred_element_type=F32).astype(jnp.int32)
    lane = lax.broadcasted_iota(jnp.int32, (TOK, SLOTS), 1)
    hot = jnp.zeros((TOK, SLOTS), F32)
    for j in range(EXP_DEV):
        hit = (picks[:, j : j + 1] > 0) & (lane == ranks[:, j : j + 1] + j * CAP)
        hot = jnp.where(hit, 1.0, hot)
    return hot.astype(BF)


def thirds(value):
    high = value.astype(BF)
    rest = value - high.astype(F32)
    middle = rest.astype(BF)
    return high, middle, (rest - middle.astype(F32)).astype(BF)


def block_rows(ref, start):
    return jnp.concatenate([ref[j, pl.ds(start, CAP), :] for j in range(EXP_DEV)], axis=0)


def expert_weights(ref):
    w_in = ref[:, 0, :GU_ROWS, :].reshape(WIDTH, FFE)
    pieces = [
        ref[:, 0, GU_ROWS + 32 * p : GU_ROWS + 32 * (p + 1), :].reshape(HALF_FFE, FFE)
        for p in range(WIDTH // FFE)
    ]
    return w_in, jnp.concatenate(pieces, axis=1)


def block_start(step, part):
    return pl.multiple_of((step * PARTS + part) * CAP, 16)


def forward_kernel(
    n_own, n_par, routes, router, weights,
    out_own, out_par, x_kept, pre_kept,
    x_slots, gate_slots,
):
    step = pl.program_id(0)

    @pl.when(step < STEPS)
    def dispatch():
        def place(n_ref, part):
            here = slice(part * TOK, (part + 1) * TOK)
            rows = n_ref[here, :]
            picks = picked_lanes(routes[here, :])
            logits = jnp.dot(rows, router[...], preferred_element_type=F32)
            keep = picks > 0
            masked = jnp.where(keep, logits, LARGE_NEGATIVE)
            exps = jnp.where(keep, jnp.exp(masked - jnp.max(masked, axis=-1, keepdims=True)), 0.0)
            gates = exps / jnp.sum(exps, axis=-1, keepdims=True)
            one_hot = slots_by_token(picks)
            spread = sum(jnp.dot(one_hot, third, preferred_element_type=F32) for third in thirds(gates))
            lane = lax.broadcasted_iota(jnp.int32, (CAP, TOK), 1)
            x = jnp.dot(one_hot, rows, preferred_element_type=F32).astype(BF)
            start = block_start(step, part)
            for j in range(EXP_DEV):
                piece = slice(j * CAP, (j + 1) * CAP)
                x_slots[j, pl.ds(start, CAP), :] = x[piece]
                gate_slots[j, pl.ds(start, CAP), :] = jnp.sum(
                    jnp.where(lane == j, spread[piece], 0.0), axis=-1, keepdims=True
                )

        @pl.when(step < STEPS // 2)
        def _():
            for part in range(PARTS):
                place(n_own, part)

        @pl.when(step >= STEPS // 2)
        def _():
            for part in range(PARTS):
                place(n_par, part)

    @pl.when((step >= STEPS) & (step < STEPS + EXP_DEV))
    def experts():
        j = step - STEPS
        w_in, w_back = expert_weights(weights)

        x = x_slots[j]
        gates = gate_slots[j]
        pre = jnp.dot(x, w_in, preferred_element_type=F32)
        x_kept[0] = x
        pre_kept[0, :, :FFE] = pre.astype(BF)
        high, middle, low = thirds(gates)
        lane = lax.broadcasted_iota(jnp.int32, (ROWS, SIDE), 1)
        pre_kept[0, :, FFE:] = jnp.where(
            lane == 0, high.astype(F32), jnp.where(lane == 1, middle.astype(F32), low.astype(F32))
        ).astype(BF)
        gate, up = pre[:, :HALF_FFE], pre[:, HALF_FFE:]
        hidden = (gate * jax.nn.sigmoid(gate) * up).astype(BF).astype(F32)
        gated = (hidden * gates).astype(BF)
        x_slots[j] = jnp.dot(gated, w_back, preferred_element_type=F32).astype(BF)

    @pl.when(step >= STEPS + EXP_DEV)
    def combine():
        block = step - STEPS - EXP_DEV

        def write(out_ref, part):
            here = slice(part * TOK, (part + 1) * TOK)
            hot = tokens_by_slot(picked_lanes(routes[here, :]))
            rows = block_rows(x_slots, block_start(block, part))
            out_ref[here, :] = jnp.dot(hot, rows, preferred_element_type=F32).astype(BF)

        @pl.when(block < STEPS // 2)
        def _():
            for part in range(PARTS):
                write(out_own, part)

        @pl.when(block >= STEPS // 2)
        def _():
            for part in range(PARTS):
                write(out_par, part)


def backward_kernel(
    place_ref, g_own, g_par, routes, x_kept, pre_kept, weights,
    back_own, back_par, grads,
    g_slots, side_slots,
):
    step = pl.program_id(0)

    @pl.when(step < STEPS)
    def dispatch():
        def place(g_ref, part):
            here = slice(part * TOK, (part + 1) * TOK)
            one_hot = slots_by_token(picked_lanes(routes[here, :]))
            g = jnp.dot(one_hot, g_ref[here, :], preferred_element_type=F32).astype(BF)
            start = block_start(step, part)
            for j in range(EXP_DEV):
                g_slots[j, pl.ds(start, CAP), :] = g[j * CAP : (j + 1) * CAP]

        @pl.when(step < STEPS // 2)
        def _():
            for part in range(PARTS):
                place(g_own, part)

        @pl.when(step >= STEPS // 2)
        def _():
            for part in range(PARTS):
                place(g_par, part)

    @pl.when((step >= STEPS) & (step < STEPS + EXP_DEV))
    def experts():
        j = step - STEPS
        w_in, w_back = expert_weights(weights)
        g = g_slots[j]
        pre = pre_kept[0, :, :FFE].astype(F32)
        kept = pre_kept[0, :, FFE:].astype(F32)
        gates = kept[:, 0:1] + kept[:, 1:2] + kept[:, 2:3]
        plain = contract(g, w_back, ((1,), (1,)))
        gate, up = pre[:, :HALF_FFE], pre[:, HALF_FFE:]
        sigmoid = jax.nn.sigmoid(gate)
        silu = gate * sigmoid
        hidden = (silu * up).astype(BF).astype(F32)
        gated = (hidden * gates).astype(BF)
        slope = jnp.sum(hidden * plain, axis=-1, keepdims=True)
        high = slope.astype(BF).astype(F32)
        lane = lax.broadcasted_iota(jnp.int32, (ROWS, SIDE), 1)
        row = lax.broadcasted_iota(jnp.int32, (ROWS, SIDE), 0)
        number = place_ref[0] * EXP_DEV + j
        first_lane = jnp.where(row < ROWS // 2, number, number + EXPERTS)
        side_slots[j] = jnp.where(
            lane == first_lane, high, jnp.where(lane == number + 2 * EXPERTS, slope - high, 0.0)
        ).astype(BF)
        grad_hidden = plain * gates
        grad_pre = jnp.concatenate(
            [grad_hidden * up * sigmoid * (1.0 + gate * (1.0 - sigmoid)), grad_hidden * silu], axis=-1
        ).astype(BF)
        grad_down = contract(gated, g, ((0,), (0,))).astype(BF)
        grad_gate_up = contract(x_kept[0], grad_pre, ((0,), (0,))).astype(BF)
        g_slots[j] = contract(grad_pre, w_in, ((1,), (1,))).astype(BF)
        grads[:, 0, :GU_ROWS, :] = grad_gate_up.reshape(N_YZ, GU_ROWS, FFE)
        for p in range(WIDTH // FFE):
            grads[:, 0, GU_ROWS + 32 * p : GU_ROWS + 32 * (p + 1), :] = grad_down[
                :, p * FFE : (p + 1) * FFE
            ].reshape(N_YZ, 32, FFE)

    @pl.when(step >= STEPS + EXP_DEV)
    def combine():
        block = step - STEPS - EXP_DEV

        def write(back_ref, part):
            here = slice(part * TOK, (part + 1) * TOK)
            hot = tokens_by_slot(picked_lanes(routes[here, :]))
            start = block_start(block, part)
            back_ref[here, :WIDTH] = jnp.dot(
                hot, block_rows(g_slots, start), preferred_element_type=F32
            ).astype(BF)
            back_ref[here, WIDTH:] = jnp.dot(
                hot, block_rows(side_slots, start), preferred_element_type=F32
            ).astype(BF)

        @pl.when(block < STEPS // 2)
        def _():
            for part in range(PARTS):
                write(back_own, part)

        @pl.when(block >= STEPS // 2)
        def _():
            for part in range(PARTS):
                write(back_par, part)


HALF_STEPS = STEPS // 2
LAST = STEPS + EXP_DEV
SPAN = PARTS * TOK


def first(i):
    return (jnp.clip(i, 0, HALF_STEPS - 1), 0)


def second(i):
    return (jnp.clip(i - HALF_STEPS, 0, HALF_STEPS - 1), 0)


def any_block(i):
    return (jnp.where(i < LAST, jnp.clip(i, 0, STEPS - 1), i - LAST), 0)


def expert(i):
    return (jnp.clip(i - STEPS, 0, EXP_DEV - 1), 0, 0)


def expert_split(i):
    return (0, jnp.clip(i - STEPS, 0, EXP_DEV - 1), 0, 0)


def out_first(i):
    return (jnp.clip(i - LAST, 0, HALF_STEPS - 1), 0)


def out_second(i):
    return (jnp.clip(i - LAST - HALF_STEPS, 0, HALF_STEPS - 1), 0)


KEPT = [
    pl.BlockSpec((1, ROWS, WIDTH), expert),
    pl.BlockSpec((1, ROWS, FFE + SIDE), expert),
]
WEIGHTS = pl.BlockSpec((N_YZ, 1, MIX_ROWS, FFE), expert_split)


def experts_forward(n_own, n_par, routes, router, weights):
    shape = jax.ShapeDtypeStruct
    return pl.pallas_call(
        forward_kernel,
        grid=(2 * STEPS + EXP_DEV,),
        in_specs=[
            pl.BlockSpec((SPAN, WIDTH), first),
            pl.BlockSpec((SPAN, WIDTH), second),
            pl.BlockSpec((SPAN, SIDE), any_block),
            pl.BlockSpec((WIDTH, SIDE), lambda i: (0, 0)),
            WEIGHTS,
        ],
        out_specs=[pl.BlockSpec((SPAN, WIDTH), out_first), pl.BlockSpec((SPAN, WIDTH), out_second), *KEPT],
        out_shape=[
            shape((SEQ, WIDTH), BF),
            shape((SEQ, WIDTH), BF),
            shape((EXP_DEV, ROWS, WIDTH), BF),
            shape((EXP_DEV, ROWS, FFE + SIDE), BF),
        ],
        scratch_shapes=[pltpu.VMEM((EXP_DEV, ROWS, WIDTH), BF), pltpu.VMEM((EXP_DEV, ROWS, 1), F32)],
        compiler_params=pltpu.CompilerParams(
            dimension_semantics=("arbitrary",), vmem_limit_bytes=56 * 1024 * 1024
        ),
        cost_estimate=pl.CostEstimate(flops=40_000_000_000, bytes_accessed=40_000_000, transcendentals=1_000_000),
        name="experts_forward",
    )(n_own, n_par, routes, router, weights)


def experts_backward(place, g_own, g_par, routes, kept, weights):
    shape = jax.ShapeDtypeStruct
    return pl.pallas_call(
        backward_kernel,
        grid=(2 * STEPS + EXP_DEV,),
        in_specs=[
            pl.BlockSpec(memory_space=pltpu.SMEM),
            pl.BlockSpec((SPAN, WIDTH), first),
            pl.BlockSpec((SPAN, WIDTH), second),
            pl.BlockSpec((SPAN, SIDE), any_block),
            *KEPT,
            WEIGHTS,
        ],
        out_specs=[
            pl.BlockSpec((SPAN, WIDTH + SIDE), out_first),
            pl.BlockSpec((SPAN, WIDTH + SIDE), out_second),
            WEIGHTS,
        ],
        out_shape=[
            shape((SEQ, WIDTH + SIDE), BF),
            shape((SEQ, WIDTH + SIDE), BF),
            shape((N_YZ, EXP_DEV, MIX_ROWS, FFE), BF),
        ],
        scratch_shapes=[
            pltpu.VMEM((EXP_DEV, ROWS, WIDTH), BF),
            pltpu.VMEM((EXP_DEV, ROWS, SIDE), BF),
        ],
        compiler_params=pltpu.CompilerParams(
            dimension_semantics=("arbitrary",), vmem_limit_bytes=60 * 1024 * 1024
        ),
        cost_estimate=pl.CostEstimate(flops=50_000_000_000, bytes_accessed=60_000_000, transcendentals=1_000_000),
        name="experts_backward",
    )(place.reshape(1), g_own, g_par, routes, *kept, weights)


def swap_halves(value):
    width = value.shape[-1]
    lane = lax.broadcasted_iota(jnp.int32, value.shape, 1)
    return jnp.where(
        lane % HEAD_SIZE < HEAD_SIZE // 2,
        pltpu.roll(value, width - HEAD_SIZE // 2, 1),
        pltpu.roll(value, HEAD_SIZE // 2, 1),
    )


def visible_tile(tile, count, seg_rows, seg_cols):
    row = lax.broadcasted_iota(jnp.int32, (TILE, count), 0) + tile * TILE
    col = lax.broadcasted_iota(jnp.int32, (TILE, count), 1)
    return (col <= row) & (seg_rows[...] == seg_cols[:, :count])


def attend_kernel(
    place_ref, block_0, block_1, block_2, block_3, packed, gain, cosine, sine, seg_rows, seg_cols,
    tokens, normed, heads, attended, attended_low, stats, keys, values,
):
    step = pl.program_id(0)
    distance = lax.rem(step - place_ref[0] + TILES, TILES)
    for k, block in enumerate((block_0, block_1, block_2, block_3)):

        @pl.when(distance == k)
        def _(block=block):
            tokens[...] = block[...]

    features = tokens[:, :WIDTH].astype(F32)
    inverse = lax.rsqrt(jnp.mean(features * features, axis=-1, keepdims=True) + EPS)
    rows = (features * inverse * gain[...]).astype(BF)
    normed[...] = rows
    projected = jnp.dot(rows, packed[...], preferred_element_type=F32)
    turned = projected[:, :QK_COLS]
    turned = (turned * cosine[...] + swap_halves(turned) * sine[...]).astype(BF)
    value_rows = projected[:, QK_COLS:QKV_COLS].astype(BF)
    heads[:, :QK_COLS] = turned
    heads[:, QK_COLS:] = jnp.concatenate([value_rows, jnp.zeros_like(value_rows)], axis=1)
    here = pl.ds(pl.multiple_of(step * TILE, TILE), TILE)
    keys[here, :] = turned[:, HEAD_COLS:]
    values[here, :] = value_rows

    for tile in range(TILES):

        @pl.when(step == tile)
        def _(tile=tile):
            count = (tile + 1) * TILE
            visible = visible_tile(tile, count, seg_rows, seg_cols)
            key_rows, value_all = keys[:count, :], values[:count, :]
            parts = []
            for h in range(GROUP):
                query = turned[:, h * HEAD_SIZE : (h + 1) * HEAD_SIZE]
                scores = contract(query, key_rows, ((1,), (1,))) * SCALE
                scores = jnp.where(visible, scores, LARGE_NEGATIVE)
                top = jnp.max(scores, axis=-1, keepdims=True)
                weights = jnp.where(visible, jnp.exp(scores - top), 0.0)
                total = jnp.sum(weights, axis=-1, keepdims=True)
                soft = (weights / total).astype(BF)
                parts.append(jnp.dot(soft, value_all, preferred_element_type=F32))
                stats[:, 2 * h : 2 * h + 1] = top
                stats[:, 2 * h + 1 : 2 * h + 2] = total
            result = jnp.concatenate(parts, axis=1)
            attended[...] = result
            attended_low[...] = result.astype(BF)


def attend_call(place, blocks, packed, gain, cosine, sine, seg_rows, seg_cols):
    def rows(i):
        return (i, 0)

    def whole(i):
        return (0, 0)

    shape = jax.ShapeDtypeStruct
    return pl.pallas_call(
        attend_kernel,
        grid=(TILES,),
        in_specs=[
            pl.BlockSpec(memory_space=pltpu.SMEM),
            *[pl.BlockSpec((TILE, WIDTH + SIDE), whole)] * TILES,
            pl.BlockSpec((WIDTH, PACK), whole),
            pl.BlockSpec((1, WIDTH), whole),
            pl.BlockSpec((TILE, QK_COLS), rows),
            pl.BlockSpec((TILE, QK_COLS), rows),
            pl.BlockSpec((TILE, 1), rows),
            pl.BlockSpec((1, SEQ), whole),
        ],
        out_specs=[
            pl.BlockSpec((TILE, WIDTH + SIDE), rows),
            pl.BlockSpec((TILE, WIDTH), rows),
            pl.BlockSpec((TILE, PACK), rows),
            pl.BlockSpec((TILE, HEAD_COLS), rows),
            pl.BlockSpec((TILE, HEAD_COLS), rows),
            pl.BlockSpec((TILE, 8), rows),
        ],
        out_shape=[
            shape((SEQ, WIDTH + SIDE), BF),
            shape((SEQ, WIDTH), BF),
            shape((SEQ, PACK), BF),
            shape((SEQ, HEAD_COLS), F32),
            shape((SEQ, HEAD_COLS), BF),
            shape((SEQ, 8), F32),
        ],
        scratch_shapes=[pltpu.VMEM((SEQ, HEAD_SIZE), BF), pltpu.VMEM((SEQ, HEAD_SIZE), BF)],
        compiler_params=pltpu.CompilerParams(
            dimension_semantics=("arbitrary",), vmem_limit_bytes=48 * 1024 * 1024
        ),
        cost_estimate=pl.CostEstimate(flops=13_000_000_000, bytes_accessed=12_000_000, transcendentals=3_000_000),
        name="attend",
    )(place.reshape(1), *blocks, packed, gain, cosine, sine, seg_rows, seg_cols)


def attend_back_kernel(
    upstream, heads, attended, stats, all_heads, cosine, sine, all_cosine, all_sine, seg_rows, seg_cols,
    grads, grad_keys, grad_values,
):
    step = pl.program_id(0)

    @pl.when(step == 0)
    def _():
        grad_keys[...] = jnp.zeros_like(grad_keys)
        grad_values[...] = jnp.zeros_like(grad_values)

    for tile in range(TILES):

        @pl.when(step == tile)
        def _(tile=tile):
            count = (tile + 1) * TILE
            visible = visible_tile(tile, count, seg_rows, seg_cols)
            key_rows = all_heads[:count, HEAD_COLS:QK_COLS]
            value_rows = all_heads[:count, QK_COLS:QKV_COLS]
            parts = []
            sum_keys, sum_values = 0.0, 0.0
            for h in range(GROUP):
                columns = slice(h * HEAD_SIZE, (h + 1) * HEAD_SIZE)
                query, grad = heads[:, columns], upstream[:, columns]
                scores = contract(query, key_rows, ((1,), (1,))) * SCALE
                scores = jnp.where(visible, scores, LARGE_NEGATIVE)
                top, total = stats[:, 2 * h : 2 * h + 1], stats[:, 2 * h + 1 : 2 * h + 2]
                soft = jnp.where(visible, jnp.exp(scores - top), 0.0) / total
                delta = jnp.sum(grad.astype(F32) * attended[:, columns], axis=-1, keepdims=True)
                grad_probs = contract(grad, value_rows, ((1,), (1,)))
                grad_scores = (soft * (grad_probs - delta)).astype(BF)
                parts.append(jnp.dot(grad_scores, key_rows, preferred_element_type=F32) * SCALE)
                sum_keys = sum_keys + contract(grad_scores, query, ((0,), (0,)))
                sum_values = sum_values + contract(soft.astype(BF), grad, ((0,), (0,)))
            grad_keys[:count, :] += sum_keys * SCALE
            grad_values[:count, :] += sum_values
            turned = jnp.concatenate([*parts, jnp.zeros_like(parts[0])], axis=1)
            turned = turned * cosine[...] - swap_halves(turned) * sine[...]
            grads[tile * TILE : count, :HEAD_COLS] = turned[:, :HEAD_COLS].astype(BF)

    @pl.when(step == TILES - 1)
    def _():
        both = jnp.concatenate([grad_keys[...], grad_values[...]], axis=1)
        turned = both * all_cosine[...] - swap_halves(both) * all_sine[...]
        lane = lax.broadcasted_iota(jnp.int32, both.shape, 1)
        both = jnp.where(lane < HEAD_SIZE, turned, both)
        grads[:, HEAD_COLS:] = jnp.concatenate([both, jnp.zeros((SEQ, HEAD_SIZE), F32)], axis=1).astype(BF)


def attend_back_call(upstream, heads, attended, stats, cosine, sine, seg_rows, seg_cols):
    def rows(i):
        return (i, 0)

    def whole(i):
        return (0, 0)

    return pl.pallas_call(
        attend_back_kernel,
        grid=(TILES,),
        in_specs=[
            pl.BlockSpec((TILE, 2 * HEAD_COLS), rows),
            pl.BlockSpec((TILE, PACK), rows),
            pl.BlockSpec((TILE, HEAD_COLS), rows),
            pl.BlockSpec((TILE, 8), rows),
            pl.BlockSpec((SEQ, PACK), whole),
            pl.BlockSpec((TILE, QK_COLS), rows),
            pl.BlockSpec((TILE, QK_COLS), rows),
            pl.BlockSpec((SEQ, 2 * HEAD_SIZE), whole),
            pl.BlockSpec((SEQ, 2 * HEAD_SIZE), whole),
            pl.BlockSpec((TILE, 1), rows),
            pl.BlockSpec((1, SEQ), whole),
        ],
        out_specs=pl.BlockSpec((SEQ, PACK), whole),
        out_shape=jax.ShapeDtypeStruct((SEQ, PACK), BF),
        scratch_shapes=[pltpu.VMEM((SEQ, HEAD_SIZE), F32), pltpu.VMEM((SEQ, HEAD_SIZE), F32)],
        compiler_params=pltpu.CompilerParams(
            dimension_semantics=("arbitrary",), vmem_limit_bytes=48 * 1024 * 1024
        ),
        cost_estimate=pl.CostEstimate(flops=11_000_000_000, bytes_accessed=8_000_000, transcendentals=3_000_000),
        name="attend_back",
    )(upstream, heads, attended, stats, heads, cosine, sine, cosine, sine, seg_rows, seg_cols)


def rotation(count, by):
    return [(i, (i + by) % count) for i in range(count)]


def straight_four(block, axis):
    return [block, *(lax.ppermute(block, axis, rotation(4, k)) for k in (3, 2, 1))]


def pair_up(own, other, index, axis):
    return jnp.where(index == 0, jnp.stack([own, other], axis=axis), jnp.stack([other, own], axis=axis))


def after(value, *others):
    return lax.optimization_barrier((value, *others))[0]


def gather_pairs(value, partner, index, axis, *others):
    pair = after(pair_up(value, partner, index, 0), *others)
    return lax.all_to_all(jnp.broadcast_to(pair[None], (4, *pair.shape)), axis, 0, 0, tiled=True)


def gather_experts(value, *others):
    partner = lax.ppermute(value, "zl", SWAP)
    return gather_pairs(value, partner, lax.axis_index("zl"), "x", *others).reshape(N_EXP, *value.shape)


def sum_start(*parts):
    x = lax.axis_index("x")
    rows = 2 * TOK

    def rows_for(k):
        start = lax.rem(x + k, 4) * rows
        return sum(lax.dynamic_slice_in_dim(part, start, rows).astype(F32) for part in parts)

    return rows_for(0), [rows_for(k).astype(BF) for k in (2, 1, 3)]


def sum_send(sent):
    return [lax.ppermute(value, "x", rotation(4, k)) for k, value in zip((2, 1, 3), sent)]


def sum_finish(own, arrived):
    zl = lax.axis_index("zl")
    total = own + sum(value.astype(F32) for value in arrived)
    keep = lax.dynamic_slice_in_dim(total, zl * TOK, TOK)
    send = lax.dynamic_slice_in_dim(total, (1 - zl) * TOK, TOK).astype(BF)
    return keep + lax.ppermute(send, "zl", SWAP).astype(F32)


def body(tokens, seg_ids, routes, gain_attn, w_qkv, w_out, gain_moe, w_router, w_gate_up, w_down, cotangent):
    e = lax.axis_index(EXP)
    c = lax.axis_index("c")
    zh = lax.axis_index("zh")

    mine_matrix, other_matrix = parity_matrix(c), parity_matrix(1 - c)
    flat_gu = w_gate_up.reshape(EXP_DEV * 96, 2 * FFE)
    gu_other = dot(flat_gu, other_matrix).astype(BF).reshape(EXP_DEV, 96, FFE)
    gu_recv = core_swap(gu_other)
    gu_mine = dot(flat_gu, mine_matrix).astype(BF).reshape(EXP_DEV, 96, FFE)
    mixed = jnp.concatenate(
        [
            pair_up(gu_mine, gu_recv, c, 1).reshape(EXP_DEV, GU_ROWS, FFE),
            *(w_down[:, :, p * FFE : (p + 1) * FFE] for p in range(WIDTH // FFE)),
        ],
        axis=1,
    )

    def own_columns(start, width):
        return lax.dynamic_slice_in_dim(w_qkv, start + e * width, width, axis=1)

    packet = jnp.concatenate(
        [
            own_columns(0, HEAD_COLS),
            own_columns(WIDTH, HEAD_SIZE),
            own_columns(WIDTH + KEY_VALUE_HEADS * HEAD_SIZE, HEAD_SIZE),
            w_router,
            gain_attn[:, None],
            gain_moe[:, None],
            jnp.zeros((w_qkv.shape[0], PACK - QKV_COLS - EXPERTS - 2), BF),
        ],
        axis=1,
    )
    packet = pair_up(packet, core_swap(packet), c, 0)
    mixed, packet = lax.optimization_barrier((mixed, packet))
    weights = lax.all_gather(mixed, YZ, axis=0, tiled=False)
    packet = pair_up(packet, lax.ppermute(packet, "zh", SWAP), zh, 0)

    tok_packet = jnp.concatenate(
        [tokens[0], routes[0].astype(BF), jnp.zeros((TOK, SIDE - routes.shape[-1]), BF)], axis=1
    )
    tok_pair = pair_up(tok_packet, lax.ppermute(tok_packet, "zl", SWAP), lax.axis_index("zl"), 0)
    tok_pair = after(tok_pair.reshape(2 * TOK, -1), packet)
    tok_blocks = straight_four(tok_pair, "x")
    y = lax.axis_index("y")
    packed = jnp.zeros((4, *packet.shape), BF)
    for k, piece in enumerate(straight_four(packet, "y")):
        packed = lax.dynamic_update_slice(packed, piece[None], (lax.rem(y + k, 4), 0, 0, 0, 0))
    packed = packed.reshape(WIDTH, PACK)
    router = packed[:, QKV_COLS : QKV_COLS + EXPERTS]
    gain_one = packed[:, QKV_COLS + EXPERTS].astype(F32)
    gain_two = packed[:, QKV_COLS + EXPERTS + 1].astype(F32)

    out_partner = lax.ppermute(w_out, ("zl", "zh"), ((0, 3), (1, 2), (2, 1), (3, 0)))
    out_mine = gather_pairs(w_out, out_partner, zh, "y")
    tok_blocks, packed, out_mine = lax.optimization_barrier((tok_blocks, packed, out_mine))

    lanes = jnp.arange(QK_COLS, dtype=jnp.int32)
    inv_freq = THETA ** (-2.0 * (lanes % (HEAD_SIZE // 2)).astype(F32) / HEAD_SIZE)
    angles = jnp.arange(SEQ, dtype=jnp.int32).astype(F32)[:, None] * inv_freq[None, :]
    cosine = jnp.cos(angles)
    sine = jnp.sin(angles) * jnp.where(lanes % HEAD_SIZE < HEAD_SIZE // 2, -1.0, 1.0)
    seg_rows, seg_cols = seg_ids[0][:, None], seg_ids
    tok_all, normed_one, heads, attended, attended_low, stats = attend_call(
        lax.axis_index("x"), tok_blocks, packed, gain_one[None], cosine, sine, seg_rows, seg_cols
    )
    routes_all = tok_all[:, WIDTH:]
    routes_pair = jnp.concatenate([routes_all, core_swap(routes_all)]).astype(jnp.int32)
    routes_turned = ((routes_pair + (EXPERTS - e * EXP_DEV)) % EXPERTS).astype(BF)
    attended_all = to_all(after(attended_low, routes_turned), EXP, N_EXP)
    full_out = jnp.zeros((4, 2, 2, *w_out.shape), BF)
    full_out = lax.dynamic_update_slice(full_out, out_mine[:, :, None], (0, 0, c, 0, 0))
    full_out = lax.dynamic_update_slice(full_out, core_swap(out_mine)[:, :, None], (0, 0, 1 - c, 0, 0))
    full_out = full_out.reshape(N_EXP, HEAD_COLS, WIDTH)

    features = tok_all[:, :WIDTH].astype(F32)
    resid = features + ein("etk,ekn->tn", attended_all, full_out)
    inv_two = rms_inverse(resid)
    normed_two = (resid * inv_two * gain_two).astype(BF)

    cot_partner = lax.ppermute(after(cotangent[0], packed), "zl", SWAP)
    cot_pair = after(pair_up(cotangent[0], cot_partner, lax.axis_index("zl"), 0), weights)
    cot_all = lax.all_gather(cot_pair, "x", axis=0, tiled=False).reshape(SEQ, WIDTH)

    def own_first(value):
        return lax.dynamic_slice_in_dim(
            jnp.concatenate([value, value], axis=1), e * EXP_DEV, EXPERTS, axis=1
        )

    router_turned = jnp.pad(own_first(router), ((0, 0), (0, SIDE - EXPERTS)))
    out_own, out_par, *kept = experts_forward(
        normed_two, core_swap(normed_two), routes_turned, router_turned, weights
    )

    out_rows, out_sent = sum_start(out_own, core_swap(out_par))
    routes_turned, out_sent = lax.optimization_barrier((routes_turned, out_sent))
    out_arrived = sum_send(out_sent)
    back_own, back_par, grad_weights = experts_backward(
        e, cot_all, core_swap(cot_all), routes_turned, kept, weights
    )
    grad_weights, out_arrived = lax.optimization_barrier((grad_weights, out_arrived))
    shard_weights = lax.psum_scatter(grad_weights, YZ, scatter_dimension=0, tiled=False)

    back_rows, back_sent = sum_start(back_own, core_swap(back_par))
    routed_back = sum_finish(back_rows, sum_send(back_sent))
    routed_total, sides = routed_back[:, :WIDTH], routed_back[:, WIDTH:]
    grad_gates = sides[:, :EXPERTS] + sides[:, EXPERTS : 2 * EXPERTS] + sides[:, 2 * EXPERTS : 3 * EXPERTS]

    def own_rows(value):
        return lax.dynamic_slice_in_dim(value, e * TOK, TOK, axis=0)

    resid_own, inv_two_own, normed_two_own = own_rows(resid), own_rows(inv_two), own_rows(normed_two)
    logits = dot(normed_two_own, router)
    picked = jnp.any(routes[0][:, :, None] == jnp.arange(EXPERTS, dtype=jnp.int32), axis=1)
    masked = jnp.where(picked, logits, LARGE_NEGATIVE)
    exps = jnp.where(picked, jnp.exp(masked - jnp.max(masked, axis=-1, keepdims=True)), 0.0)
    gates = exps / jnp.sum(exps, axis=-1, keepdims=True)
    upstream = cotangent[0].astype(F32)
    grad_logits = (
        gates * (grad_gates - jnp.sum(gates * grad_gates, axis=-1, keepdims=True))
    ).astype(BF)
    router_part = dot(normed_two_own.T, grad_logits)
    grad_normed_two = dot(grad_logits, router.T) + routed_total
    grad_rows, gain_two_part = rms_backward(resid_own, inv_two_own, gain_two, grad_normed_two)
    grad_resid = upstream + grad_rows
    grad_branch = grad_resid.astype(BF)
    grad_attended_own = ein("tn,ekn->etk", grad_branch, full_out).astype(BF)
    branch_blocks = jnp.transpose(grad_branch.reshape(TOK, N_EXP, HEAD_COLS), (1, 0, 2))
    back = exchange(jnp.concatenate([grad_attended_own, branch_blocks], axis=-1), EXP)
    back = back.reshape(SEQ, 2 * HEAD_COLS)
    output = (resid_own + sum_finish(out_rows, after(out_arrived, back))).astype(BF)

    grad_projected = attend_back_call(
        back, heads, attended, stats, cosine, sine, seg_rows, seg_cols
    )

    columns = [
        ein("etk,tn->ekn", attended_all, back[:, HEAD_COLS:]).reshape(WIDTH, HEAD_COLS),
        contract(normed_one, grad_projected, ((0,), (0,)))[:, :QKV_COLS],
        router_part,
        gain_two_part[:, None],
        jnp.zeros((WIDTH, DENSE_COLS - HEAD_COLS - QKV_COLS - EXPERTS - 1), F32),
    ]
    parts = jnp.concatenate([column.astype(BF) for column in columns], axis=1)
    parts = parts.reshape(N_YZ, 2, WIDTH // N_FSDP, DENSE_COLS)
    grad_projected, parts = lax.optimization_barrier((grad_projected, parts))
    normed_grad_part = contract(grad_projected, packed, ((1,), (1,)))
    gain_one_part = jnp.sum(features * rms_inverse(features) * normed_grad_part, axis=0)
    gain_blocks = gain_one_part.astype(BF).reshape(N_YZ, 2, WIDTH // N_FSDP, 1)
    parts = jnp.where(jnp.arange(DENSE_COLS, dtype=jnp.int32) == DENSE_COLS - 1, gain_blocks, parts)
    keep = jnp.where(c == 0, parts[:, 0], parts[:, 1])
    arrived = core_swap(jnp.where(c == 0, parts[:, 1], parts[:, 0]))
    parts = (keep.astype(F32) + arrived.astype(F32)).astype(BF)
    normed_rows, normed_sent = sum_start(normed_grad_part.astype(BF))
    normed_arrived = sum_send(normed_sent)
    exchanged = exchange(parts, YZ)

    first_rows, second_rows = shard_weights[:, :96], shard_weights[:, 96:GU_ROWS]
    keep = jnp.where(c == 0, first_rows, second_rows).reshape(-1, FFE)
    arrived = core_swap(jnp.where(c == 0, second_rows, first_rows)).reshape(-1, FFE)
    total_gu = (dot(keep, mine_matrix.T) + dot(arrived, other_matrix.T)).reshape(EXP_DEV, 96, 2 * FFE)
    total_down = jnp.concatenate(
        [shard_weights[:, GU_ROWS + 32 * p : GU_ROWS + 32 * (p + 1)] for p in range(WIDTH // FFE)], axis=2
    ).astype(F32)

    exchanged, normed_arrived, total_gu, total_down = lax.optimization_barrier(
        (exchanged, normed_arrived, total_gu, total_down)
    )
    summed = jnp.sum(exchanged.astype(F32), axis=0).astype(BF)
    totals = to_all(summed, EXP, N_EXP).astype(F32)
    grad_normed_one = sum_finish(normed_rows, after(normed_arrived, summed))

    def head_columns(start, width):
        return jnp.transpose(totals[..., start : start + width], (1, 0, 2)).reshape(-1, N_EXP * width)

    total_out = head_columns(0, HEAD_COLS)
    total_qkv = jnp.concatenate(
        [
            head_columns(HEAD_COLS, HEAD_COLS),
            head_columns(2 * HEAD_COLS, HEAD_SIZE),
            head_columns(2 * HEAD_COLS + HEAD_SIZE, HEAD_SIZE),
        ],
        axis=1,
    )
    shared = jnp.sum(totals[..., HEAD_COLS + QKV_COLS :], axis=0)

    own_tokens = tokens[0].astype(F32)
    grad_in, _ = rms_backward(own_tokens, rms_inverse(own_tokens), gain_one, grad_normed_one)
    grad_tokens = (grad_resid + grad_in).astype(BF)

    return (
        output[None],
        grad_tokens[None],
        shared[:, -1],
        total_qkv,
        total_out,
        shared[:, EXPERTS],
        shared[:, :EXPERTS],
        total_gu,
        total_down,
    )


def solution(mesh):
    fine = Mesh(mesh.devices.reshape(4, 2, 4, 2, 2), ("x", "zl", "y", "zh", "c"))
    rows = P(FSDP, EXP, None)
    weight = P(FSDP, None)
    expert_weight = P(EXP, FSDP, None)
    in_specs = (
        rows,
        P(FSDP, None),
        rows,
        P(FSDP),
        weight,
        weight,
        P(FSDP),
        weight,
        expert_weight,
        expert_weight,
        rows,
    )
    out_specs = (rows, rows, P(FSDP), weight, weight, P(FSDP), weight, expert_weight, expert_weight)
    return jax.shard_map(body, mesh=fine, in_specs=in_specs, out_specs=out_specs, check_vma=False)
```

time: 653 us -> 561 us (0.86)
  waiting for transfers between devices: 288 us -> 231 us
  starting transfers between devices: 83.7 us -> 62.7 us
  other arithmetic: 65.9 us -> 48.1 us
  Pallas kernels: 95.5 us -> 112 us
  local copies, waits for them, and re-layouts: 63.2 us -> 53.8 us
    all_to_all x6 -> x2, waiting for transfers between devices: 137 us -> 6.94 us  [exchange(): return lax.all_to_all(value, axes, 0, 0, tiled=True)]
    ppermute x9 -> x22, waiting for transfers between devices: 25.6 us -> 144 us  [the longest x6 52.9 us: straight_four(): lax.ppermute(block, axis, rotation(4, k))]
    all_to_all x6 -> x2, waiting for transfers between devices: 93.9 us -> 47.5 us  [to_all(): return lax.all_to_all(spread, axes, 0, 0, tiled=True)]
    all_to_all x6 -> x2, starting transfers between devices: 33.2 us -> 7.52 us  [exchange(): return lax.all_to_all(value, axes, 0, 0, tiled=True)]
    all_to_all x6 -> x2, starting transfers between devices: 26.5 us -> 9.64 us  [to_all(): return lax.all_to_all(spread, axes, 0, 0, tiled=True)]
    pallas_call x2 -> x3, Pallas kernels: 84.8 us -> 101 us  [the longest x1 46.6 us: experts_backward(): pl.pallas_call(backward_kernel, grid=(2 * STEPS + EXP_DEV,), in_specs=[pl...]
    ppermute x9 -> x22, starting transfers between devices: 13.6 us -> 28.2 us  [the longest x9 13.9 us: sum_send(): lax.ppermute(value, 'x', rotation(4, k))]
    reduce_or x1 -> x0, other arithmetic: 12.4 us -> none  [body(): jnp.any(routes_turned[:, :, None] == jnp.arange(SIDE, dtype=jnp.int32), a...]
  transfers between devices with their start and end apart: 30 -> 40, of which waited for: 16 -> 20; matrix products, arithmetic and copies ran while one was open for 23% -> 19% of each run, Pallas kernels for 4% -> 20%
where the time goes in v3:
time: 561 us; the launch traced here: 554 us
  waiting for transfers between devices  231 us (41%)
  Pallas kernels  112 us (20%)
  starting transfers between devices  62.7 us (11%)
  local copies, waits for them, and re-layouts  53.8 us (10%)
  other arithmetic  48.1 us (9%)
  matrix products  32.5 us (6%)
  between operations  14.8 us (3%)
    ppermute x6, waiting for transfers between devices, straight_four(): lax.ppermute(block, axis, rotation(4, k))  52.9 us
    ppermute x9, waiting for transfers between devices, sum_send(): lax.ppermute(value, 'x', rotation(4, k))  50.7 us
    all_to_all x2, waiting for transfers between devices, to_all(): return lax.all_to_all(spread, axes, 0, 0, tiled=True)  47.5 us
    pallas_call x1, Pallas kernels, experts_backward(): pl.pallas_call(backward_kernel, grid=(2 * STEPS + EXP_DEV,), in_specs=[pl...  46.6 us
    pallas_call x1, Pallas kernels, experts_forward(): pl.pallas_call(forward_kernel, grid=(2 * STEPS + EXP_DEV,), in_specs=[pl....  40.3 us
    ppermute x3, waiting for transfers between devices, sum_finish(): return keep + lax.ppermute(send, 'zl', SWAP).astype(F32)  19.6 us
    dot_general x3, matrix products, ein(): return jnp.einsum(spec, *args, preferred_element_type=F32)  17 us
    unnamed x77, local copies, waits for them, and re-layouts  15.6 us
  transfers between devices with their start and end apart: 40, of which 20 were waited for; matrix products, arithmetic and copies ran while one was open for 19% of the time, Pallas kernels for 20%

profile of v3, /device:TPU:1, one launch (start us, length us, event | category | flops | bytes accessed | tf_op | source)
XLA Modules:
  0.0 554.2 jit_solution(4638947397614706125)
XLA Ops:
  18.0 3.9 collective-permute-start.10
  22.3 6.9 %collective-permute-done.10 = bf16[96,1536]{1,0:T(8,128)(2,1)S(1)} collective-permute-done((bf16[96,1536]{1,0:T(8,128)(2,1)S(1)}, bf16[96,1536]{1,0:T(8,128)(2,1)S(1)}, u32[]{:S(2)}, u32[]{:S(2)}) %collective-permute-start.10) | collective-permute-done | bytes 294944 | tf_op jit(solution)/shard_map/ppermute | solution.py:730
  30.9 4.8 all-to-all-start
  37.0 5.6 %fusion.12 = (f32[1024,256]{1,0:T(8,128)}, f32[1024,256]{1,0:T(8,128)}) fusion(f32[256]{0:T(256)S(1)} %get-tuple-element.178, f32[256]{0:T(256)S(1)} %get-tuple-element.179, f32[1024]{0:T(1024)S(1)} %iota_convert_fusion), kind=kLoop, calls=%fused_computation.45 | loop fusion | flops 524288 | bytes 2103296 | tf_op jit(solution)/shard_map/mul | solution.py:738
  42.6 3.7 collective-permute-done.3
  46.3 2.7 collective-permute-start.7
  50.3 2.5 collective-permute-start.4
  53.5 35.5 %collective-permute-done.7 = bf16[2,2,96,384]{3,2,1,0:T(8,128)(2,1)S(1)} collective-permute-done((bf16[2,2,96,384]{3,2,1,0:T(8,128)(2,1)S(1)}, bf16[2,2,96,384]{3,2,1,0:T(8,128)(2,1)S(1)}, u32[]{:S(2)}, u32[]{:S(2)}) %collective-permute-start.7) | collective-permute-done | bytes 294944 | tf_op jit(solution)/shard_map/ppermute | solution.py:633
  90.5 5.8 %collective-permute-done.9 = bf16[2,2,96,384]{3,2,1,0:T(8,128)(2,1)S(1)} collective-permute-done((bf16[2,2,96,384]{3,2,1,0:T(8,128)(2,1)S(1)}, bf16[2,2,96,384]{3,2,1,0:T(8,128)(2,1)S(1)}, u32[]{:S(2)}, u32[]{:S(2)}) %collective-permute-start.9) | collective-permute-done | bytes 294944 | tf_op jit(solution)/shard_map/ppermute | solution.py:633
  98.3 11.5 %collective-permute-done.6.block_3 = bf16[256,1664]{1,0:T(8,128)(2,1)S(1)} collective-permute-done((bf16[256,1664]{1,0:T(8,128)(2,1)S(1)}, bf16[256,1664]{1,0:T(8,128)(2,1)S(1)}, u32[]{:S(2)}, u32[]{:S(2)}) %collective-permute-start.6) | collective-permute-done | bytes 852000 | tf_op jit(solution)/shard_map/ppermute | solution.py:633
  113.1 13.8 %attend.1 = (bf16[1024,1664]{1,0:T(8,128)(2,1)}, bf16[1024,1536]{1,0:T(8,128)(2,1)}, bf16[1024,384]{1,0:T(8,128)(2,1)S(1)}, f32[1024,192]{1,0:T(8,128)}, bf16[10...) custom-call(s32[1]{0:T(128)} %bitcast.place_ref, bf16[256,1664]{1,0:T(8,128)(2,1)S(1)} %bitcast.116, ...), custom_call_target="tpu_custom_call" | custom-call | flops 12999999488 | bytes 12000000 | tf_op jit(solution)/shard_map/attend/pallas_call | solution.py:507
  136.4 4.5 all-to-all-start.1
  140.9 2.5 broadcast_in_dim.121
  143.5 3.2 bitcast_dynamic-update-slice_fusion
  146.7 3.2 bitcast_dynamic-update-slice_fusion.1
  149.9 36.2 %all-to-all-done.1 = bf16[8,1024,192]{1,2,0:T(8,128)(2,1)} async-done(((bf16[8,1024,192]{1,2,0:T(8,128)(2,1)}), bf16[8,1024,192]{1,2,0:T(8,128)(2,1)}, u32[]{:S(2)}, u32[]{:S(2)}) %all-to-all-start.1) | async-done | bytes 3145760 | tf_op jit(solution)/shard_map/all_to_all | solution.py:69
  186.1 9.3 %multiply_reduce_fusion = (f32[1024]{0:T(1024)S(1)}, f32[1024,1536]{1,0:T(8,128)S(1)}) fusion(bf16[8,1024,192]{1,2,0:T(8,128)(2,1)} %all-to-all-done.1, bf16[8,192,1536]{2,1,0:T(8,128)(2,1)} %bitcast.32, bf16[1024,1664]{1,0:T(8,128)(2,1)} %get-tuple-element.63), kind=kOutput, calls=%fused_computation.7 | convolution fusion | flops 4838128640 | bytes 17305600 | tf_op jit(solution)/shard_map/etk,ekn->tn/dot_general | solution.py:60
  195.5 2.6 copy-done.13
  202.4 10.0 %collective-permute-done.15 = bf16[128,1536]{1,0:T(8,128)(2,1)S(1)} collective-permute-done((bf16[128,1536]{1,0:T(8,128)(2,1)S(1)}, bf16[128,1536]{1,0:T(8,128)(2,1)S(1)}, u32[]{:S(2)}, u32[]{:S(2)}) %collective-permute-start.15) | collective-permute-done | bytes 393248 | tf_op jit(solution)/shard_map/ppermute | solution.py:757
  213.4 14.5 %all-gather.5.cloned.1.call-done = bf16[40,288,512]{2,1,0:T(8,128)(2,1)} async-done(((bf16[5,288,512]{2,1,0:T(8,128)(2,1)}), bf16[40,288,512]{2,1,0:T(8,128)(2,1)}) %all-gather.5.cloned.1.call-update) | async-done | bytes 11796496 | tf_op jit(solution)/shard_map/all_gather | solution.py:712
  229.9 40.3 %experts_forward.1 = (bf16[1024,1536]{1,0:T(8,128)(2,1)}, bf16[1024,1536]{1,0:T(8,128)(2,1)}, bf16[5,768,1536]{2,1,0:T(8,128)(2,1)}, bf16[5,768,640]{2,1,0:T(8,128)(2,1)}) custom-call(bf16[1024,1536]{1,0:T(8,128)(2,1)} %multiply_convert_fusion.n_own, bf16[1024,1536]{1,0:T(8,128)(2,1)} %collective-permute-done.13.n_par, bf16[2048,128]{1,0:T(8,128)(2,1)} %fusion.13.routes, ...), custom_call_target="tpu_custom_call" | custom-call | flops 40000000000 | bytes 40000000 | tf_op jit(solution)/shard_map/experts_forward/pallas_call | solution.py:372
  272.0 5.3 collective-permute-done.14
  277.3 4.0 add_convert_fusion.3
  281.3 4.1 collective-permute-start.17
  285.5 2.7 collective-permute-start.19
  288.2 46.6 %experts_backward.1 = (bf16[1024,1664]{1,0:T(8,128)(2,1)}, bf16[1024,1664]{1,0:T(8,128)(2,1)}, bf16[8,5,288,512]{3,2,1,0:T(8,128)(2,1)}) custom-call(s32[1]{0:T(128)} %bitcast.35.place_ref, bf16[1024,1536]{1,0:T(8,128)(2,1)} %bitcast.160, bf16[1024,1536]{1,0:T(8,128)(2,1)} %collective-permute-done.16.g_par, bf16[2048,128]{1,0:T(8,128)(2,1)} %fusion.13.routes, ...), custom_call_target="tpu_custom_call" | custom-call | flops 49999998976 | bytes 60000000 | tf_op jit(solution)/shard_map/experts_backward/pallas_call | solution.py:400
  336.9 5.9 %collective-permute-done.20 = bf16[1024,1664]{1,0:T(8,128)(2,1)S(1)} collective-permute-done((bf16[1024,1664]{1,0:T(8,128)(2,1)}, bf16[1024,1664]{1,0:T(8,128)(2,1)S(1)}, u32[]{:S(2)}, u32[]{:S(2)}) %collective-permute-start.20) | collective-permute-done | bytes 3407904 | tf_op jit(solution)/shard_map/ppermute | solution.py:64
  342.8 4.7 add_convert_fusion.2
  350.3 19.2 %collective-permute-done.21 = bf16[256,1664]{1,0:T(8,128)(2,1)} collective-permute-done((bf16[256,1664]{1,0:T(8,128)(2,1)}, bf16[256,1664]{1,0:T(8,128)(2,1)}, u32[]{:S(2)}, u32[]{:S(2)}) %collective-permute-start.21) | collective-permute-done | bytes 852000 | tf_op jit(solution)/shard_map/ppermute | solution.py:666
  369.5 18.4 %collective-permute-done.22 = bf16[256,1664]{1,0:T(8,128)(2,1)} collective-permute-done((bf16[256,1664]{1,0:T(8,128)(2,1)}, bf16[256,1664]{1,0:T(8,128)(2,1)}, u32[]{:S(2)}, u32[]{:S(2)}) %collective-permute-start.22) | collective-permute-done | bytes 852000 | tf_op jit(solution)/shard_map/ppermute | solution.py:666
  387.9 2.7 add_add_fusion
  392.7 17.6 %collective-permute-done.24 = bf16[128,1664]{1,0:T(8,128)(2,1)S(1)} collective-permute-done((bf16[128,1664]{1,0:T(8,128)(2,1)S(1)}, bf16[128,1664]{1,0:T(8,128)(2,1)S(1)}, u32[]{:S(2)}, u32[]{:S(2)}) %collective-permute-start.24) | collective-permute-done | bytes 426016 | tf_op jit(solution)/shard_map/ppermute | solution.py:674
  414.9 3.7 fusion.11
  419.6 4.0 all-to-all-start.2
  423.6 2.6 fusion
  429.2 6.9 %all-to-all-done.2 = bf16[8,128,384]{1,2,0:T(8,128)(2,1)S(1)} async-done(((bf16[8,128,384]{1,2,0:T(8,128)(2,1)}), bf16[8,128,384]{1,2,0:T(8,128)(2,1)S(1)}, u32[]{:S(2)}, u32[]{:S(2)}) %all-to-all-start.2) | async-done | bytes 786464 | tf_op jit(solution)/shard_map/all_to_all | solution.py:73
  439.9 11.0 %attend_back.1 = bf16[1024,384]{1,0:T(8,128)(2,1)S(1)} custom-call(bf16[1024,384]{1,0:T(8,128)(2,1)S(1)} %bitcast.117, bf16[1024,384]{1,0:T(8,128)(2,1)S(1)} %copy-done.10, f32[1024,192]{1,0:T(8,128)S(1)} %copy-done.8, f32[1024,8]{1,0:T(8,128)S(1)} %copy-done.12, bf16[1024,384]{1,0:T(8,128)(2,1)S(1)} %copy-done.10, f32[1024,256]{1,0:T(8,128)S(1)} %copy-done.2, ...), custom_call_target="tpu_custom_call" | custom-call | flops 11000000512 | bytes 8000000 | tf_op jit(solution)/shard_map/attend_back/pallas_call | solution.py:601
  453.9 3.9 convolution_convert_fusion.1
  457.9 5.2 concatenate.54
  463.1 5.4 fusion.55
  470.6 2.7 collective-permute-start.26
  476.8 2.4 collective-permute-start.29
  479.3 2.6 add_add_fusion.2
  483.9 3.6 all-to-all-start.3
  487.5 4.7 reduce-scatter.2.cloned.1.call-done
  499.9 13.1 %collective-permute-done.28 = bf16[256,1536]{1,0:T(8,128)(2,1)} collective-permute-done((bf16[256,1536]{1,0:T(8,128)(2,1)}, bf16[256,1536]{1,0:T(8,128)(2,1)}, u32[]{:S(2)}, u32[]{:S(2)}) %collective-permute-start.28) | collective-permute-done | bytes 786464 | tf_op jit(solution)/shard_map/ppermute | solution.py:666
  520.0 5.2 all-to-all-start.4
  528.7 11.3 %all-to-all-done.4 = bf16[8,96,640]{2,1,0:T(8,128)(2,1)S(1)} async-done(((bf16[8,96,640]{2,1,0:T(8,128)(2,1)}), bf16[8,96,640]{2,1,0:T(8,128)(2,1)S(1)}, u32[]{:S(2)}, u32[]{:S(2)}) %all-to-all-start.4) | async-done | bytes 983072 | tf_op jit(solution)/shard_map/all_to_all | solution.py:69
  (229 shorter events, 96.7 us)
Async XLA Ops:
  7.2 6.0 %copy-start = (bf16[5,96,1024]{2,1,0:T(8,128)(2,1)S(1)}, bf16[5,96,1024]{2,1,0:T(8,128)(2,1)}, u32[]{:S(2)}) copy-start(bf16[5,96,1024]{2,1,0:T(8,128)(2,1)} %param.19) | copy-start | bytes 2949124
  7.2 220.7 %all-gather.5.cloned.1.call-start = ((), (), s32[]{:S(2)}) async-start(), calls=%async_computation.7 | async-start | bytes 13271040 | tf_op jit(solution)/shard_map/all_gather | solution.py:712
  11.6 3.9 collective-permute-start.2
  14.5 1.9 collective-permute-start.1
  18.0 11.2 %collective-permute-start.10 = (bf16[96,1536]{1,0:T(8,128)(2,1)S(1)}, bf16[96,1536]{1,0:T(8,128)(2,1)S(1)}, u32[]{:S(2)}, u32[]{:S(2)}) collective-permute-start(bf16[96,1536]{1,0:T(8,128)(2,1)S(1)} %copy-done.28), channel_id=1, source_target_pairs={{0,18},{2,16},{16,2},{18,0},{1,19},{3,17},{17,3},{19,1},{4,22},{6,... | collective-permute-start | bytes 884744 | tf_op jit(solution)/shard_map/ppermute | solution.py:730
  22.2 26.9 %collective-permute-start = (bf16[128,1664]{1,0:T(8,128)(2,1)S(1)}, bf16[128,1664]{1,0:T(8,128)(2,1)S(1)}, u32[]{:S(2)}, u32[]{:S(2)}) collective-permute-start(bf16[128,1664]{1,0:T(8,128)(2,1)S(1)} %concatenate.46), channel_id=1, source_target_pairs={{0,16},{16,0},{1,17},{17,1},{2,18},{18,2},{3,19},{19,3},{4,20},{20... | collective-permute-start | bytes 1277960 | tf_op jit(solution)/shard_map/ppermute | solution.py:718
  30.9 79.9 %all-to-all-start = ((bf16[4,2,96,1536]{3,2,1,0:T(8,128)(2,1)}), bf16[4,2,96,1536]{3,2,1,0:T(8,128)(2,1)}, u32[]{:S(2)}, u32[]{:S(2)}) async-start(bf16[4,2,96,1536]{3,2,1,0:T(8,128)(2,1)} %broadcast_in_dim.117), calls=%async_computation | async-start | bytes 4718592 | tf_op jit(solution)/shard_map/all_to_all | solution.py:646
  35.9 10.3 %collective-permute-start.3 = (bf16[2,96,384]{2,1,0:T(8,128)(2,1)S(1)}, bf16[2,96,384]{2,1,0:T(8,128)(2,1)S(1)}, u32[]{:S(2)}, u32[]{:S(2)}) collective-permute-start(bf16[2,96,384]{2,1,0:T(8,128)(2,1)S(1)} %maximum_select_fusion.6), channel_id=1, source_target_pairs={{0,2},{2,0},{1,3},{3,1},{4,6},{6,4},{5,7},{7,5},{8,10},{10,8},{9,1... | collective-permute-start | bytes 442376 | tf_op jit(solution)/shard_map/ppermute | solution.py:713
  46.3 42.7 %collective-permute-start.7 = (bf16[2,2,96,384]{3,2,1,0:T(8,128)(2,1)S(1)}, bf16[2,2,96,384]{3,2,1,0:T(8,128)(2,1)S(1)}, u32[]{:S(2)}, u32[]{:S(2)}) collective-permute-start(bf16[2,2,96,384]{3,2,1,0:T(8,128)(2,1)S(1)} %maximum_select_fusion.4), channel_id=1, source_target_pairs={{0,12},{4,0},{8,4},{12,8},{1,13},{5,1},{9,5},{13,9},{2,14},{6,2},{... | collective-permute-start | bytes 884744 | tf_op jit(solution)/shard_map/ppermute | solution.py:633
  49.2 41.2 %collective-permute-start.8 = (bf16[2,2,96,384]{3,2,1,0:T(8,128)(2,1)S(1)}, bf16[2,2,96,384]{3,2,1,0:T(8,128)(2,1)S(1)}, u32[]{:S(2)}, u32[]{:S(2)}) collective-permute-start(bf16[2,2,96,384]{3,2,1,0:T(8,128)(2,1)S(1)} %maximum_select_fusion.4), channel_id=1, source_target_pairs={{0,8},{4,12},{8,0},{12,4},{1,9},{5,13},{9,1},{13,5},{2,10},{6,14},... | collective-permute-start | bytes 884744 | tf_op jit(solution)/shard_map/ppermute | solution.py:633
  49.7 46.6 %collective-permute-start.9 = (bf16[2,2,96,384]{3,2,1,0:T(8,128)(2,1)S(1)}, bf16[2,2,96,384]{3,2,1,0:T(8,128)(2,1)S(1)}, u32[]{:S(2)}, u32[]{:S(2)}) collective-permute-start(bf16[2,2,96,384]{3,2,1,0:T(8,128)(2,1)S(1)} %maximum_select_fusion.4), channel_id=1, source_target_pairs={{0,4},{4,8},{8,12},{12,0},{1,5},{5,9},{9,13},{13,1},{2,6},{6,10},{... | collective-permute-start | bytes 884744 | tf_op jit(solution)/shard_map/ppermute | solution.py:633
  50.3 46.6 %collective-permute-start.4 = (bf16[256,1664]{1,0:T(8,128)(2,1)S(1)}, bf16[256,1664]{1,0:T(8,128)(2,1)S(1)}, u32[]{:S(2)}, u32[]{:S(2)}) collective-permute-start(bf16[256,1664]{1,0:T(8,128)(2,1)S(1)} %bitcast.113), channel_id=1, source_target_pairs={{0,96},{32,0},{64,32},{96,64},{1,97},{33,1},{65,33},{97,65},{2,98}... | collective-permute-start | bytes 2555912 | tf_op jit(solution)/shard_map/ppermute | solution.py:633
  52.8 44.2 %collective-permute-start.5 = (bf16[256,1664]{1,0:T(8,128)(2,1)S(1)}, bf16[256,1664]{1,0:T(8,128)(2,1)S(1)}, u32[]{:S(2)}, u32[]{:S(2)}) collective-permute-start(bf16[256,1664]{1,0:T(8,128)(2,1)S(1)} %bitcast.114), channel_id=1, source_target_pairs={{0,64},{32,96},{64,0},{96,32},{1,65},{33,97},{65,1},{97,33},{2,66}... | collective-permute-start | bytes 2555912 | tf_op jit(solution)/shard_map/ppermute | solution.py:633
  89.0 20.9 %collective-permute-start.6 = (bf16[256,1664]{1,0:T(8,128)(2,1)S(1)}, bf16[256,1664]{1,0:T(8,128)(2,1)S(1)}, u32[]{:S(2)}, u32[]{:S(2)}) collective-permute-start(bf16[256,1664]{1,0:T(8,128)(2,1)S(1)} %bitcast.115), channel_id=1, source_target_pairs={{0,32},{32,64},{64,96},{96,0},{1,33},{33,65},{65,97},{97,1},{2,34}... | collective-permute-start | bytes 2555912 | tf_op jit(solution)/shard_map/ppermute | solution.py:633
  96.9 30.0 %copy-start.29 = (f32[1536]{0:T(1024)}, f32[1536]{0:T(1024)S(1)}, u32[]{:S(2)}) copy-start(f32[1536]{0:T(1024)S(1)} %get-tuple-element.133) | copy-start | bytes 18436
  129.6 3.1 collective-permute-start.11
  131.5 15.2 %collective-permute-start.12 = (bf16[4,2,96,1536]{3,2,1,0:T(8,128)(2,1)}, bf16[4,2,96,1536]{3,2,1,0:T(8,128)(2,1)}, u32[]{:S(2)}, u32[]{:S(2)}) collective-permute-start(bf16[4,2,96,1536]{3,2,1,0:T(8,128)(2,1)} %all-to-all-done), channel_id=1, source_target_pairs={{0,1},{1,0},{2,3},{3,2},{4,5},{5,4},{6,7},{7,6},{8,9},{9,8},{10,11... | collective-permute-start | bytes 7077896 | tf_op jit(solution)/shard_map/ppermute | solution.py:64
  136.4 49.7 %all-to-all-start.1 = ((bf16[8,1024,192]{1,2,0:T(8,128)(2,1)}), bf16[8,1024,192]{1,2,0:T(8,128)(2,1)}, u32[]{:S(2)}, u32[]{:S(2)}) async-start(bf16[8,1024,192]{1,2,0:T(8,128)(2,1)} %broadcast_in_dim.120), calls=%async_computation.1 | async-start | bytes 6291456 | tf_op jit(solution)/shard_map/all_to_all | solution.py:69
  140.9 130.8 %all-gather.7.cloned.1.call-start = ((), (), s32[]{:S(2)}) async-start(), calls=%async_computation.8 | async-start | bytes 3932160 | tf_op jit(solution)/shard_map/all_gather | solution.py:759
  200.4 28.1 %copy-start.15 = (bf16[4,2,2,96,384]{4,3,2,1,0:T(8,128)(2,1)S(1)}, bf16[4,2,2,96,384]{4,3,2,1,0:T(8,128)(2,1)}, u32[]{:S(2)}) copy-start(bf16[4,2,2,96,384]{4,3,2,1,0:T(8,128)(2,1)} %copy-done.14) | copy-start | bytes 3538948
  200.4 29.5 %collective-permute-start.13 = (bf16[1024,1536]{1,0:T(8,128)(2,1)}, bf16[1024,1536]{1,0:T(8,128)(2,1)}, u32[]{:S(2)}, u32[]{:S(2)}) collective-permute-start(bf16[1024,1536]{1,0:T(8,128)(2,1)} %multiply_convert_fusion.n_own), channel_id=1, source_target_pairs={{0,1},{1,0},{2,3},{3,2},{4,5},{5,4},{6,7},{7,6},{8,9},{9,8},{10,11... | collective-permute-start | bytes 9437192 | tf_op jit(solution)/shard_map/ppermute | solution.py:64
  201.6 10.8 %collective-permute-start.15 = (bf16[128,1536]{1,0:T(8,128)(2,1)S(1)}, bf16[128,1536]{1,0:T(8,128)(2,1)S(1)}, u32[]{:S(2)}, u32[]{:S(2)}) collective-permute-start(bf16[128,1536]{1,0:T(8,128)(2,1)S(1)} %bitcast.133), channel_id=1, source_target_pairs={{0,16},{16,0},{1,17},{17,1},{2,18},{18,2},{3,19},{19,3},{4,20},{20... | collective-permute-start | bytes 1179656 | tf_op jit(solution)/shard_map/ppermute | solution.py:757
  228.0 264.2 %reduce-scatter.2.cloned.1.call-start = ((), (), s32[]{:S(2)}) async-start(), calls=%async_computation.6 | async-start | bytes 13271040 | tf_op jit(solution)/shard_map/reduce_scatter | solution.py:778
  270.2 7.1 %collective-permute-start.14 = (bf16[1024,1536]{1,0:T(8,128)(2,1)}, bf16[1024,1536]{1,0:T(8,128)(2,1)}, u32[]{:S(2)}, u32[]{:S(2)}) collective-permute-start(bf16[1024,1536]{1,0:T(8,128)(2,1)} %get-tuple-element.69), channel_id=1, source_target_pairs={{0,1},{1,0},{2,3},{3,2},{4,5},{5,4},{6,7},{7,6},{8,9},{9,8},{10,11... | collective-permute-start | bytes 9437192 | tf_op jit(solution)/shard_map/ppermute | solution.py:64
  271.7 16.5 %collective-permute-start.16 = (bf16[1024,1536]{1,0:T(8,128)(2,1)}, bf16[1024,1536]{1,0:T(8,128)(2,1)}, u32[]{:S(2)}, u32[]{:S(2)}) collective-permute-start(bf16[1024,1536]{1,0:T(8,128)(2,1)} %bitcast.159), channel_id=1, source_target_pairs={{0,1},{1,0},{2,3},{3,2},{4,5},{5,4},{6,7},{7,6},{8,9},{9,8},{10,11... | collective-permute-start | bytes 9437192 | tf_op jit(solution)/shard_map/ppermute | solution.py:64
  281.3 53.5 %collective-permute-start.17 = (bf16[256,1536]{1,0:T(8,128)(2,1)}, bf16[256,1536]{1,0:T(8,128)(2,1)S(1)}, u32[]{:S(2)}, u32[]{:S(2)}) collective-permute-start(bf16[256,1536]{1,0:T(8,128)(2,1)} %get-tuple-element.76), channel_id=1, source_target_pairs={{0,64},{32,96},{64,0},{96,32},{1,65},{33,97},{65,1},{97,33},{2,66}... | collective-permute-start | bytes 2359304 | tf_op jit(solution)/shard_map/ppermute | solution.py:666
  285.5 49.3 %collective-permute-start.18 = (bf16[256,1536]{1,0:T(8,128)(2,1)}, bf16[256,1536]{1,0:T(8,128)(2,1)}, u32[]{:S(2)}, u32[]{:S(2)}) collective-permute-start(bf16[256,1536]{1,0:T(8,128)(2,1)} %get-tuple-element.77), channel_id=1, source_target_pairs={{0,32},{32,64},{64,96},{96,0},{1,33},{33,65},{65,97},{97,1},{2,34}... | collective-permute-start | bytes 2359304 | tf_op jit(solution)/shard_map/ppermute | solution.py:666
  285.5 49.3 %collective-permute-start.19 = (bf16[256,1536]{1,0:T(8,128)(2,1)}, bf16[256,1536]{1,0:T(8,128)(2,1)}, u32[]{:S(2)}, u32[]{:S(2)}) collective-permute-start(bf16[256,1536]{1,0:T(8,128)(2,1)} %get-tuple-element.78), channel_id=1, source_target_pairs={{0,96},{32,0},{64,32},{96,64},{1,97},{33,1},{65,33},{97,65},{2,98}... | collective-permute-start | bytes 2359304 | tf_op jit(solution)/shard_map/ppermute | solution.py:666
  335.7 7.1 %collective-permute-start.20 = (bf16[1024,1664]{1,0:T(8,128)(2,1)}, bf16[1024,1664]{1,0:T(8,128)(2,1)S(1)}, u32[]{:S(2)}, u32[]{:S(2)}) collective-permute-start(bf16[1024,1664]{1,0:T(8,128)(2,1)} %get-tuple-element.83), channel_id=1, source_target_pairs={{0,1},{1,0},{2,3},{3,2},{4,5},{5,4},{6,7},{7,6},{8,9},{9,8},{10,11... | collective-permute-start | bytes 10223624 | tf_op jit(solution)/shard_map/ppermute | solution.py:64
  347.5 22.0 %collective-permute-start.21 = (bf16[256,1664]{1,0:T(8,128)(2,1)}, bf16[256,1664]{1,0:T(8,128)(2,1)}, u32[]{:S(2)}, u32[]{:S(2)}) collective-permute-start(bf16[256,1664]{1,0:T(8,128)(2,1)} %get-tuple-element.142), channel_id=1, source_target_pairs={{0,64},{32,96},{64,0},{96,32},{1,65},{33,97},{65,1},{97,33},{2,66}... | collective-permute-start | bytes 2555912 | tf_op jit(solution)/shard_map/ppermute | solution.py:666
  347.5 40.4 %collective-permute-start.22 = (bf16[256,1664]{1,0:T(8,128)(2,1)}, bf16[256,1664]{1,0:T(8,128)(2,1)}, u32[]{:S(2)}, u32[]{:S(2)}) collective-permute-start(bf16[256,1664]{1,0:T(8,128)(2,1)} %get-tuple-element.144), channel_id=1, source_target_pairs={{0,32},{32,64},{64,96},{96,0},{1,33},{33,65},{65,97},{97,1},{2,34}... | collective-permute-start | bytes 2555912 | tf_op jit(solution)/shard_map/ppermute | solution.py:666
  347.8 40.0 %collective-permute-start.23 = (bf16[256,1664]{1,0:T(8,128)(2,1)}, bf16[256,1664]{1,0:T(8,128)(2,1)}, u32[]{:S(2)}, u32[]{:S(2)}) collective-permute-start(bf16[256,1664]{1,0:T(8,128)(2,1)} %get-tuple-element.143), channel_id=1, source_target_pairs={{0,96},{32,0},{64,32},{96,64},{1,97},{33,1},{65,33},{97,65},{2,98}... | collective-permute-start | bytes 2555912 | tf_op jit(solution)/shard_map/ppermute | solution.py:666
  390.7 19.5 %collective-permute-start.24 = (bf16[128,1664]{1,0:T(8,128)(2,1)S(1)}, bf16[128,1664]{1,0:T(8,128)(2,1)S(1)}, u32[]{:S(2)}, u32[]{:S(2)}) collective-permute-start(bf16[128,1664]{1,0:T(8,128)(2,1)S(1)} %dynamic-slice_convert_fusion), channel_id=1, source_target_pairs={{0,16},{16,0},{1,17},{17,1},{2,18},{18,2},{3,19},{19,3},{4,20},{20... | collective-permute-start | bytes 1277960 | tf_op jit(solution)/shard_map/ppermute | solution.py:674
  419.6 16.5 %all-to-all-start.2 = ((bf16[8,128,384]{1,2,0:T(8,128)(2,1)}), bf16[8,128,384]{1,2,0:T(8,128)(2,1)S(1)}, u32[]{:S(2)}, u32[]{:S(2)}) async-start(bf16[8,128,384]{1,2,0:T(8,128)(2,1)} %pad_maximum_fusion.2), calls=%async_computation.2 | async-start | bytes 1572864 | tf_op jit(solution)/shard_map/all_to_all | solution.py:73
  426.1 10.4 %copy-start.2 = (f32[1024,256]{1,0:T(8,128)S(1)}, f32[1024,256]{1,0:T(8,128)}, u32[]{:S(2)}) copy-start(f32[1024,256]{1,0:T(8,128)} %get-tuple-element.168.cosine.all_cosine) | copy-start | bytes 3145732
  439.9 11.0 %copy-start.36 = (bf16[1024,1536]{1,0:T(8,128)(2,1)S(1)}, bf16[1024,1536]{1,0:T(8,128)(2,1)}, u32[]{:S(2)}) copy-start(bf16[1024,1536]{1,0:T(8,128)(2,1)} %get-tuple-element.90) | copy-start | bytes 9437188
  470.6 12.0 %collective-permute-start.26 = (bf16[8,96,640]{2,1,0:T(8,128)(2,1)S(1)}, bf16[8,96,640]{2,1,0:T(8,128)(2,1)S(1)}, u32[]{:S(2)}, u32[]{:S(2)}) collective-permute-start(bf16[8,96,640]{2,1,0:T(8,128)(2,1)S(1)} %select_bitcast_fusion), channel_id=1, source_target_pairs={{0,1},{1,0},{2,3},{3,2},{4,5},{5,4},{6,7},{7,6},{8,9},{9,8},{10,11... | collective-permute-start | bytes 2949128 | tf_op jit(solution)/shard_map/ppermute | solution.py:64
  473.4 5.9 %copy-start.25 = (bf16[256,1536]{1,0:T(8,128)(2,1)S(1)}, bf16[256,1536]{1,0:T(8,128)(2,1)}, u32[]{:S(2)}) copy-start(bf16[256,1536]{1,0:T(8,128)(2,1)} %copy-done.24) | copy-start | bytes 2359300
  474.8 25.0 %collective-permute-start.27 = (bf16[256,1536]{1,0:T(8,128)(2,1)}, bf16[256,1536]{1,0:T(8,128)(2,1)}, u32[]{:S(2)}, u32[]{:S(2)}) collective-permute-start(bf16[256,1536]{1,0:T(8,128)(2,1)} %get-tuple-element.152), channel_id=1, source_target_pairs={{0,64},{32,96},{64,0},{96,32},{1,65},{33,97},{65,1},{97,33},{2,66}... | collective-permute-start | bytes 2359304 | tf_op jit(solution)/shard_map/ppermute | solution.py:666
  476.6 36.4 %collective-permute-start.28 = (bf16[256,1536]{1,0:T(8,128)(2,1)}, bf16[256,1536]{1,0:T(8,128)(2,1)}, u32[]{:S(2)}, u32[]{:S(2)}) collective-permute-start(bf16[256,1536]{1,0:T(8,128)(2,1)} %get-tuple-element.151), channel_id=1, source_target_pairs={{0,32},{32,64},{64,96},{96,0},{1,33},{33,65},{65,97},{97,1},{2,34}... | collective-permute-start | bytes 2359304 | tf_op jit(solution)/shard_map/ppermute | solution.py:666
  476.8 36.2 %collective-permute-start.29 = (bf16[256,1536]{1,0:T(8,128)(2,1)}, bf16[256,1536]{1,0:T(8,128)(2,1)}, u32[]{:S(2)}, u32[]{:S(2)}) collective-permute-start(bf16[256,1536]{1,0:T(8,128)(2,1)} %get-tuple-element.150), channel_id=1, source_target_pairs={{0,96},{32,0},{64,32},{96,64},{1,97},{33,1},{65,33},{97,65},{2,98}... | collective-permute-start | bytes 2359304 | tf_op jit(solution)/shard_map/ppermute | solution.py:666
  482.6 34.2 %collective-permute-start.25 = (bf16[128,1536]{1,0:T(8,128)(2,1)}, bf16[128,1536]{1,0:T(8,128)(2,1)}, u32[]{:S(2)}, u32[]{:S(2)}) collective-permute-start(bf16[128,1536]{1,0:T(8,128)(2,1)} %dynamic-slice_convert_fusion.2), channel_id=1, source_target_pairs={{0,16},{16,0},{1,17},{17,1},{2,18},{18,2},{3,19},{19,3},{4,20},{20... | collective-permute-start | bytes 1179656 | tf_op jit(solution)/shard_map/ppermute | solution.py:674
  483.9 29.0 %all-to-all-start.3 = ((bf16[8,96,640]{2,1,0:T(8,128)(2,1)}), bf16[8,96,640]{2,1,0:T(8,128)(2,1)S(1)}, u32[]{:S(2)}, u32[]{:S(2)}) async-start(bf16[8,96,640]{2,1,0:T(8,128)(2,1)} %fusion.7), calls=%async_computation.3 | async-start | bytes 1966080 | tf_op jit(solution)/shard_map/all_to_all | solution.py:73
  494.6 3.3 collective-permute-start.30
  516.8 10.4 %collective-permute-start.31 = (bf16[128,1536]{1,0:T(8,128)(2,1)}, bf16[128,1536]{1,0:T(8,128)(2,1)S(1)}, u32[]{:S(2)}, u32[]{:S(2)}) collective-permute-start(bf16[128,1536]{1,0:T(8,128)(2,1)} %dynamic-slice_convert_fusion.1), channel_id=1, source_target_pairs={{0,16},{16,0},{1,17},{17,1},{2,18},{18,2},{3,19},{19,3},{4,20},{20... | collective-permute-start | bytes 1179656 | tf_op jit(solution)/shard_map/ppermute | solution.py:674
  518.9 8.3 %copy-start.18 = (bf16[1,128,1536]{2,1,0:T(8,128)(2,1)S(1)}, bf16[1,128,1536]{2,1,0:T(8,128)(2,1)}, u32[]{:S(2)}) copy-start(bf16[1,128,1536]{2,1,0:T(8,128)(2,1)} %param.11) | copy-start | bytes 1179652
  518.9 8.3 %copy-start.30 = (f32[1536]{0:T(1024)S(1)}, f32[1536]{0:T(1024)}, u32[]{:S(2)}) copy-start(f32[1536]{0:T(1024)} %copy-done.29) | copy-start | bytes 18436
  520.0 20.0 %all-to-all-start.4 = ((bf16[8,96,640]{2,1,0:T(8,128)(2,1)}), bf16[8,96,640]{2,1,0:T(8,128)(2,1)S(1)}, u32[]{:S(2)}, u32[]{:S(2)}) async-start(bf16[8,96,640]{2,1,0:T(8,128)(2,1)} %broadcast_in_dim.131), calls=%async_computation.5 | async-start | bytes 1966080 | tf_op jit(solution)/shard_map/all_to_all | solution.py:69
  (29 other events, 72.2 us)
Sparse Core Ops, SparseCore 0:
  18.1 209.7 all-gather.4
  230.2 38.9 all-gather.6
  335.0 157.1 reduce-scatter.1

commit v4 on v3

--- a/solution.py
+++ b/solution.py
@@ -625,6 +625,96 @@
     )(upstream, heads, attended, stats, heads, cosine, sine, cosine, sine, seg_rows, seg_cols)
 
 
+def arrange_kernel(totals, total_out, total_qkv, shared):
+    blocks = [totals[e].astype(F32) for e in range(N_EXP)]
+
+    def side_by_side(start, width):
+        return jnp.concatenate([block[:, start : start + width] for block in blocks], axis=1)
+
+    total_out[...] = side_by_side(0, HEAD_COLS)
+    total_qkv[:, :WIDTH] = side_by_side(HEAD_COLS, HEAD_COLS)
+    total_qkv[:, WIDTH : WIDTH + KEY_VALUE_HEADS * HEAD_SIZE] = side_by_side(2 * HEAD_COLS, HEAD_SIZE)
+    total_qkv[:, WIDTH + KEY_VALUE_HEADS * HEAD_SIZE :] = side_by_side(2 * HEAD_COLS + HEAD_SIZE, HEAD_SIZE)
+    shared[...] = sum(block[:, HEAD_COLS + QKV_COLS :] for block in blocks)
+
+
+def arrange_call(totals):
+    rows = totals.shape[1]
+    widths = (WIDTH, WIDTH + 2 * KEY_VALUE_HEADS * HEAD_SIZE, SIDE)
+    return pl.pallas_call(
+        arrange_kernel,
+        out_shape=[jax.ShapeDtypeStruct((rows, width), F32) for width in widths],
+        compiler_params=pltpu.CompilerParams(vmem_limit_bytes=32 * 1024 * 1024),
+        cost_estimate=pl.CostEstimate(flops=1_000_000, bytes_accessed=3_000_000, transcendentals=0),
+        name="arrange",
+    )(totals)
+
+
+def small_call(kernel, out_shape, name, *operands):
+    return pl.pallas_call(
+        kernel,
+        in_specs=[
+            pl.BlockSpec(memory_space=pltpu.SMEM if operand.ndim == 1 else pltpu.VMEM) for operand in operands
+        ],
+        out_shape=out_shape,
+        compiler_params=pltpu.CompilerParams(vmem_limit_bytes=48 * 1024 * 1024),
+        cost_estimate=pl.CostEstimate(flops=0, bytes_accessed=0, transcendentals=0),
+        name=name,
+    )(*operands)
+
+
+def line_up_kernel(start, piece_0, piece_1, piece_2, piece_3, lined):
+    for k, piece in enumerate((piece_0, piece_1, piece_2, piece_3)):
+        lined[pl.ds(lax.rem(start[0] + k, 4), 1)] = piece[...][None]
+
+
+def line_up(pieces, start):
+    shape = jax.ShapeDtypeStruct((4, *pieces[0].shape), pieces[0].dtype)
+    return small_call(line_up_kernel, shape, "line_up", start.reshape(1), *pieces)
+
+
+def both_cores_kernel(core, mine, other, both):
+    both[:, :, pl.ds(core[0], 1)] = mine[...][:, :, None]
+    both[:, :, pl.ds(1 - core[0], 1)] = other[...][:, :, None]
+
+
+def both_cores(mine, other, core):
+    shape = jax.ShapeDtypeStruct((4, 2, 2, *mine.shape[2:]), mine.dtype)
+    return small_call(both_cores_kernel, shape, "both_cores", core.reshape(1), mine, other)
+
+
+def dense_kernel(core, attended_all, back, normed, grad_projected, packed, side, keep, send, parts):
+    branch = back[:, HEAD_COLS:]
+    for e in range(N_EXP):
+        parts[e * HEAD_COLS : (e + 1) * HEAD_COLS, :HEAD_COLS] = contract(attended_all[e], branch, ((0,), (0,)))
+    for half in range(2):
+        rows = slice(half * WIDTH // 2, (half + 1) * WIDTH // 2)
+        grads = contract(normed[:, rows], grad_projected[...], ((0,), (0,)))
+        weight = packed[rows, :].astype(F32)
+        gain = weight[:, QKV_COLS + EXPERTS : QKV_COLS + EXPERTS + 1]
+        slope = jnp.sum(grads * weight, axis=-1, keepdims=True) / gain
+        lane = lax.broadcasted_iota(jnp.int32, (WIDTH // 2, SIDE), 1)
+        last = jnp.where(lane == SIDE - 1, slope, side[rows, :])
+        parts[rows, HEAD_COLS:] = jnp.concatenate([grads[:, :QKV_COLS], last], axis=1)
+    for k in range(N_YZ):
+        for ref, index in ((keep, core[0]), (send, 1 - core[0])):
+            start = pl.multiple_of((2 * k + index) * (WIDTH // N_FSDP), 8)
+            ref[k] = parts[pl.ds(start, WIDTH // N_FSDP), :].astype(BF)
+
+
+def dense_call(core, attended_all, back, normed, grad_projected, packed, side):
+    shape = jax.ShapeDtypeStruct((N_YZ, WIDTH // N_FSDP, DENSE_COLS), BF)
+    return pl.pallas_call(
+        dense_kernel,
+        in_specs=[pl.BlockSpec(memory_space=pltpu.SMEM), *[pl.BlockSpec(memory_space=pltpu.VMEM)] * 6],
+        out_shape=[shape, shape],
+        scratch_shapes=[pltpu.VMEM((WIDTH, DENSE_COLS), F32)],
+        compiler_params=pltpu.CompilerParams(vmem_limit_bytes=48 * 1024 * 1024),
+        cost_estimate=pl.CostEstimate(flops=0, bytes_accessed=0, transcendentals=0),
+        name="dense",
+    )(core.reshape(1), attended_all, back, normed, grad_projected, packed, side)
+
+
 def rotation(count, by):
     return [(i, (i + by) % count) for i in range(count)]
 
@@ -639,16 +729,6 @@
 
 def after(value, *others):
     return lax.optimization_barrier((value, *others))[0]
-
-
-def gather_pairs(value, partner, index, axis, *others):
-    pair = after(pair_up(value, partner, index, 0), *others)
-    return lax.all_to_all(jnp.broadcast_to(pair[None], (4, *pair.shape)), axis, 0, 0, tiled=True)
-
-
-def gather_experts(value, *others):
-    partner = lax.ppermute(value, "zl", SWAP)
-    return gather_pairs(value, partner, lax.axis_index("zl"), "x", *others).reshape(N_EXP, *value.shape)
 
 
 def sum_start(*parts):
@@ -708,28 +788,31 @@
         axis=1,
     )
     packet = pair_up(packet, core_swap(packet), c, 0)
-    mixed, packet = lax.optimization_barrier((mixed, packet))
-    weights = lax.all_gather(mixed, YZ, axis=0, tiled=False)
     packet = pair_up(packet, lax.ppermute(packet, "zh", SWAP), zh, 0)
 
     tok_packet = jnp.concatenate(
         [tokens[0], routes[0].astype(BF), jnp.zeros((TOK, SIDE - routes.shape[-1]), BF)], axis=1
     )
     tok_pair = pair_up(tok_packet, lax.ppermute(tok_packet, "zl", SWAP), lax.axis_index("zl"), 0)
-    tok_pair = after(tok_pair.reshape(2 * TOK, -1), packet)
+    out_partner = lax.ppermute(w_out, ("zl", "zh"), ((0, 3), (1, 2), (2, 1), (3, 0)))
+
+    mixed, tok_pair, packet, out_partner = lax.optimization_barrier((mixed, tok_pair, packet, out_partner))
+    weights = lax.all_gather(mixed, YZ, axis=0, tiled=False)
+    tok_pair = tok_pair.reshape(2 * TOK, -1)
     tok_blocks = straight_four(tok_pair, "x")
-    y = lax.axis_index("y")
+    packet_pieces = straight_four(packet, "y")
+
+    tok_blocks, packet_pieces = lax.optimization_barrier((tok_blocks, packet_pieces))
+    out_pair = after(pair_up(w_out, out_partner, zh, 0), packet_pieces)
+    out_pieces = straight_four(out_pair, "y")
     packed = jnp.zeros((4, *packet.shape), BF)
-    for k, piece in enumerate(straight_four(packet, "y")):
-        packed = lax.dynamic_update_slice(packed, piece[None], (lax.rem(y + k, 4), 0, 0, 0, 0))
+    for k, piece in enumerate(packet_pieces):
+        spot = lax.rem(lax.axis_index("y") + k, 4)
+        packed = lax.dynamic_update_slice(packed, piece[None], (spot, 0, 0, 0, 0))
     packed = packed.reshape(WIDTH, PACK)
     router = packed[:, QKV_COLS : QKV_COLS + EXPERTS]
     gain_one = packed[:, QKV_COLS + EXPERTS].astype(F32)
     gain_two = packed[:, QKV_COLS + EXPERTS + 1].astype(F32)
-
-    out_partner = lax.ppermute(w_out, ("zl", "zh"), ((0, 3), (1, 2), (2, 1), (3, 0)))
-    out_mine = gather_pairs(w_out, out_partner, zh, "y")
-    tok_blocks, packed, out_mine = lax.optimization_barrier((tok_blocks, packed, out_mine))
 
     lanes = jnp.arange(QK_COLS, dtype=jnp.int32)
     inv_freq = THETA ** (-2.0 * (lanes % (HEAD_SIZE // 2)).astype(F32) / HEAD_SIZE)
@@ -743,10 +826,10 @@
     routes_all = tok_all[:, WIDTH:]
     routes_pair = jnp.concatenate([routes_all, core_swap(routes_all)]).astype(jnp.int32)
     routes_turned = ((routes_pair + (EXPERTS - e * EXP_DEV)) % EXPERTS).astype(BF)
-    attended_all = to_all(after(attended_low, routes_turned), EXP, N_EXP)
-    full_out = jnp.zeros((4, 2, 2, *w_out.shape), BF)
-    full_out = lax.dynamic_update_slice(full_out, out_mine[:, :, None], (0, 0, c, 0, 0))
-    full_out = lax.dynamic_update_slice(full_out, core_swap(out_mine)[:, :, None], (0, 0, 1 - c, 0, 0))
+    attended_pair = pair_up(attended_low, lax.ppermute(attended_low, "zl", SWAP), lax.axis_index("zl"), 0)
+    attended_all = to_all(after(attended_pair, routes_turned), "x", 4).reshape(N_EXP, SEQ, HEAD_COLS)
+    out_mine = line_up(after(out_pieces, attended_low), lax.axis_index("y"))
+    full_out = both_cores(out_mine, core_swap(out_mine), c)
     full_out = full_out.reshape(N_EXP, HEAD_COLS, WIDTH)
 
     features = tok_all[:, :WIDTH].astype(F32)
@@ -810,23 +893,12 @@
         back, heads, attended, stats, cosine, sine, seg_rows, seg_cols
     )
 
-    columns = [
-        ein("etk,tn->ekn", attended_all, back[:, HEAD_COLS:]).reshape(WIDTH, HEAD_COLS),
-        contract(normed_one, grad_projected, ((0,), (0,)))[:, :QKV_COLS],
-        router_part,
-        gain_two_part[:, None],
-        jnp.zeros((WIDTH, DENSE_COLS - HEAD_COLS - QKV_COLS - EXPERTS - 1), F32),
-    ]
-    parts = jnp.concatenate([column.astype(BF) for column in columns], axis=1)
-    parts = parts.reshape(N_YZ, 2, WIDTH // N_FSDP, DENSE_COLS)
-    grad_projected, parts = lax.optimization_barrier((grad_projected, parts))
+    side = jnp.concatenate(
+        [router_part, gain_two_part[:, None], jnp.zeros((WIDTH, SIDE - EXPERTS - 1), F32)], axis=1
+    )
     normed_grad_part = contract(grad_projected, packed, ((1,), (1,)))
-    gain_one_part = jnp.sum(features * rms_inverse(features) * normed_grad_part, axis=0)
-    gain_blocks = gain_one_part.astype(BF).reshape(N_YZ, 2, WIDTH // N_FSDP, 1)
-    parts = jnp.where(jnp.arange(DENSE_COLS, dtype=jnp.int32) == DENSE_COLS - 1, gain_blocks, parts)
-    keep = jnp.where(c == 0, parts[:, 0], parts[:, 1])
-    arrived = core_swap(jnp.where(c == 0, parts[:, 1], parts[:, 0]))
-    parts = (keep.astype(F32) + arrived.astype(F32)).astype(BF)
+    keep, send = dense_call(c, attended_all, back, normed_one, grad_projected, packed, side)
+    parts = (keep.astype(F32) + core_swap(send).astype(F32)).astype(BF)
     normed_rows, normed_sent = sum_start(normed_grad_part.astype(BF))
     normed_arrived = sum_send(normed_sent)
     exchanged = exchange(parts, YZ)
@@ -843,22 +915,9 @@
         (exchanged, normed_arrived, total_gu, total_down)
     )
     summed = jnp.sum(exchanged.astype(F32), axis=0).astype(BF)
-    totals = to_all(summed, EXP, N_EXP).astype(F32)
+    totals = to_all(summed, EXP, N_EXP)
     grad_normed_one = sum_finish(normed_rows, after(normed_arrived, summed))
-
-    def head_columns(start, width):
-        return jnp.transpose(totals[..., start : start + width], (1, 0, 2)).reshape(-1, N_EXP * width)
-
-    total_out = head_columns(0, HEAD_COLS)
-    total_qkv = jnp.concatenate(
-        [
-            head_columns(HEAD_COLS, HEAD_COLS),
-            head_columns(2 * HEAD_COLS, HEAD_SIZE),
-            head_columns(2 * HEAD_COLS + HEAD_SIZE, HEAD_SIZE),
-        ],
-        axis=1,
-    )
-    shared = jnp.sum(totals[..., HEAD_COLS + QKV_COLS :], axis=0)
+    total_out, total_qkv, shared = arrange_call(totals)
 
     own_tokens = tokens[0].astype(F32)
     grad_in, _ = rms_backward(own_tokens, rms_inverse(own_tokens), gain_one, grad_normed_one)
@@ -867,7 +926,7 @@
     return (
         output[None],
         grad_tokens[None],
-        shared[:, -1],
+        shared[:, SIDE - 1],
         total_qkv,
         total_out,
         shared[:, EXPERTS],

time: 561 us -> 541 us (0.964)
  waiting for transfers between devices: 231 us -> 208 us
  Pallas kernels: 112 us -> 127 us
  local copies, waits for them, and re-layouts: 53.8 us -> 45.1 us
  matrix products: 32.5 us -> 25.1 us
    ppermute x0 -> x1, waiting for transfers between devices: none -> 23.5 us  [body(): lax.ppermute(attended_low, 'zl', SWAP)]
    ppermute x6 -> x9, waiting for transfers between devices: 52.9 us -> 32.3 us  [straight_four(): lax.ppermute(block, axis, rotation(4, k))]
    ppermute x9, waiting for transfers between devices: 50.7 us -> 30.3 us  [sum_send(): lax.ppermute(value, 'x', rotation(4, k))]
    pallas_call x0 -> x4, Pallas kernels: none -> 14.9 us  [the longest x1 9.42 us: dense_call(): pl.pallas_call(dense_kernel, in_specs=[pl.BlockSpec(memory_space=pltpu.SM...]
    all_gather x1, waiting for transfers between devices: 14.5 us -> 0.01 us  [body(): weights = lax.all_gather(mixed, YZ, axis=0, tiled=False)]
    reduce_scatter x1, waiting for transfers between devices: 4.68 us -> 16.6 us  [body(): lax.psum_scatter(grad_weights, YZ, scatter_dimension=0, tiled=False)]
    ppermute x1, waiting for transfers between devices: 3.65 us -> 10.9 us  [body(): packet = pair_up(packet, lax.ppermute(packet, 'zh', SWAP), zh, 0)]
    ppermute x1, waiting for transfers between devices: 6.9 us -> 0.01 us  [body(): lax.ppermute(w_out, ('zl', 'zh'), ((0, 3), (1, 2), (2, 1), (3, 0)))]
  transfers between devices with their start and end apart: 40 -> 43, of which waited for: 20 -> 16; matrix products, arithmetic and copies ran while one was open for 19% -> 18% of each run, Pallas kernels for 20% -> 24%
where the time goes in v4:
time: 541 us; the launch traced here: 534 us
  waiting for transfers between devices  208 us (38%)
  Pallas kernels  127 us (23%)
  starting transfers between devices  65.2 us (12%)
  other arithmetic  49.5 us (9%)
  local copies, waits for them, and re-layouts  45.1 us (8%)
  matrix products  25.1 us (5%)
  between operations  14.8 us (3%)
    pallas_call x1, Pallas kernels, experts_backward(): pl.pallas_call(backward_kernel, grid=(2 * STEPS + EXP_DEV,), in_specs=[pl...  46.7 us
    all_to_all x2, waiting for transfers between devices, to_all(): return lax.all_to_all(spread, axes, 0, 0, tiled=True)  44.6 us
    pallas_call x1, Pallas kernels, experts_forward(): pl.pallas_call(forward_kernel, grid=(2 * STEPS + EXP_DEV,), in_specs=[pl....  40.4 us
    ppermute x9, waiting for transfers between devices, straight_four(): lax.ppermute(block, axis, rotation(4, k))  32.3 us
    ppermute x9, waiting for transfers between devices, sum_send(): lax.ppermute(value, 'x', rotation(4, k))  30.3 us
    ppermute x1, waiting for transfers between devices, body(): lax.ppermute(attended_low, 'zl', SWAP)  23.5 us
    unnamed x99, local copies, waits for them, and re-layouts  18.9 us
    ppermute x3, waiting for transfers between devices, sum_finish(): return keep + lax.ppermute(send, 'zl', SWAP).astype(F32)  16.9 us
  transfers between devices with their start and end apart: 43, of which 16 were waited for; matrix products, arithmetic and copies ran while one was open for 18% of the time, Pallas kernels for 24%

profile of v4, /device:TPU:1, one launch (start us, length us, event | category | flops | bytes accessed | tf_op | source)
XLA Modules:
  0.0 534.3 jit_solution(10252217824462120696)
XLA Ops:
  16.9 2.2 collective-permute-start.4
  21.9 10.9 %collective-permute-done.3 = bf16[2,96,384]{2,1,0:T(8,128)(2,1)S(1)} collective-permute-done((bf16[2,96,384]{2,1,0:T(8,128)(2,1)S(1)}, bf16[2,96,384]{2,1,0:T(8,128)(2,1)S(1)}, u32[]{:S(2)}, u32[]{:S(2)}) %collective-permute-start.3) | collective-permute-done | bytes 147488 | tf_op jit(solution)/shard_map/ppermute | solution.py:791
  37.6 2.5 collective-permute-start.5
  44.1 4.9 collective-permute-done.10
  51.0 5.6 %fusion.8 = (f32[1024,256]{1,0:T(8,128)}, f32[1024,256]{1,0:T(8,128)}) fusion(f32[256]{0:T(256)S(1)} %get-tuple-element.203, f32[256]{0:T(256)S(1)} %get-tuple-element.204, f32[1024]{0:T(1024)S(1)} %iota_convert_fusion), kind=kLoop, calls=%fused_computation.33 | loop fusion | flops 524288 | bytes 2103296 | tf_op jit(solution)/shard_map/mul | solution.py:821
  56.6 7.8 %collective-permute-done.9 = bf16[2,2,96,384]{3,2,1,0:T(8,128)(2,1)} collective-permute-done((bf16[2,2,96,384]{3,2,1,0:T(8,128)(2,1)S(1)}, bf16[2,2,96,384]{3,2,1,0:T(8,128)(2,1)}, u32[]{:S(2)}, u32[]{:S(2)}) %collective-permute-start.9) | collective-permute-done | bytes 294944 | tf_op jit(solution)/shard_map/ppermute | solution.py:723
  65.3 15.6 %collective-permute-done.7.block_3 = bf16[256,1664]{1,0:T(8,128)(2,1)} collective-permute-done((bf16[256,1664]{1,0:T(8,128)(2,1)S(1)}, bf16[256,1664]{1,0:T(8,128)(2,1)}, u32[]{:S(2)}, u32[]{:S(2)}) %collective-permute-start.7) | collective-permute-done | bytes 852000 | tf_op jit(solution)/shard_map/ppermute | solution.py:723
  84.4 14.1 %attend.1 = (bf16[1024,1664]{1,0:T(8,128)(2,1)}, bf16[1024,1536]{1,0:T(8,128)(2,1)}, bf16[1024,384]{1,0:T(8,128)(2,1)S(1)}, f32[1024,192]{1,0:T(8,128)}, bf16[10...) custom-call(s32[1]{0:T(128)} %bitcast.place_ref, bf16[256,1664]{1,0:T(8,128)(2,1)S(1)} %bitcast.102, ...), custom_call_target="tpu_custom_call" | custom-call | flops 12999999488 | bytes 12000000 | tf_op jit(solution)/shard_map/attend/pallas_call | solution.py:507
  101.6 2.8 collective-permute-start.13
  107.0 23.5 %collective-permute-done.11 = bf16[1024,192]{1,0:T(8,128)(2,1)S(1)} collective-permute-done((bf16[1024,192]{1,0:T(8,128)(2,1)}, bf16[1024,192]{1,0:T(8,128)(2,1)S(1)}, u32[]{:S(2)}, u32[]{:S(2)}) %collective-permute-start.11) | collective-permute-done | bytes 393248 | tf_op jit(solution)/shard_map/ppermute | solution.py:829
  130.5 2.6 maximum_select_fusion
  134.0 3.9 collective-permute-done.15.piece_3
  143.4 2.1 broadcast_in_dim.96
  145.5 4.7 all-to-all-start
  150.2 4.1 both_cores.1
  154.3 33.5 %all-to-all-done = bf16[4,2,1024,192]{2,3,1,0:T(8,128)(2,1)} async-done(((bf16[4,2,1024,192]{2,3,1,0:T(8,128)(2,1)}), bf16[4,2,1024,192]{2,3,1,0:T(8,128)(2,1)}, u32[]{:S(2)}, u32[]{:S(2)}) %all-to-all-start) | async-done | bytes 3145760 | tf_op jit(solution)/shard_map/all_to_all | solution.py:69
  187.8 9.3 %multiply_reduce_fusion = (f32[1024]{0:T(1024)S(1)}, f32[1024,1536]{1,0:T(8,128)S(1)}) fusion(bf16[8,1024,192]{1,2,0:T(8,128)(2,1)} %bitcast.30, bf16[8,192,1536]{2,1,0:T(8,128)(2,1)} %bitcast.106, bf16[1024,1664]{1,0:T(8,128)(2,1)} %get-tuple-element.77), kind=kOutput, calls=%fused_computation.2 | convolution fusion | flops 4838128640 | bytes 17305600 | tf_op jit(solution)/shard_map/etk,ekn->tn/dot_general | solution.py:60
  197.1 2.6 copy-done.19
  199.7 2.2 multiply_convert_fusion.n_own
  202.9 10.7 %collective-permute-done.19 = bf16[128,1536]{1,0:T(8,128)(2,1)S(1)} collective-permute-done((bf16[128,1536]{1,0:T(8,128)(2,1)S(1)}, bf16[128,1536]{1,0:T(8,128)(2,1)S(1)}, u32[]{:S(2)}, u32[]{:S(2)}) %collective-permute-start.19) | collective-permute-done | bytes 393248 | tf_op jit(solution)/shard_map/ppermute | solution.py:840
  216.2 40.4 %experts_forward.1 = (bf16[1024,1536]{1,0:T(8,128)(2,1)}, bf16[1024,1536]{1,0:T(8,128)(2,1)}, bf16[5,768,1536]{2,1,0:T(8,128)(2,1)}, bf16[5,768,640]{2,1,0:T(8,128)(2,1)}) custom-call(bf16[1024,1536]{1,0:T(8,128)(2,1)} %multiply_convert_fusion.n_own, bf16[1024,1536]{1,0:T(8,128)(2,1)} %collective-permute-done.17.n_par, bf16[2048,128]{1,0:T(8,128)(2,1)} %fusion.9.routes, ...), custom_call_target="tpu_custom_call" | custom-call | flops 40000000000 | bytes 40000000 | tf_op jit(solution)/shard_map/experts_forward/pallas_call | solution.py:372
  257.7 5.3 collective-permute-done.18
  263.1 4.0 add_convert_fusion.4
  270.0 46.7 %experts_backward.1 = (bf16[1024,1664]{1,0:T(8,128)(2,1)}, bf16[1024,1664]{1,0:T(8,128)(2,1)}, bf16[8,5,288,512]{3,2,1,0:T(8,128)(2,1)}) custom-call(s32[1]{0:T(128)} %bitcast.38.place_ref, bf16[1024,1536]{1,0:T(8,128)(2,1)} %bitcast.133, bf16[1024,1536]{1,0:T(8,128)(2,1)} %collective-permute-done.20.g_par, bf16[2048,128]{1,0:T(8,128)(2,1)} %fusion.9.routes, ...), custom_call_target="tpu_custom_call" | custom-call | flops 49999998976 | bytes 60000000 | tf_op jit(solution)/shard_map/experts_backward/pallas_call | solution.py:400
  319.2 5.9 %collective-permute-done.24 = bf16[1024,1664]{1,0:T(8,128)(2,1)S(1)} collective-permute-done((bf16[1024,1664]{1,0:T(8,128)(2,1)}, bf16[1024,1664]{1,0:T(8,128)(2,1)S(1)}, u32[]{:S(2)}, u32[]{:S(2)}) %collective-permute-start.24) | collective-permute-done | bytes 3407904 | tf_op jit(solution)/shard_map/ppermute | solution.py:64
  325.0 4.8 add_convert_fusion.3
  331.8 2.4 collective-permute-start.27
  334.4 6.0 %copy.68 = bf16[4,2,1024,192]{3,2,1,0:T(8,128)(2,1)} copy(bf16[4,2,1024,192]{2,3,1,0:T(8,128)(2,1)} %all-to-all-done) | data formatting | bytes 6291456 | tf_op jit(solution)/shard_map/all_to_all | solution.py:69
  340.5 11.2 %collective-permute-done.25 = bf16[256,1664]{1,0:T(8,128)(2,1)S(1)} collective-permute-done((bf16[256,1664]{1,0:T(8,128)(2,1)}, bf16[256,1664]{1,0:T(8,128)(2,1)S(1)}, u32[]{:S(2)}, u32[]{:S(2)}) %collective-permute-start.25) | collective-permute-done | bytes 852000 | tf_op jit(solution)/shard_map/ppermute | solution.py:746
  351.7 19.0 %collective-permute-done.26 = bf16[256,1664]{1,0:T(8,128)(2,1)S(1)} collective-permute-done((bf16[256,1664]{1,0:T(8,128)(2,1)}, bf16[256,1664]{1,0:T(8,128)(2,1)S(1)}, u32[]{:S(2)}, u32[]{:S(2)}) %collective-permute-start.26) | collective-permute-done | bytes 852000 | tf_op jit(solution)/shard_map/ppermute | solution.py:746
  371.7 2.8 add_add_fusion
  376.6 16.8 %collective-permute-done.28 = bf16[128,1664]{1,0:T(8,128)(2,1)S(1)} collective-permute-done((bf16[128,1664]{1,0:T(8,128)(2,1)S(1)}, bf16[128,1664]{1,0:T(8,128)(2,1)S(1)}, u32[]{:S(2)}, u32[]{:S(2)}) %collective-permute-start.28) | collective-permute-done | bytes 426016 | tf_op jit(solution)/shard_map/ppermute | solution.py:754
  395.6 2.3 fusion.53
  398.1 3.7 fusion.7
  402.8 4.6 all-to-all-start.1
  409.3 10.6 %all-to-all-done.1 = bf16[8,128,384]{1,2,0:T(8,128)(2,1)} async-done(((bf16[8,128,384]{1,2,0:T(8,128)(2,1)}), bf16[8,128,384]{1,2,0:T(8,128)(2,1)}, u32[]{:S(2)}, u32[]{:S(2)}) %all-to-all-start.1) | async-done | bytes 786464 | tf_op jit(solution)/shard_map/all_to_all | solution.py:73
  426.0 10.9 %attend_back.1.grad_projected = bf16[1024,384]{1,0:T(8,128)(2,1)S(1)} custom-call(bf16[1024,384]{1,0:T(8,128)(2,1)S(1)} %bitcast.97, bf16[1024,384]{1,0:T(8,128)(2,1)S(1)} %copy-done.16, f32[1024,192]{1,0:T(8,128)S(1)} %copy-done.14, f32[1024,8]{1,0:T(8,128)S(1)} %copy-done.18, bf16[1024,384]{1,0:T(8,128)(2,1)S(1)} %copy-done.16, f32[1024,256]{1,0:T(8,128)S(1)} %copy-done.4, ...), custom_call_target="tpu_custom_call" | custom-call | flops 11000000512 | bytes 8000000 | tf_op jit(solution)/shard_map/attend_back/pallas_call | solution.py:601
  436.9 9.4 %dense.1 = (bf16[8,96,640]{2,1,0:T(8,128)(2,1)S(1)}, bf16[8,96,640]{2,1,0:T(8,128)(2,1)S(1)}) custom-call(s32[1]{0:T(128)} %bitcast.31.core, bf16[8,1024,192]{2,1,0:T(8,128)(2,1)} %bitcast.105, bf16[1024,384]{1,0:T(8,128)(2,1)S(1)} %bitcast.98, bf16[1024,1536]{1,0:T(8,128)(2,1)} %get-tuple-element.109.normed, ...), custom_call_target="tpu_custom_call" | custom-call | tf_op jit(solution)/shard_map/dense/pallas_call | solution.py:707
  446.3 2.8 collective-permute-start.30
  455.6 2.4 collective-permute-start.33
  462.1 4.7 all-to-all-start.2
  466.9 16.6 %reduce-scatter.2.cloned.1.call-done = bf16[1,5,288,512]{3,2,1,0:T(8,128)(2,1)} async-done(((bf16[8,5,288,512]{3,2,1,0:T(8,128)(2,1)}), bf16[1,5,288,512]{3,2,1,0:T(8,128)(2,1)}) %reduce-scatter.2.cloned.1.call-update) | async-done | bytes 1474576 | tf_op jit(solution)/shard_map/reduce_scatter | solution.py:861
  485.9 2.4 collective-permute-start.34
  493.9 2.2 add_add_fusion.1
  496.9 2.1 fusion.23
  500.0 10.0 %all-to-all-start.3 = ((bf16[8,96,640]{2,1,0:T(8,128)(2,1)}), bf16[8,96,640]{2,1,0:T(8,128)(2,1)S(1)}, u32[]{:S(2)}, u32[]{:S(2)}) async-start(bf16[8,96,640]{2,1,0:T(8,128)(2,1)} %broadcast_in_dim.103), calls=%async_computation.4 | async-start | bytes 1966080 | tf_op jit(solution)/shard_map/all_to_all | solution.py:69
  511.4 2.3 fusion.24
  513.8 11.1 %all-to-all-done.3.totals = bf16[8,96,640]{2,1,0:T(8,128)(2,1)S(1)} async-done(((bf16[8,96,640]{2,1,0:T(8,128)(2,1)}), bf16[8,96,640]{2,1,0:T(8,128)(2,1)S(1)}, u32[]{:S(2)}, u32[]{:S(2)}) %all-to-all-start.3) | async-done | bytes 983072 | tf_op jit(solution)/shard_map/all_to_all | solution.py:69
  (237 shorter events, 89.9 us)
Async XLA Ops:
  7.2 207.4 %all-gather.5.cloned.1.call-start = ((), (), s32[]{:S(2)}) async-start(), calls=%async_computation.6 | async-start | bytes 13271040 | tf_op jit(solution)/shard_map/all_gather | solution.py:800
  11.7 8.9 %collective-permute-start.2 = (bf16[96,384]{1,0:T(8,128)(2,1)S(1)}, bf16[96,384]{1,0:T(8,128)(2,1)S(1)}, u32[]{:S(2)}, u32[]{:S(2)}) collective-permute-start(bf16[96,384]{1,0:T(8,128)(2,1)S(1)} %concatenate.40), channel_id=1, source_target_pairs={{0,1},{1,0},{2,3},{3,2},{4,5},{5,4},{6,7},{7,6},{8,9},{9,8},{10,11... | collective-permute-start | bytes 221192 | tf_op jit(solution)/shard_map/ppermute | solution.py:64
  14.8 20.2 %collective-permute-start = (bf16[5,96,512]{2,1,0:T(8,128)(2,1)}, bf16[5,96,512]{2,1,0:T(8,128)(2,1)}, u32[]{:S(2)}, u32[]{:S(2)}) collective-permute-start(bf16[5,96,512]{2,1,0:T(8,128)(2,1)} %bitcast.5), channel_id=1, source_target_pairs={{0,1},{1,0},{2,3},{3,2},{4,5},{5,4},{6,7},{7,6},{8,9},{9,8},{10,11... | collective-permute-start | bytes 1474568 | tf_op jit(solution)/shard_map/ppermute | solution.py:64
  15.1 17.8 %collective-permute-start.1 = (bf16[128,1664]{1,0:T(8,128)(2,1)S(1)}, bf16[128,1664]{1,0:T(8,128)(2,1)S(1)}, u32[]{:S(2)}, u32[]{:S(2)}) collective-permute-start(bf16[128,1664]{1,0:T(8,128)(2,1)S(1)} %concatenate.39), channel_id=1, source_target_pairs={{0,16},{16,0},{1,17},{17,1},{2,18},{18,2},{3,19},{19,3},{4,20},{20... | collective-permute-start | bytes 1277960 | tf_op jit(solution)/shard_map/ppermute | solution.py:796
  16.9 20.8 %collective-permute-start.4 = (bf16[96,1536]{1,0:T(8,128)(2,1)}, bf16[96,1536]{1,0:T(8,128)(2,1)}, u32[]{:S(2)}, u32[]{:S(2)}) collective-permute-start(bf16[96,1536]{1,0:T(8,128)(2,1)} %param.16), channel_id=1, source_target_pairs={{0,18},{2,16},{16,2},{18,0},{1,19},{3,17},{17,3},{19,1},{4,22},{6,... | collective-permute-start | bytes 884744 | tf_op jit(solution)/shard_map/ppermute | solution.py:797
  20.7 12.1 %collective-permute-start.3 = (bf16[2,96,384]{2,1,0:T(8,128)(2,1)S(1)}, bf16[2,96,384]{2,1,0:T(8,128)(2,1)S(1)}, u32[]{:S(2)}, u32[]{:S(2)}) collective-permute-start(bf16[2,96,384]{2,1,0:T(8,128)(2,1)S(1)} %maximum_select_fusion.7), channel_id=1, source_target_pairs={{0,2},{2,0},{1,3},{3,1},{4,6},{6,4},{5,7},{7,5},{8,10},{10,8},{9,1... | collective-permute-start | bytes 442376 | tf_op jit(solution)/shard_map/ppermute | solution.py:791
  32.8 16.2 %copy-start.26 = (bf16[2,2,96,384]{3,2,1,0:T(8,128)(2,1)}, bf16[2,2,96,384]{3,2,1,0:T(8,128)(2,1)S(1)}, u32[]{:S(2)}) copy-start(bf16[2,2,96,384]{3,2,1,0:T(8,128)(2,1)S(1)} %maximum_select_fusion.5) | copy-start | bytes 884740
  37.6 26.8 %collective-permute-start.5 = (bf16[256,1664]{1,0:T(8,128)(2,1)S(1)}, bf16[256,1664]{1,0:T(8,128)(2,1)S(1)}, u32[]{:S(2)}, u32[]{:S(2)}) collective-permute-start(bf16[256,1664]{1,0:T(8,128)(2,1)S(1)} %bitcast.99), channel_id=1, source_target_pairs={{0,96},{32,0},{64,32},{96,64},{1,97},{33,1},{65,33},{97,65},{2,98}... | collective-permute-start | bytes 2555912 | tf_op jit(solution)/shard_map/ppermute | solution.py:723
  40.2 24.2 %collective-permute-start.6 = (bf16[256,1664]{1,0:T(8,128)(2,1)S(1)}, bf16[256,1664]{1,0:T(8,128)(2,1)S(1)}, u32[]{:S(2)}, u32[]{:S(2)}) collective-permute-start(bf16[256,1664]{1,0:T(8,128)(2,1)S(1)} %bitcast.100), channel_id=1, source_target_pairs={{0,64},{32,96},{64,0},{96,32},{1,65},{33,97},{65,1},{97,33},{2,66}... | collective-permute-start | bytes 2555912 | tf_op jit(solution)/shard_map/ppermute | solution.py:723
  40.7 40.2 %collective-permute-start.7 = (bf16[256,1664]{1,0:T(8,128)(2,1)S(1)}, bf16[256,1664]{1,0:T(8,128)(2,1)}, u32[]{:S(2)}, u32[]{:S(2)}) collective-permute-start(bf16[256,1664]{1,0:T(8,128)(2,1)S(1)} %bitcast.101), channel_id=1, source_target_pairs={{0,32},{32,64},{64,96},{96,0},{1,33},{33,65},{65,97},{97,1},{2,34}... | collective-permute-start | bytes 2555912 | tf_op jit(solution)/shard_map/ppermute | solution.py:723
  41.3 7.7 %collective-permute-start.10 = (bf16[2,2,96,384]{3,2,1,0:T(8,128)(2,1)S(1)}, bf16[2,2,96,384]{3,2,1,0:T(8,128)(2,1)S(1)}, u32[]{:S(2)}, u32[]{:S(2)}) collective-permute-start(bf16[2,2,96,384]{3,2,1,0:T(8,128)(2,1)S(1)} %maximum_select_fusion.5), channel_id=1, source_target_pairs={{0,4},{4,8},{8,12},{12,0},{1,5},{5,9},{9,13},{13,1},{2,6},{6,10},{... | collective-permute-start | bytes 884744 | tf_op jit(solution)/shard_map/ppermute | solution.py:723
  42.6 14.0 %collective-permute-start.8 = (bf16[2,2,96,384]{3,2,1,0:T(8,128)(2,1)S(1)}, bf16[2,2,96,384]{3,2,1,0:T(8,128)(2,1)}, u32[]{:S(2)}, u32[]{:S(2)}) collective-permute-start(bf16[2,2,96,384]{3,2,1,0:T(8,128)(2,1)S(1)} %maximum_select_fusion.5), channel_id=1, source_target_pairs={{0,12},{4,0},{8,4},{12,8},{1,13},{5,1},{9,5},{13,9},{2,14},{6,2},{... | collective-permute-start | bytes 884744 | tf_op jit(solution)/shard_map/ppermute | solution.py:723
  49.0 15.4 %collective-permute-start.9 = (bf16[2,2,96,384]{3,2,1,0:T(8,128)(2,1)S(1)}, bf16[2,2,96,384]{3,2,1,0:T(8,128)(2,1)}, u32[]{:S(2)}, u32[]{:S(2)}) collective-permute-start(bf16[2,2,96,384]{3,2,1,0:T(8,128)(2,1)S(1)} %maximum_select_fusion.5), channel_id=1, source_target_pairs={{0,8},{4,12},{8,0},{12,4},{1,9},{5,13},{9,1},{13,5},{2,10},{6,14},... | collective-permute-start | bytes 884744 | tf_op jit(solution)/shard_map/ppermute | solution.py:723
  51.0 32.9 %copy-start.9 = (s32[1024,1]{1,0:T(8,128)}, s32[1024,1]{1,0:T(8,128)S(1)}, u32[]{:S(2)}) copy-start(s32[1024,1]{1,0:T(8,128)S(1)} %copy.66.seg_rows) | copy-start | bytes 12292
  51.0 30.0 %copy-start.27 = (bf16[2,2,96,384]{3,2,1,0:T(8,128)(2,1)S(1)}, bf16[2,2,96,384]{3,2,1,0:T(8,128)(2,1)}, u32[]{:S(2)}) copy-start(bf16[2,2,96,384]{3,2,1,0:T(8,128)(2,1)} %copy-done.26) | copy-start | bytes 884740
  56.6 26.6 %copy-start.40 = (bf16[2,2,96,384]{3,2,1,0:T(8,128)(2,1)S(1)}, bf16[2,2,96,384]{3,2,1,0:T(8,128)(2,1)}, u32[]{:S(2)}) copy-start(bf16[2,2,96,384]{3,2,1,0:T(8,128)(2,1)} %copy-done.39) | copy-start | bytes 884740
  99.7 5.8 %collective-permute-start.12 = (bf16[1024,128]{1,0:T(8,128)(2,1)S(1)}, bf16[1024,128]{1,0:T(8,128)(2,1)S(1)}, u32[]{:S(2)}, u32[]{:S(2)}) collective-permute-start(bf16[1024,128]{1,0:T(8,128)(2,1)S(1)} %slice.69), channel_id=1, source_target_pairs={{0,1},{1,0},{2,3},{3,2},{4,5},{5,4},{6,7},{7,6},{8,9},{9,8},{10,11... | collective-permute-start | bytes 786440 | tf_op jit(solution)/shard_map/ppermute | solution.py:64
  101.6 31.5 %collective-permute-start.13 = (bf16[2,96,1536]{2,1,0:T(8,128)(2,1)S(1)}, bf16[2,96,1536]{2,1,0:T(8,128)(2,1)S(1)}, u32[]{:S(2)}, u32[]{:S(2)}) collective-permute-start(bf16[2,96,1536]{2,1,0:T(8,128)(2,1)S(1)} %maximum_select_fusion.4.piece_0), channel_id=1, source_target_pairs={{0,12},{4,0},{8,4},{12,8},{1,13},{5,1},{9,5},{13,9},{2,14},{6,2},{... | collective-permute-start | bytes 1769480 | tf_op jit(solution)/shard_map/ppermute | solution.py:723
  104.5 28.7 %collective-permute-start.14 = (bf16[2,96,1536]{2,1,0:T(8,128)(2,1)S(1)}, bf16[2,96,1536]{2,1,0:T(8,128)(2,1)S(1)}, u32[]{:S(2)}, u32[]{:S(2)}) collective-permute-start(bf16[2,96,1536]{2,1,0:T(8,128)(2,1)S(1)} %maximum_select_fusion.4.piece_0), channel_id=1, source_target_pairs={{0,8},{4,12},{8,0},{12,4},{1,9},{5,13},{9,1},{13,5},{2,10},{6,14},... | collective-permute-start | bytes 1769480 | tf_op jit(solution)/shard_map/ppermute | solution.py:723
  104.8 33.1 %collective-permute-start.15 = (bf16[2,96,1536]{2,1,0:T(8,128)(2,1)S(1)}, bf16[2,96,1536]{2,1,0:T(8,128)(2,1)S(1)}, u32[]{:S(2)}, u32[]{:S(2)}) collective-permute-start(bf16[2,96,1536]{2,1,0:T(8,128)(2,1)S(1)} %maximum_select_fusion.4.piece_0), channel_id=1, source_target_pairs={{0,4},{4,8},{8,12},{12,0},{1,5},{5,9},{9,13},{13,1},{2,6},{6,10},{... | collective-permute-start | bytes 1769480 | tf_op jit(solution)/shard_map/ppermute | solution.py:723
  105.5 25.0 %collective-permute-start.11 = (bf16[1024,192]{1,0:T(8,128)(2,1)}, bf16[1024,192]{1,0:T(8,128)(2,1)S(1)}, u32[]{:S(2)}, u32[]{:S(2)}) collective-permute-start(bf16[1024,192]{1,0:T(8,128)(2,1)} %get-tuple-element.78), channel_id=1, source_target_pairs={{0,16},{16,0},{1,17},{17,1},{2,18},{18,2},{3,19},{19,3},{4,20},{20... | collective-permute-start | bytes 1179656 | tf_op jit(solution)/shard_map/ppermute | solution.py:829
  141.0 9.2 %collective-permute-start.16 = (bf16[4,2,96,1536]{3,2,1,0:T(8,128)(2,1)S(1)}, bf16[4,2,96,1536]{3,2,1,0:T(8,128)(2,1)}, u32[]{:S(2)}, u32[]{:S(2)}) collective-permute-start(bf16[4,2,96,1536]{3,2,1,0:T(8,128)(2,1)S(1)} %line_up.1.mine), channel_id=1, source_target_pairs={{0,1},{1,0},{2,3},{3,2},{4,5},{5,4},{6,7},{7,6},{8,9},{9,8},{10,11... | collective-permute-start | bytes 7077896 | tf_op jit(solution)/shard_map/ppermute | solution.py:64
  145.5 42.3 %all-to-all-start = ((bf16[4,2,1024,192]{2,3,1,0:T(8,128)(2,1)}), bf16[4,2,1024,192]{2,3,1,0:T(8,128)(2,1)}, u32[]{:S(2)}, u32[]{:S(2)}) async-start(bf16[4,2,1024,192]{2,3,1,0:T(8,128)(2,1)} %broadcast_in_dim.96), calls=%async_computation | async-start | bytes 6291456 | tf_op jit(solution)/shard_map/all_to_all | solution.py:69
  150.1 107.3 %all-gather.7.cloned.1.call-start = ((), (), s32[]{:S(2)}) async-start(), calls=%async_computation.7 | async-start | bytes 3932160 | tf_op jit(solution)/shard_map/all_gather | solution.py:842
  202.0 14.2 %collective-permute-start.17 = (bf16[1024,1536]{1,0:T(8,128)(2,1)}, bf16[1024,1536]{1,0:T(8,128)(2,1)}, u32[]{:S(2)}, u32[]{:S(2)}) collective-permute-start(bf16[1024,1536]{1,0:T(8,128)(2,1)} %multiply_convert_fusion.n_own), channel_id=1, source_target_pairs={{0,1},{1,0},{2,3},{3,2},{4,5},{5,4},{6,7},{7,6},{8,9},{9,8},{10,11... | collective-permute-start | bytes 9437192 | tf_op jit(solution)/shard_map/ppermute | solution.py:64
  202.9 10.7 %collective-permute-start.19 = (bf16[128,1536]{1,0:T(8,128)(2,1)S(1)}, bf16[128,1536]{1,0:T(8,128)(2,1)S(1)}, u32[]{:S(2)}, u32[]{:S(2)}) collective-permute-start(bf16[128,1536]{1,0:T(8,128)(2,1)S(1)} %bitcast.113), channel_id=1, source_target_pairs={{0,16},{16,0},{1,17},{17,1},{2,18},{18,2},{3,19},{19,3},{4,20},{20... | collective-permute-start | bytes 1179656 | tf_op jit(solution)/shard_map/ppermute | solution.py:840
  214.7 268.8 %reduce-scatter.2.cloned.1.call-start = ((), (), s32[]{:S(2)}) async-start(), calls=%async_computation.5 | async-start | bytes 13271040 | tf_op jit(solution)/shard_map/reduce_scatter | solution.py:861
  256.6 6.5 %collective-permute-start.18 = (bf16[1024,1536]{1,0:T(8,128)(2,1)}, bf16[1024,1536]{1,0:T(8,128)(2,1)}, u32[]{:S(2)}, u32[]{:S(2)}) collective-permute-start(bf16[1024,1536]{1,0:T(8,128)(2,1)} %get-tuple-element.88), channel_id=1, source_target_pairs={{0,1},{1,0},{2,3},{3,2},{4,5},{5,4},{6,7},{7,6},{8,9},{9,8},{10,11... | collective-permute-start | bytes 9437192 | tf_op jit(solution)/shard_map/ppermute | solution.py:64
  257.4 12.6 %collective-permute-start.20 = (bf16[1024,1536]{1,0:T(8,128)(2,1)}, bf16[1024,1536]{1,0:T(8,128)(2,1)}, u32[]{:S(2)}, u32[]{:S(2)}) collective-permute-start(bf16[1024,1536]{1,0:T(8,128)(2,1)} %bitcast.132), channel_id=1, source_target_pairs={{0,1},{1,0},{2,3},{3,2},{4,5},{5,4},{6,7},{7,6},{8,9},{9,8},{10,11... | collective-permute-start | bytes 9437192 | tf_op jit(solution)/shard_map/ppermute | solution.py:64
  267.1 49.6 %collective-permute-start.21 = (bf16[256,1536]{1,0:T(8,128)(2,1)}, bf16[256,1536]{1,0:T(8,128)(2,1)S(1)}, u32[]{:S(2)}, u32[]{:S(2)}) collective-permute-start(bf16[256,1536]{1,0:T(8,128)(2,1)} %get-tuple-element.95), channel_id=1, source_target_pairs={{0,64},{32,96},{64,0},{96,32},{1,65},{33,97},{65,1},{97,33},{2,66}... | collective-permute-start | bytes 2359304 | tf_op jit(solution)/shard_map/ppermute | solution.py:746
  267.4 49.4 %collective-permute-start.22 = (bf16[256,1536]{1,0:T(8,128)(2,1)}, bf16[256,1536]{1,0:T(8,128)(2,1)S(1)}, u32[]{:S(2)}, u32[]{:S(2)}) collective-permute-start(bf16[256,1536]{1,0:T(8,128)(2,1)} %get-tuple-element.96), channel_id=1, source_target_pairs={{0,32},{32,64},{64,96},{96,0},{1,33},{33,65},{65,97},{97,1},{2,34}... | collective-permute-start | bytes 2359304 | tf_op jit(solution)/shard_map/ppermute | solution.py:746
  268.6 48.2 %collective-permute-start.23 = (bf16[256,1536]{1,0:T(8,128)(2,1)}, bf16[256,1536]{1,0:T(8,128)(2,1)}, u32[]{:S(2)}, u32[]{:S(2)}) collective-permute-start(bf16[256,1536]{1,0:T(8,128)(2,1)} %get-tuple-element.97), channel_id=1, source_target_pairs={{0,96},{32,0},{64,32},{96,64},{1,97},{33,1},{65,33},{97,65},{2,98}... | collective-permute-start | bytes 2359304 | tf_op jit(solution)/shard_map/ppermute | solution.py:746
  317.9 7.1 %collective-permute-start.24 = (bf16[1024,1664]{1,0:T(8,128)(2,1)}, bf16[1024,1664]{1,0:T(8,128)(2,1)S(1)}, u32[]{:S(2)}, u32[]{:S(2)}) collective-permute-start(bf16[1024,1664]{1,0:T(8,128)(2,1)} %get-tuple-element.102), channel_id=1, source_target_pairs={{0,1},{1,0},{2,3},{3,2},{4,5},{5,4},{6,7},{7,6},{8,9},{9,8},{10,11... | collective-permute-start | bytes 10223624 | tf_op jit(solution)/shard_map/ppermute | solution.py:64
  329.8 21.9 %collective-permute-start.25 = (bf16[256,1664]{1,0:T(8,128)(2,1)}, bf16[256,1664]{1,0:T(8,128)(2,1)S(1)}, u32[]{:S(2)}, u32[]{:S(2)}) collective-permute-start(bf16[256,1664]{1,0:T(8,128)(2,1)} %get-tuple-element.173), channel_id=1, source_target_pairs={{0,64},{32,96},{64,0},{96,32},{1,65},{33,97},{65,1},{97,33},{2,66}... | collective-permute-start | bytes 2555912 | tf_op jit(solution)/shard_map/ppermute | solution.py:746
  331.5 39.2 %collective-permute-start.26 = (bf16[256,1664]{1,0:T(8,128)(2,1)}, bf16[256,1664]{1,0:T(8,128)(2,1)S(1)}, u32[]{:S(2)}, u32[]{:S(2)}) collective-permute-start(bf16[256,1664]{1,0:T(8,128)(2,1)} %get-tuple-element.175), channel_id=1, source_target_pairs={{0,32},{32,64},{64,96},{96,0},{1,33},{33,65},{65,97},{97,1},{2,34}... | collective-permute-start | bytes 2555912 | tf_op jit(solution)/shard_map/ppermute | solution.py:746
  331.8 39.8 %collective-permute-start.27 = (bf16[256,1664]{1,0:T(8,128)(2,1)}, bf16[256,1664]{1,0:T(8,128)(2,1)}, u32[]{:S(2)}, u32[]{:S(2)}) collective-permute-start(bf16[256,1664]{1,0:T(8,128)(2,1)} %get-tuple-element.174), channel_id=1, source_target_pairs={{0,96},{32,0},{64,32},{96,64},{1,97},{33,1},{65,33},{97,65},{2,98}... | collective-permute-start | bytes 2555912 | tf_op jit(solution)/shard_map/ppermute | solution.py:746
  351.7 19.1 %copy-start.28 = (bf16[256,1664]{1,0:T(8,128)(2,1)}, bf16[256,1664]{1,0:T(8,128)(2,1)S(1)}, u32[]{:S(2)}) copy-start(bf16[256,1664]{1,0:T(8,128)(2,1)S(1)} %collective-permute-done.25) | copy-start | bytes 2555908
  374.5 18.9 %collective-permute-start.28 = (bf16[128,1664]{1,0:T(8,128)(2,1)S(1)}, bf16[128,1664]{1,0:T(8,128)(2,1)S(1)}, u32[]{:S(2)}, u32[]{:S(2)}) collective-permute-start(bf16[128,1664]{1,0:T(8,128)(2,1)S(1)} %dynamic-slice_convert_fusion), channel_id=1, source_target_pairs={{0,16},{16,0},{1,17},{17,1},{2,18},{18,2},{3,19},{19,3},{4,20},{20... | collective-permute-start | bytes 1277960 | tf_op jit(solution)/shard_map/ppermute | solution.py:754
  402.8 17.1 %all-to-all-start.1 = ((bf16[8,128,384]{1,2,0:T(8,128)(2,1)}), bf16[8,128,384]{1,2,0:T(8,128)(2,1)}, u32[]{:S(2)}, u32[]{:S(2)}) async-start(bf16[8,128,384]{1,2,0:T(8,128)(2,1)} %pad_maximum_fusion.1), calls=%async_computation.1 | async-start | bytes 1572864 | tf_op jit(solution)/shard_map/all_to_all | solution.py:73
  446.3 14.7 %collective-permute-start.30 = (bf16[8,96,640]{2,1,0:T(8,128)(2,1)S(1)}, bf16[8,96,640]{2,1,0:T(8,128)(2,1)S(1)}, u32[]{:S(2)}, u32[]{:S(2)}) collective-permute-start(bf16[8,96,640]{2,1,0:T(8,128)(2,1)S(1)} %get-tuple-element.111), channel_id=1, source_target_pairs={{0,1},{1,0},{2,3},{3,2},{4,5},{5,4},{6,7},{7,6},{8,9},{9,8},{10,11... | collective-permute-start | bytes 2949128 | tf_op jit(solution)/shard_map/ppermute | solution.py:64
  453.4 38.7 %collective-permute-start.31 = (bf16[256,1536]{1,0:T(8,128)(2,1)}, bf16[256,1536]{1,0:T(8,128)(2,1)S(1)}, u32[]{:S(2)}, u32[]{:S(2)}) collective-permute-start(bf16[256,1536]{1,0:T(8,128)(2,1)} %get-tuple-element.181), channel_id=1, source_target_pairs={{0,64},{32,96},{64,0},{96,32},{1,65},{33,97},{65,1},{97,33},{2,66}... | collective-permute-start | bytes 2359304 | tf_op jit(solution)/shard_map/ppermute | solution.py:746
  455.4 36.7 %collective-permute-start.32 = (bf16[256,1536]{1,0:T(8,128)(2,1)}, bf16[256,1536]{1,0:T(8,128)(2,1)}, u32[]{:S(2)}, u32[]{:S(2)}) collective-permute-start(bf16[256,1536]{1,0:T(8,128)(2,1)} %get-tuple-element.180), channel_id=1, source_target_pairs={{0,32},{32,64},{64,96},{96,0},{1,33},{33,65},{65,97},{97,1},{2,34}... | collective-permute-start | bytes 2359304 | tf_op jit(solution)/shard_map/ppermute | solution.py:746
  455.6 36.5 %collective-permute-start.33 = (bf16[256,1536]{1,0:T(8,128)(2,1)}, bf16[256,1536]{1,0:T(8,128)(2,1)}, u32[]{:S(2)}, u32[]{:S(2)}) collective-permute-start(bf16[256,1536]{1,0:T(8,128)(2,1)} %get-tuple-element.179), channel_id=1, source_target_pairs={{0,96},{32,0},{64,32},{96,64},{1,97},{33,1},{65,33},{97,65},{2,98}... | collective-permute-start | bytes 2359304 | tf_op jit(solution)/shard_map/ppermute | solution.py:746
  460.9 35.9 %collective-permute-start.29 = (bf16[128,1536]{1,0:T(8,128)(2,1)}, bf16[128,1536]{1,0:T(8,128)(2,1)}, u32[]{:S(2)}, u32[]{:S(2)}) collective-permute-start(bf16[128,1536]{1,0:T(8,128)(2,1)} %dynamic-slice_convert_fusion.2), channel_id=1, source_target_pairs={{0,16},{16,0},{1,17},{17,1},{2,18},{18,2},{3,19},{19,3},{4,20},{20... | collective-permute-start | bytes 1179656 | tf_op jit(solution)/shard_map/ppermute | solution.py:754
  462.1 30.0 %all-to-all-start.2 = ((bf16[8,96,640]{2,1,0:T(8,128)(2,1)}), bf16[8,96,640]{2,1,0:T(8,128)(2,1)S(1)}, u32[]{:S(2)}, u32[]{:S(2)}) async-start(bf16[8,96,640]{2,1,0:T(8,128)(2,1)} %add_convert_fusion), calls=%async_computation.2 | async-start | bytes 1966080 | tf_op jit(solution)/shard_map/all_to_all | solution.py:73
  485.9 4.2 collective-permute-start.34
  496.9 13.1 %collective-permute-start.35 = (bf16[128,1536]{1,0:T(8,128)(2,1)}, bf16[128,1536]{1,0:T(8,128)(2,1)}, u32[]{:S(2)}, u32[]{:S(2)}) collective-permute-start(bf16[128,1536]{1,0:T(8,128)(2,1)} %dynamic-slice_convert_fusion.1), channel_id=1, source_target_pairs={{0,16},{16,0},{1,17},{17,1},{2,18},{18,2},{3,19},{19,3},{4,20},{20... | collective-permute-start | bytes 1179656 | tf_op jit(solution)/shard_map/ppermute | solution.py:754
  500.0 24.8 %all-to-all-start.3 = ((bf16[8,96,640]{2,1,0:T(8,128)(2,1)}), bf16[8,96,640]{2,1,0:T(8,128)(2,1)S(1)}, u32[]{:S(2)}, u32[]{:S(2)}) async-start(bf16[8,96,640]{2,1,0:T(8,128)(2,1)} %broadcast_in_dim.103), calls=%async_computation.4 | async-start | bytes 1966080 | tf_op jit(solution)/shard_map/all_to_all | solution.py:69
  (43 other events, 210.5 us)
Sparse Core Ops, SparseCore 0:
  37.8 151.9 all-gather.4
  214.8 37.7 all-gather.6
  316.9 166.5 reduce-scatter.1

commit v5 on v4

--- a/solution.py
+++ b/solution.py
@@ -897,10 +897,11 @@
         [router_part, gain_two_part[:, None], jnp.zeros((WIDTH, SIDE - EXPERTS - 1), F32)], axis=1
     )
     normed_grad_part = contract(grad_projected, packed, ((1,), (1,)))
-    keep, send = dense_call(c, attended_all, back, normed_one, grad_projected, packed, side)
-    parts = (keep.astype(F32) + core_swap(send).astype(F32)).astype(BF)
     normed_rows, normed_sent = sum_start(normed_grad_part.astype(BF))
     normed_arrived = sum_send(normed_sent)
+    keep, send = dense_call(c, attended_all, back, normed_one, grad_projected, packed, side)
+    keep, send, normed_arrived = lax.optimization_barrier((keep, send, normed_arrived))
+    parts = (keep.astype(F32) + core_swap(send).astype(F32)).astype(BF)
     exchanged = exchange(parts, YZ)
 
     first_rows, second_rows = shard_weights[:, :96], shard_weights[:, 96:GU_ROWS]
@@ -911,9 +912,7 @@
         [shard_weights[:, GU_ROWS + 32 * p : GU_ROWS + 32 * (p + 1)] for p in range(WIDTH // FFE)], axis=2
     ).astype(F32)
 
-    exchanged, normed_arrived, total_gu, total_down = lax.optimization_barrier(
-        (exchanged, normed_arrived, total_gu, total_down)
-    )
+    exchanged, total_gu, total_down = lax.optimization_barrier((exchanged, total_gu, total_down))
     summed = jnp.sum(exchanged.astype(F32), axis=0).astype(BF)
     totals = to_all(summed, EXP, N_EXP)
     grad_normed_one = sum_finish(normed_rows, after(normed_arrived, summed))

time: 541 us -> 545 us (level)
  blocking collectives: 0 us -> 15 us
  starting transfers between devices: 65.2 us -> 54.6 us
    ppermute x9, waiting for transfers between devices: 30.3 us -> 51 us  [sum_send(): lax.ppermute(value, 'x', rotation(4, k))]
    reduce_scatter x1, waiting for transfers between devices: 16.6 us -> 0.01 us  [body(): lax.psum_scatter(grad_weights, YZ, scatter_dimension=0, tiled=False)]
    all_to_all x0 -> x1, blocking collectives: none -> 15 us  [exchange(): return lax.all_to_all(value, axes, 0, 0, tiled=True)]
    all_to_all x2, starting transfers between devices: 14.6 us -> 8.77 us  [to_all(): return lax.all_to_all(spread, axes, 0, 0, tiled=True)]
    unnamed x99 -> x109, local copies, waits for them, and re-layouts: 18.9 us -> 16.7 us
  transfers between devices with their start and end apart: 43 -> 42, of which waited for: 16 -> 17; matrix products, arithmetic and copies ran while one was open for 18% -> 18% of each run, Pallas kernels for 24% -> 23%
where the time goes in v5:
time: 545 us; the launch traced here: 538 us
  waiting for transfers between devices  209 us (38%)
  Pallas kernels  127 us (23%)
  starting transfers between devices  54.6 us (10%)
  other arithmetic  48.6 us (9%)
  local copies, waits for them, and re-layouts  43 us (8%)
  matrix products  25.7 us (5%)
  blocking collectives  15 us (3%)
  between operations  14.8 us (3%)
    ppermute x9, waiting for transfers between devices, sum_send(): lax.ppermute(value, 'x', rotation(4, k))  51 us
    pallas_call x1, Pallas kernels, experts_backward(): pl.pallas_call(backward_kernel, grid=(2 * STEPS + EXP_DEV,), in_specs=[pl...  46.6 us
    all_to_all x2, waiting for transfers between devices, to_all(): return lax.all_to_all(spread, axes, 0, 0, tiled=True)  41.5 us
    pallas_call x1, Pallas kernels, experts_forward(): pl.pallas_call(forward_kernel, grid=(2 * STEPS + EXP_DEV,), in_specs=[pl....  40.4 us
    ppermute x9, waiting for transfers between devices, straight_four(): lax.ppermute(block, axis, rotation(4, k))  32.3 us
    ppermute x1, waiting for transfers between devices, body(): lax.ppermute(attended_low, 'zl', SWAP)  23.5 us
    ppermute x3, waiting for transfers between devices, sum_finish(): return keep + lax.ppermute(send, 'zl', SWAP).astype(F32)  19.1 us
    unnamed x109, local copies, waits for them, and re-layouts  16.7 us
  transfers between devices with their start and end apart: 42, of which 17 were waited for; matrix products, arithmetic and copies ran while one was open for 18% of the time, Pallas kernels for 23%

profile of v5, /device:TPU:1, one launch (start us, length us, event | category | flops | bytes accessed | tf_op | source)
XLA Modules:
  0.0 538.1 jit_solution(297976821865417283)
XLA Ops:
  16.9 2.2 collective-permute-start.4
  21.9 10.9 %collective-permute-done.3 = bf16[2,96,384]{2,1,0:T(8,128)(2,1)S(1)} collective-permute-done((bf16[2,96,384]{2,1,0:T(8,128)(2,1)S(1)}, bf16[2,96,384]{2,1,0:T(8,128)(2,1)S(1)}, u32[]{:S(2)}, u32[]{:S(2)}) %collective-permute-start.3) | collective-permute-done | bytes 147488 | tf_op jit(solution)/shard_map/ppermute | solution.py:791
  37.6 2.5 collective-permute-start.5
  44.0 4.9 collective-permute-done.10
  51.0 5.6 %fusion.8 = (f32[1024,256]{1,0:T(8,128)}, f32[1024,256]{1,0:T(8,128)}) fusion(f32[256]{0:T(256)S(1)} %get-tuple-element.207, f32[256]{0:T(256)S(1)} %get-tuple-element.208, f32[1024]{0:T(1024)S(1)} %iota_convert_fusion), kind=kLoop, calls=%fused_computation.33 | loop fusion | flops 524288 | bytes 2103296 | tf_op jit(solution)/shard_map/mul | solution.py:821
  56.6 7.8 %collective-permute-done.9 = bf16[2,2,96,384]{3,2,1,0:T(8,128)(2,1)} collective-permute-done((bf16[2,2,96,384]{3,2,1,0:T(8,128)(2,1)S(1)}, bf16[2,2,96,384]{3,2,1,0:T(8,128)(2,1)}, u32[]{:S(2)}, u32[]{:S(2)}) %collective-permute-start.9) | collective-permute-done | bytes 294944 | tf_op jit(solution)/shard_map/ppermute | solution.py:723
  65.3 15.6 %collective-permute-done.7.block_3 = bf16[256,1664]{1,0:T(8,128)(2,1)} collective-permute-done((bf16[256,1664]{1,0:T(8,128)(2,1)S(1)}, bf16[256,1664]{1,0:T(8,128)(2,1)}, u32[]{:S(2)}, u32[]{:S(2)}) %collective-permute-start.7) | collective-permute-done | bytes 852000 | tf_op jit(solution)/shard_map/ppermute | solution.py:723
  84.3 14.1 %attend.1 = (bf16[1024,1664]{1,0:T(8,128)(2,1)}, bf16[1024,1536]{1,0:T(8,128)(2,1)}, bf16[1024,384]{1,0:T(8,128)(2,1)S(1)}, f32[1024,192]{1,0:T(8,128)}, bf16[10...) custom-call(s32[1]{0:T(128)} %bitcast.place_ref, bf16[256,1664]{1,0:T(8,128)(2,1)S(1)} %bitcast.102, ...), custom_call_target="tpu_custom_call" | custom-call | flops 12999999488 | bytes 12000000 | tf_op jit(solution)/shard_map/attend/pallas_call | solution.py:507
  101.7 2.8 collective-permute-start.13
  107.1 23.5 %collective-permute-done.11 = bf16[1024,192]{1,0:T(8,128)(2,1)S(1)} collective-permute-done((bf16[1024,192]{1,0:T(8,128)(2,1)}, bf16[1024,192]{1,0:T(8,128)(2,1)S(1)}, u32[]{:S(2)}, u32[]{:S(2)}) %collective-permute-start.11) | collective-permute-done | bytes 393248 | tf_op jit(solution)/shard_map/ppermute | solution.py:829
  130.6 2.6 maximum_select_fusion
  134.0 3.9 collective-permute-done.15.piece_3
  145.5 4.7 all-to-all-start
  150.2 4.1 both_cores.1
  154.3 33.5 %all-to-all-done = bf16[4,2,1024,192]{2,3,1,0:T(8,128)(2,1)} async-done(((bf16[4,2,1024,192]{2,3,1,0:T(8,128)(2,1)}), bf16[4,2,1024,192]{2,3,1,0:T(8,128)(2,1)}, u32[]{:S(2)}, u32[]{:S(2)}) %all-to-all-start) | async-done | bytes 3145760 | tf_op jit(solution)/shard_map/all_to_all | solution.py:69
  187.8 9.3 %multiply_reduce_fusion = (f32[1024]{0:T(1024)S(1)}, f32[1024,1536]{1,0:T(8,128)S(1)}) fusion(bf16[8,1024,192]{1,2,0:T(8,128)(2,1)} %bitcast.30, bf16[8,192,1536]{2,1,0:T(8,128)(2,1)} %bitcast.106, bf16[1024,1664]{1,0:T(8,128)(2,1)} %get-tuple-element.79), kind=kOutput, calls=%fused_computation.2 | convolution fusion | flops 4838128640 | bytes 17305600 | tf_op jit(solution)/shard_map/etk,ekn->tn/dot_general | solution.py:60
  197.2 2.6 copy-done.21
  199.8 2.2 multiply_convert_fusion.n_own
  202.9 10.7 %collective-permute-done.19 = bf16[128,1536]{1,0:T(8,128)(2,1)S(1)} collective-permute-done((bf16[128,1536]{1,0:T(8,128)(2,1)S(1)}, bf16[128,1536]{1,0:T(8,128)(2,1)S(1)}, u32[]{:S(2)}, u32[]{:S(2)}) %collective-permute-start.19) | collective-permute-done | bytes 393248 | tf_op jit(solution)/shard_map/ppermute | solution.py:840
  216.2 40.4 %experts_forward.1 = (bf16[1024,1536]{1,0:T(8,128)(2,1)}, bf16[1024,1536]{1,0:T(8,128)(2,1)}, bf16[5,768,1536]{2,1,0:T(8,128)(2,1)}, bf16[5,768,640]{2,1,0:T(8,128)(2,1)}) custom-call(bf16[1024,1536]{1,0:T(8,128)(2,1)} %multiply_convert_fusion.n_own, bf16[1024,1536]{1,0:T(8,128)(2,1)} %collective-permute-done.17.n_par, bf16[2048,128]{1,0:T(8,128)(2,1)} %fusion.9.routes, ...), custom_call_target="tpu_custom_call" | custom-call | flops 40000000000 | bytes 40000000 | tf_op jit(solution)/shard_map/experts_forward/pallas_call | solution.py:372
  257.7 5.3 collective-permute-done.18
  263.0 4.0 add_convert_fusion.4
  270.0 46.6 %experts_backward.1 = (bf16[1024,1664]{1,0:T(8,128)(2,1)}, bf16[1024,1664]{1,0:T(8,128)(2,1)}, bf16[8,5,288,512]{3,2,1,0:T(8,128)(2,1)}) custom-call(s32[1]{0:T(128)} %bitcast.38.place_ref, bf16[1024,1536]{1,0:T(8,128)(2,1)} %bitcast.133, bf16[1024,1536]{1,0:T(8,128)(2,1)} %collective-permute-done.20.g_par, bf16[2048,128]{1,0:T(8,128)(2,1)} %fusion.9.routes, ...), custom_call_target="tpu_custom_call" | custom-call | flops 49999998976 | bytes 60000000 | tf_op jit(solution)/shard_map/experts_backward/pallas_call | solution.py:400
  319.1 5.9 %collective-permute-done.24 = bf16[1024,1664]{1,0:T(8,128)(2,1)S(1)} collective-permute-done((bf16[1024,1664]{1,0:T(8,128)(2,1)}, bf16[1024,1664]{1,0:T(8,128)(2,1)S(1)}, u32[]{:S(2)}, u32[]{:S(2)}) %collective-permute-start.24) | collective-permute-done | bytes 3407904 | tf_op jit(solution)/shard_map/ppermute | solution.py:64
  324.9 4.8 add_convert_fusion.3
  331.7 2.4 collective-permute-start.27
  334.3 17.3 %collective-permute-done.25 = bf16[256,1664]{1,0:T(8,128)(2,1)S(1)} collective-permute-done((bf16[256,1664]{1,0:T(8,128)(2,1)}, bf16[256,1664]{1,0:T(8,128)(2,1)S(1)}, u32[]{:S(2)}, u32[]{:S(2)}) %collective-permute-start.25) | collective-permute-done | bytes 852000 | tf_op jit(solution)/shard_map/ppermute | solution.py:746
  351.6 19.0 %collective-permute-done.26 = bf16[256,1664]{1,0:T(8,128)(2,1)S(1)} collective-permute-done((bf16[256,1664]{1,0:T(8,128)(2,1)}, bf16[256,1664]{1,0:T(8,128)(2,1)S(1)}, u32[]{:S(2)}, u32[]{:S(2)}) %collective-permute-start.26) | collective-permute-done | bytes 852000 | tf_op jit(solution)/shard_map/ppermute | solution.py:746
  371.5 2.8 add_add_fusion
  376.4 16.9 %collective-permute-done.28 = bf16[128,1664]{1,0:T(8,128)(2,1)S(1)} collective-permute-done((bf16[128,1664]{1,0:T(8,128)(2,1)S(1)}, bf16[128,1664]{1,0:T(8,128)(2,1)S(1)}, u32[]{:S(2)}, u32[]{:S(2)}) %collective-permute-start.28) | collective-permute-done | bytes 426016 | tf_op jit(solution)/shard_map/ppermute | solution.py:754
  393.9 2.3 multiply_reduce_fusion.1
  396.1 2.3 fusion.53
  398.7 3.7 fusion.7
  402.5 15.0 %all_to_all.20 = bf16[8,128,384]{1,2,0:T(8,128)(2,1)} all-to-all(bf16[8,128,384]{1,2,0:T(8,128)(2,1)S(1)} %pad_maximum_fusion.1), channel_id=1, replica_groups=mesh['x'=4,'zl'=2,'y'=4,'zh'=2,'c'=2] {'x','zl'}, dimensions={0} | all-to-all | bytes 1572864 | tf_op jit(solution)/shard_map/all_to_all | solution.py:73
  422.4 10.7 %attend_back.1.grad_projected = bf16[1024,384]{1,0:T(8,128)(2,1)S(1)} custom-call(bf16[1024,384]{1,0:T(8,128)(2,1)S(1)} %bitcast.97, bf16[1024,384]{1,0:T(8,128)(2,1)S(1)} %copy-done.18, f32[1024,192]{1,0:T(8,128)S(1)} %copy-done.16, f32[1024,8]{1,0:T(8,128)S(1)} %copy-done.20, bf16[1024,384]{1,0:T(8,128)(2,1)S(1)} %copy-done.18, f32[1024,256]{1,0:T(8,128)S(1)} %copy-done.4, ...), custom_call_target="tpu_custom_call" | custom-call | flops 11000000512 | bytes 8000000 | tf_op jit(solution)/shard_map/attend_back/pallas_call | solution.py:601
  437.3 4.2 collective-permute-start.30
  442.1 2.3 collective-permute-start.32
  444.5 6.1 %copy.68 = bf16[4,2,1024,192]{3,2,1,0:T(8,128)(2,1)} copy(bf16[4,2,1024,192]{2,3,1,0:T(8,128)(2,1)} %all-to-all-done) | data formatting | bytes 6291456 | tf_op jit(solution)/shard_map/all_to_all | solution.py:69
  452.5 9.5 %dense.1 = (bf16[8,96,640]{2,1,0:T(8,128)(2,1)S(1)}, bf16[8,96,640]{2,1,0:T(8,128)(2,1)S(1)}) custom-call(s32[1]{0:T(128)} %bitcast.31.core, bf16[8,1024,192]{2,1,0:T(8,128)(2,1)} %bitcast.105, bf16[1024,384]{1,0:T(8,128)(2,1)S(1)} %bitcast.98, bf16[1024,1536]{1,0:T(8,128)(2,1)} %get-tuple-element.111.normed, bf16[1024,384]{1,0:T(8,128)(2,1)S(1)} %copy-done.6, ...), custom_call_target="tpu_custom_call" | custom-call | tf_op jit(solution)/shard_map/dense/pallas_call | solution.py:707
  462.1 14.6 %collective-permute-done.31 = bf16[256,1536]{1,0:T(8,128)(2,1)S(1)} collective-permute-done((bf16[256,1536]{1,0:T(8,128)(2,1)}, bf16[256,1536]{1,0:T(8,128)(2,1)S(1)}, u32[]{:S(2)}, u32[]{:S(2)}) %collective-permute-start.31) | collective-permute-done | bytes 786464 | tf_op jit(solution)/shard_map/ppermute | solution.py:746
  482.1 4.8 all-to-all-start.2
  493.8 9.3 %all-to-all-done.2 = bf16[8,96,640]{2,1,0:T(8,128)(2,1)S(1)} async-done(((bf16[8,96,640]{2,1,0:T(8,128)(2,1)}), bf16[8,96,640]{2,1,0:T(8,128)(2,1)S(1)}, u32[]{:S(2)}, u32[]{:S(2)}) %all-to-all-start.2) | async-done | bytes 983072 | tf_op jit(solution)/shard_map/all_to_all | solution.py:73
  503.9 2.2 add_add_fusion.1
  507.6 2.1 fusion.23
  510.8 4.1 all-to-all-start.3
  514.9 2.1 collective-permute-done.35
  518.4 2.3 fusion.24
  520.7 8.0 %all-to-all-done.3.totals = bf16[8,96,640]{2,1,0:T(8,128)(2,1)S(1)} async-done(((bf16[8,96,640]{2,1,0:T(8,128)(2,1)}), bf16[8,96,640]{2,1,0:T(8,128)(2,1)S(1)}, u32[]{:S(2)}, u32[]{:S(2)}) %all-to-all-start.3) | async-done | bytes 983072 | tf_op jit(solution)/shard_map/all_to_all | solution.py:69
  (246 shorter events, 88.2 us)
Async XLA Ops:
  7.2 207.4 %all-gather.5.cloned.1.call-start = ((), (), s32[]{:S(2)}) async-start(), calls=%async_computation.6 | async-start | bytes 13271040 | tf_op jit(solution)/shard_map/all_gather | solution.py:800
  11.7 8.9 %collective-permute-start.2 = (bf16[96,384]{1,0:T(8,128)(2,1)S(1)}, bf16[96,384]{1,0:T(8,128)(2,1)S(1)}, u32[]{:S(2)}, u32[]{:S(2)}) collective-permute-start(bf16[96,384]{1,0:T(8,128)(2,1)S(1)} %concatenate.40), channel_id=1, source_target_pairs={{0,1},{1,0},{2,3},{3,2},{4,5},{5,4},{6,7},{7,6},{8,9},{9,8},{10,11... | collective-permute-start | bytes 221192 | tf_op jit(solution)/shard_map/ppermute | solution.py:64
  14.8 20.2 %collective-permute-start = (bf16[5,96,512]{2,1,0:T(8,128)(2,1)}, bf16[5,96,512]{2,1,0:T(8,128)(2,1)}, u32[]{:S(2)}, u32[]{:S(2)}) collective-permute-start(bf16[5,96,512]{2,1,0:T(8,128)(2,1)} %bitcast.5), channel_id=1, source_target_pairs={{0,1},{1,0},{2,3},{3,2},{4,5},{5,4},{6,7},{7,6},{8,9},{9,8},{10,11... | collective-permute-start | bytes 1474568 | tf_op jit(solution)/shard_map/ppermute | solution.py:64
  15.1 17.8 %collective-permute-start.1 = (bf16[128,1664]{1,0:T(8,128)(2,1)S(1)}, bf16[128,1664]{1,0:T(8,128)(2,1)S(1)}, u32[]{:S(2)}, u32[]{:S(2)}) collective-permute-start(bf16[128,1664]{1,0:T(8,128)(2,1)S(1)} %concatenate.39), channel_id=1, source_target_pairs={{0,16},{16,0},{1,17},{17,1},{2,18},{18,2},{3,19},{19,3},{4,20},{20... | collective-permute-start | bytes 1277960 | tf_op jit(solution)/shard_map/ppermute | solution.py:796
  16.9 20.7 %collective-permute-start.4 = (bf16[96,1536]{1,0:T(8,128)(2,1)}, bf16[96,1536]{1,0:T(8,128)(2,1)}, u32[]{:S(2)}, u32[]{:S(2)}) collective-permute-start(bf16[96,1536]{1,0:T(8,128)(2,1)} %param.16), channel_id=1, source_target_pairs={{0,18},{2,16},{16,2},{18,0},{1,19},{3,17},{17,3},{19,1},{4,22},{6,... | collective-permute-start | bytes 884744 | tf_op jit(solution)/shard_map/ppermute | solution.py:797
  20.7 12.1 %collective-permute-start.3 = (bf16[2,96,384]{2,1,0:T(8,128)(2,1)S(1)}, bf16[2,96,384]{2,1,0:T(8,128)(2,1)S(1)}, u32[]{:S(2)}, u32[]{:S(2)}) collective-permute-start(bf16[2,96,384]{2,1,0:T(8,128)(2,1)S(1)} %maximum_select_fusion.7), channel_id=1, source_target_pairs={{0,2},{2,0},{1,3},{3,1},{4,6},{6,4},{5,7},{7,5},{8,10},{10,8},{9,1... | collective-permute-start | bytes 442376 | tf_op jit(solution)/shard_map/ppermute | solution.py:791
  37.6 26.8 %collective-permute-start.5 = (bf16[256,1664]{1,0:T(8,128)(2,1)S(1)}, bf16[256,1664]{1,0:T(8,128)(2,1)S(1)}, u32[]{:S(2)}, u32[]{:S(2)}) collective-permute-start(bf16[256,1664]{1,0:T(8,128)(2,1)S(1)} %bitcast.99), channel_id=1, source_target_pairs={{0,96},{32,0},{64,32},{96,64},{1,97},{33,1},{65,33},{97,65},{2,98}... | collective-permute-start | bytes 2555912 | tf_op jit(solution)/shard_map/ppermute | solution.py:723
  40.2 24.2 %collective-permute-start.6 = (bf16[256,1664]{1,0:T(8,128)(2,1)S(1)}, bf16[256,1664]{1,0:T(8,128)(2,1)S(1)}, u32[]{:S(2)}, u32[]{:S(2)}) collective-permute-start(bf16[256,1664]{1,0:T(8,128)(2,1)S(1)} %bitcast.100), channel_id=1, source_target_pairs={{0,64},{32,96},{64,0},{96,32},{1,65},{33,97},{65,1},{97,33},{2,66}... | collective-permute-start | bytes 2555912 | tf_op jit(solution)/shard_map/ppermute | solution.py:723
  40.7 40.2 %collective-permute-start.7 = (bf16[256,1664]{1,0:T(8,128)(2,1)S(1)}, bf16[256,1664]{1,0:T(8,128)(2,1)}, u32[]{:S(2)}, u32[]{:S(2)}) collective-permute-start(bf16[256,1664]{1,0:T(8,128)(2,1)S(1)} %bitcast.101), channel_id=1, source_target_pairs={{0,32},{32,64},{64,96},{96,0},{1,33},{33,65},{65,97},{97,1},{2,34}... | collective-permute-start | bytes 2555912 | tf_op jit(solution)/shard_map/ppermute | solution.py:723
  41.3 7.7 %collective-permute-start.10 = (bf16[2,2,96,384]{3,2,1,0:T(8,128)(2,1)S(1)}, bf16[2,2,96,384]{3,2,1,0:T(8,128)(2,1)S(1)}, u32[]{:S(2)}, u32[]{:S(2)}) collective-permute-start(bf16[2,2,96,384]{3,2,1,0:T(8,128)(2,1)S(1)} %maximum_select_fusion.5), channel_id=1, source_target_pairs={{0,4},{4,8},{8,12},{12,0},{1,5},{5,9},{9,13},{13,1},{2,6},{6,10},{... | collective-permute-start | bytes 884744 | tf_op jit(solution)/shard_map/ppermute | solution.py:723
  42.6 14.0 %collective-permute-start.8 = (bf16[2,2,96,384]{3,2,1,0:T(8,128)(2,1)S(1)}, bf16[2,2,96,384]{3,2,1,0:T(8,128)(2,1)}, u32[]{:S(2)}, u32[]{:S(2)}) collective-permute-start(bf16[2,2,96,384]{3,2,1,0:T(8,128)(2,1)S(1)} %maximum_select_fusion.5), channel_id=1, source_target_pairs={{0,12},{4,0},{8,4},{12,8},{1,13},{5,1},{9,5},{13,9},{2,14},{6,2},{... | collective-permute-start | bytes 884744 | tf_op jit(solution)/shard_map/ppermute | solution.py:723
  49.0 15.4 %collective-permute-start.9 = (bf16[2,2,96,384]{3,2,1,0:T(8,128)(2,1)S(1)}, bf16[2,2,96,384]{3,2,1,0:T(8,128)(2,1)}, u32[]{:S(2)}, u32[]{:S(2)}) collective-permute-start(bf16[2,2,96,384]{3,2,1,0:T(8,128)(2,1)S(1)} %maximum_select_fusion.5), channel_id=1, source_target_pairs={{0,8},{4,12},{8,0},{12,4},{1,9},{5,13},{9,1},{13,5},{2,10},{6,14},... | collective-permute-start | bytes 884744 | tf_op jit(solution)/shard_map/ppermute | solution.py:723
  50.9 32.9 %copy-start.11 = (s32[1024,1]{1,0:T(8,128)}, s32[1024,1]{1,0:T(8,128)S(1)}, u32[]{:S(2)}) copy-start(s32[1024,1]{1,0:T(8,128)S(1)} %copy.66.seg_rows) | copy-start | bytes 12292
  51.0 30.0 %copy-start.29 = (bf16[2,2,96,384]{3,2,1,0:T(8,128)(2,1)S(1)}, bf16[2,2,96,384]{3,2,1,0:T(8,128)(2,1)}, u32[]{:S(2)}) copy-start(bf16[2,2,96,384]{3,2,1,0:T(8,128)(2,1)} %copy-done.28) | copy-start | bytes 884740
  56.6 26.6 %copy-start.44 = (bf16[2,2,96,384]{3,2,1,0:T(8,128)(2,1)S(1)}, bf16[2,2,96,384]{3,2,1,0:T(8,128)(2,1)}, u32[]{:S(2)}) copy-start(bf16[2,2,96,384]{3,2,1,0:T(8,128)(2,1)} %copy-done.43) | copy-start | bytes 884740
  99.7 5.9 %collective-permute-start.12 = (bf16[1024,128]{1,0:T(8,128)(2,1)S(1)}, bf16[1024,128]{1,0:T(8,128)(2,1)S(1)}, u32[]{:S(2)}, u32[]{:S(2)}) collective-permute-start(bf16[1024,128]{1,0:T(8,128)(2,1)S(1)} %slice.69), channel_id=1, source_target_pairs={{0,1},{1,0},{2,3},{3,2},{4,5},{5,4},{6,7},{7,6},{8,9},{9,8},{10,11... | collective-permute-start | bytes 786440 | tf_op jit(solution)/shard_map/ppermute | solution.py:64
  101.7 31.5 %collective-permute-start.13 = (bf16[2,96,1536]{2,1,0:T(8,128)(2,1)S(1)}, bf16[2,96,1536]{2,1,0:T(8,128)(2,1)S(1)}, u32[]{:S(2)}, u32[]{:S(2)}) collective-permute-start(bf16[2,96,1536]{2,1,0:T(8,128)(2,1)S(1)} %maximum_select_fusion.4.piece_0), channel_id=1, source_target_pairs={{0,12},{4,0},{8,4},{12,8},{1,13},{5,1},{9,5},{13,9},{2,14},{6,2},{... | collective-permute-start | bytes 1769480 | tf_op jit(solution)/shard_map/ppermute | solution.py:723
  104.5 28.7 %collective-permute-start.14 = (bf16[2,96,1536]{2,1,0:T(8,128)(2,1)S(1)}, bf16[2,96,1536]{2,1,0:T(8,128)(2,1)S(1)}, u32[]{:S(2)}, u32[]{:S(2)}) collective-permute-start(bf16[2,96,1536]{2,1,0:T(8,128)(2,1)S(1)} %maximum_select_fusion.4.piece_0), channel_id=1, source_target_pairs={{0,8},{4,12},{8,0},{12,4},{1,9},{5,13},{9,1},{13,5},{2,10},{6,14},... | collective-permute-start | bytes 1769480 | tf_op jit(solution)/shard_map/ppermute | solution.py:723
  104.8 33.1 %collective-permute-start.15 = (bf16[2,96,1536]{2,1,0:T(8,128)(2,1)S(1)}, bf16[2,96,1536]{2,1,0:T(8,128)(2,1)S(1)}, u32[]{:S(2)}, u32[]{:S(2)}) collective-permute-start(bf16[2,96,1536]{2,1,0:T(8,128)(2,1)S(1)} %maximum_select_fusion.4.piece_0), channel_id=1, source_target_pairs={{0,4},{4,8},{8,12},{12,0},{1,5},{5,9},{9,13},{13,1},{2,6},{6,10},{... | collective-permute-start | bytes 1769480 | tf_op jit(solution)/shard_map/ppermute | solution.py:723
  105.5 25.0 %collective-permute-start.11 = (bf16[1024,192]{1,0:T(8,128)(2,1)}, bf16[1024,192]{1,0:T(8,128)(2,1)S(1)}, u32[]{:S(2)}, u32[]{:S(2)}) collective-permute-start(bf16[1024,192]{1,0:T(8,128)(2,1)} %get-tuple-element.80), channel_id=1, source_target_pairs={{0,16},{16,0},{1,17},{17,1},{2,18},{18,2},{3,19},{19,3},{4,20},{20... | collective-permute-start | bytes 1179656 | tf_op jit(solution)/shard_map/ppermute | solution.py:829
  141.1 9.2 %collective-permute-start.16 = (bf16[4,2,96,1536]{3,2,1,0:T(8,128)(2,1)S(1)}, bf16[4,2,96,1536]{3,2,1,0:T(8,128)(2,1)}, u32[]{:S(2)}, u32[]{:S(2)}) collective-permute-start(bf16[4,2,96,1536]{3,2,1,0:T(8,128)(2,1)S(1)} %line_up.1.mine), channel_id=1, source_target_pairs={{0,1},{1,0},{2,3},{3,2},{4,5},{5,4},{6,7},{7,6},{8,9},{9,8},{10,11... | collective-permute-start | bytes 7077896 | tf_op jit(solution)/shard_map/ppermute | solution.py:64
  145.5 42.3 %all-to-all-start = ((bf16[4,2,1024,192]{2,3,1,0:T(8,128)(2,1)}), bf16[4,2,1024,192]{2,3,1,0:T(8,128)(2,1)}, u32[]{:S(2)}, u32[]{:S(2)}) async-start(bf16[4,2,1024,192]{2,3,1,0:T(8,128)(2,1)} %broadcast_in_dim.96), calls=%async_computation | async-start | bytes 6291456 | tf_op jit(solution)/shard_map/all_to_all | solution.py:69
  150.2 107.2 %all-gather.7.cloned.1.call-start = ((), (), s32[]{:S(2)}) async-start(), calls=%async_computation.7 | async-start | bytes 3932160 | tf_op jit(solution)/shard_map/all_gather | solution.py:842
  202.0 14.2 %collective-permute-start.17 = (bf16[1024,1536]{1,0:T(8,128)(2,1)}, bf16[1024,1536]{1,0:T(8,128)(2,1)}, u32[]{:S(2)}, u32[]{:S(2)}) collective-permute-start(bf16[1024,1536]{1,0:T(8,128)(2,1)} %multiply_convert_fusion.n_own), channel_id=1, source_target_pairs={{0,1},{1,0},{2,3},{3,2},{4,5},{5,4},{6,7},{7,6},{8,9},{9,8},{10,11... | collective-permute-start | bytes 9437192 | tf_op jit(solution)/shard_map/ppermute | solution.py:64
  202.9 10.7 %collective-permute-start.19 = (bf16[128,1536]{1,0:T(8,128)(2,1)S(1)}, bf16[128,1536]{1,0:T(8,128)(2,1)S(1)}, u32[]{:S(2)}, u32[]{:S(2)}) collective-permute-start(bf16[128,1536]{1,0:T(8,128)(2,1)S(1)} %bitcast.113), channel_id=1, source_target_pairs={{0,16},{16,0},{1,17},{17,1},{2,18},{18,2},{3,19},{19,3},{4,20},{20... | collective-permute-start | bytes 1179656 | tf_op jit(solution)/shard_map/ppermute | solution.py:840
  214.7 272.3 %reduce-scatter.2.cloned.1.call-start = ((), (), s32[]{:S(2)}) async-start(), calls=%async_computation.5 | async-start | bytes 13271040 | tf_op jit(solution)/shard_map/reduce_scatter | solution.py:861
  256.5 6.5 %collective-permute-start.18 = (bf16[1024,1536]{1,0:T(8,128)(2,1)}, bf16[1024,1536]{1,0:T(8,128)(2,1)}, u32[]{:S(2)}, u32[]{:S(2)}) collective-permute-start(bf16[1024,1536]{1,0:T(8,128)(2,1)} %get-tuple-element.90), channel_id=1, source_target_pairs={{0,1},{1,0},{2,3},{3,2},{4,5},{5,4},{6,7},{7,6},{8,9},{9,8},{10,11... | collective-permute-start | bytes 9437192 | tf_op jit(solution)/shard_map/ppermute | solution.py:64
  257.4 12.6 %collective-permute-start.20 = (bf16[1024,1536]{1,0:T(8,128)(2,1)}, bf16[1024,1536]{1,0:T(8,128)(2,1)}, u32[]{:S(2)}, u32[]{:S(2)}) collective-permute-start(bf16[1024,1536]{1,0:T(8,128)(2,1)} %bitcast.132), channel_id=1, source_target_pairs={{0,1},{1,0},{2,3},{3,2},{4,5},{5,4},{6,7},{7,6},{8,9},{9,8},{10,11... | collective-permute-start | bytes 9437192 | tf_op jit(solution)/shard_map/ppermute | solution.py:64
  267.0 49.6 %collective-permute-start.21 = (bf16[256,1536]{1,0:T(8,128)(2,1)}, bf16[256,1536]{1,0:T(8,128)(2,1)S(1)}, u32[]{:S(2)}, u32[]{:S(2)}) collective-permute-start(bf16[256,1536]{1,0:T(8,128)(2,1)} %get-tuple-element.97), channel_id=1, source_target_pairs={{0,64},{32,96},{64,0},{96,32},{1,65},{33,97},{65,1},{97,33},{2,66}... | collective-permute-start | bytes 2359304 | tf_op jit(solution)/shard_map/ppermute | solution.py:746
  267.3 49.3 %collective-permute-start.22 = (bf16[256,1536]{1,0:T(8,128)(2,1)}, bf16[256,1536]{1,0:T(8,128)(2,1)S(1)}, u32[]{:S(2)}, u32[]{:S(2)}) collective-permute-start(bf16[256,1536]{1,0:T(8,128)(2,1)} %get-tuple-element.98), channel_id=1, source_target_pairs={{0,32},{32,64},{64,96},{96,0},{1,33},{33,65},{65,97},{97,1},{2,34}... | collective-permute-start | bytes 2359304 | tf_op jit(solution)/shard_map/ppermute | solution.py:746
  268.5 48.2 %collective-permute-start.23 = (bf16[256,1536]{1,0:T(8,128)(2,1)}, bf16[256,1536]{1,0:T(8,128)(2,1)}, u32[]{:S(2)}, u32[]{:S(2)}) collective-permute-start(bf16[256,1536]{1,0:T(8,128)(2,1)} %get-tuple-element.99), channel_id=1, source_target_pairs={{0,96},{32,0},{64,32},{96,64},{1,97},{33,1},{65,33},{97,65},{2,98}... | collective-permute-start | bytes 2359304 | tf_op jit(solution)/shard_map/ppermute | solution.py:746
  317.8 7.1 %collective-permute-start.24 = (bf16[1024,1664]{1,0:T(8,128)(2,1)}, bf16[1024,1664]{1,0:T(8,128)(2,1)S(1)}, u32[]{:S(2)}, u32[]{:S(2)}) collective-permute-start(bf16[1024,1664]{1,0:T(8,128)(2,1)} %get-tuple-element.104), channel_id=1, source_target_pairs={{0,1},{1,0},{2,3},{3,2},{4,5},{5,4},{6,7},{7,6},{8,9},{9,8},{10,11... | collective-permute-start | bytes 10223624 | tf_op jit(solution)/shard_map/ppermute | solution.py:64
  329.7 21.9 %collective-permute-start.25 = (bf16[256,1664]{1,0:T(8,128)(2,1)}, bf16[256,1664]{1,0:T(8,128)(2,1)S(1)}, u32[]{:S(2)}, u32[]{:S(2)}) collective-permute-start(bf16[256,1664]{1,0:T(8,128)(2,1)} %get-tuple-element.177), channel_id=1, source_target_pairs={{0,64},{32,96},{64,0},{96,32},{1,65},{33,97},{65,1},{97,33},{2,66}... | collective-permute-start | bytes 2555912 | tf_op jit(solution)/shard_map/ppermute | solution.py:746
  331.4 39.2 %collective-permute-start.26 = (bf16[256,1664]{1,0:T(8,128)(2,1)}, bf16[256,1664]{1,0:T(8,128)(2,1)S(1)}, u32[]{:S(2)}, u32[]{:S(2)}) collective-permute-start(bf16[256,1664]{1,0:T(8,128)(2,1)} %get-tuple-element.179), channel_id=1, source_target_pairs={{0,32},{32,64},{64,96},{96,0},{1,33},{33,65},{65,97},{97,1},{2,34}... | collective-permute-start | bytes 2555912 | tf_op jit(solution)/shard_map/ppermute | solution.py:746
  331.7 39.8 %collective-permute-start.27 = (bf16[256,1664]{1,0:T(8,128)(2,1)}, bf16[256,1664]{1,0:T(8,128)(2,1)}, u32[]{:S(2)}, u32[]{:S(2)}) collective-permute-start(bf16[256,1664]{1,0:T(8,128)(2,1)} %get-tuple-element.178), channel_id=1, source_target_pairs={{0,96},{32,0},{64,32},{96,64},{1,97},{33,1},{65,33},{97,65},{2,98}... | collective-permute-start | bytes 2555912 | tf_op jit(solution)/shard_map/ppermute | solution.py:746
  351.6 19.0 %copy-start.30 = (bf16[256,1664]{1,0:T(8,128)(2,1)}, bf16[256,1664]{1,0:T(8,128)(2,1)S(1)}, u32[]{:S(2)}) copy-start(bf16[256,1664]{1,0:T(8,128)(2,1)S(1)} %collective-permute-done.25) | copy-start | bytes 2555908
  374.4 19.0 %collective-permute-start.28 = (bf16[128,1664]{1,0:T(8,128)(2,1)S(1)}, bf16[128,1664]{1,0:T(8,128)(2,1)S(1)}, u32[]{:S(2)}, u32[]{:S(2)}) collective-permute-start(bf16[128,1664]{1,0:T(8,128)(2,1)S(1)} %dynamic-slice_convert_fusion), channel_id=1, source_target_pairs={{0,16},{16,0},{1,17},{17,1},{2,18},{18,2},{3,19},{19,3},{4,20},{20... | collective-permute-start | bytes 1277960 | tf_op jit(solution)/shard_map/ppermute | solution.py:754
  437.3 24.8 %collective-permute-start.30 = (bf16[256,1536]{1,0:T(8,128)(2,1)}, bf16[256,1536]{1,0:T(8,128)(2,1)S(1)}, u32[]{:S(2)}, u32[]{:S(2)}) collective-permute-start(bf16[256,1536]{1,0:T(8,128)(2,1)} %get-tuple-element.185), channel_id=1, source_target_pairs={{0,64},{32,96},{64,0},{96,32},{1,65},{33,97},{65,1},{97,33},{2,66}... | collective-permute-start | bytes 2359304 | tf_op jit(solution)/shard_map/ppermute | solution.py:746
  441.6 35.2 %collective-permute-start.31 = (bf16[256,1536]{1,0:T(8,128)(2,1)}, bf16[256,1536]{1,0:T(8,128)(2,1)S(1)}, u32[]{:S(2)}, u32[]{:S(2)}) collective-permute-start(bf16[256,1536]{1,0:T(8,128)(2,1)} %get-tuple-element.184), channel_id=1, source_target_pairs={{0,32},{32,64},{64,96},{96,0},{1,33},{33,65},{65,97},{97,1},{2,34}... | collective-permute-start | bytes 2359304 | tf_op jit(solution)/shard_map/ppermute | solution.py:746
  442.1 34.6 %collective-permute-start.32 = (bf16[256,1536]{1,0:T(8,128)(2,1)}, bf16[256,1536]{1,0:T(8,128)(2,1)}, u32[]{:S(2)}, u32[]{:S(2)}) collective-permute-start(bf16[256,1536]{1,0:T(8,128)(2,1)} %get-tuple-element.183), channel_id=1, source_target_pairs={{0,96},{32,0},{64,32},{96,64},{1,97},{33,1},{65,33},{97,65},{2,98}... | collective-permute-start | bytes 2359304 | tf_op jit(solution)/shard_map/ppermute | solution.py:746
  452.5 25.3 %copy-start.35 = (bf16[256,1536]{1,0:T(8,128)(2,1)S(1)}, bf16[256,1536]{1,0:T(8,128)(2,1)}, u32[]{:S(2)}) copy-start(bf16[256,1536]{1,0:T(8,128)(2,1)} %copy-done.34) | copy-start | bytes 2359300
  452.5 25.3 %copy-start.37 = (bf16[256,1536]{1,0:T(8,128)(2,1)S(1)}, bf16[256,1536]{1,0:T(8,128)(2,1)}, u32[]{:S(2)}) copy-start(bf16[256,1536]{1,0:T(8,128)(2,1)} %copy-done.36) | copy-start | bytes 2359300
  476.7 4.2 collective-permute-start.33
  480.7 26.9 %collective-permute-start.29 = (bf16[128,1536]{1,0:T(8,128)(2,1)}, bf16[128,1536]{1,0:T(8,128)(2,1)}, u32[]{:S(2)}, u32[]{:S(2)}) collective-permute-start(bf16[128,1536]{1,0:T(8,128)(2,1)} %dynamic-slice_convert_fusion.2), channel_id=1, source_target_pairs={{0,16},{16,0},{1,17},{17,1},{2,18},{18,2},{3,19},{19,3},{4,20},{20... | collective-permute-start | bytes 1179656 | tf_op jit(solution)/shard_map/ppermute | solution.py:754
  482.1 21.0 %all-to-all-start.2 = ((bf16[8,96,640]{2,1,0:T(8,128)(2,1)}), bf16[8,96,640]{2,1,0:T(8,128)(2,1)S(1)}, u32[]{:S(2)}, u32[]{:S(2)}) async-start(bf16[8,96,640]{2,1,0:T(8,128)(2,1)} %add_convert_fusion), calls=%async_computation.2 | async-start | bytes 1966080 | tf_op jit(solution)/shard_map/all_to_all | solution.py:73
  489.3 2.5 collective-permute-start.34
  506.9 10.1 %collective-permute-start.35 = (bf16[128,1536]{1,0:T(8,128)(2,1)}, bf16[128,1536]{1,0:T(8,128)(2,1)}, u32[]{:S(2)}, u32[]{:S(2)}) collective-permute-start(bf16[128,1536]{1,0:T(8,128)(2,1)} %dynamic-slice_convert_fusion.1), channel_id=1, source_target_pairs={{0,16},{16,0},{1,17},{17,1},{2,18},{18,2},{3,19},{19,3},{4,20},{20... | collective-permute-start | bytes 1179656 | tf_op jit(solution)/shard_map/ppermute | solution.py:754
  510.8 17.9 %all-to-all-start.3 = ((bf16[8,96,640]{2,1,0:T(8,128)(2,1)}), bf16[8,96,640]{2,1,0:T(8,128)(2,1)S(1)}, u32[]{:S(2)}, u32[]{:S(2)}) async-start(bf16[8,96,640]{2,1,0:T(8,128)(2,1)} %broadcast_in_dim.103), calls=%async_computation.4 | async-start | bytes 1966080 | tf_op jit(solution)/shard_map/all_to_all | solution.py:69
  (47 other events, 256.5 us)
Sparse Core Ops, SparseCore 0:
  37.7 151.9 all-gather.4
  214.8 37.3 all-gather.6
  316.8 161.2 reduce-scatter.1
